TPU v7x, 32 devices: a whole 2x2x4 slice. The times are simulated.
32 devices in a mesh: grp: 4 (over z), dev: 8 (over y, x, core).
Axes of the slice: x: 2, y: 2, z: 4, core: 2. Of those that a mesh axis runs over, the one named last changes fastest.
Arguments:
- particles: bfloat16 [512, 2, 6144], P(('grp', 'dev')), may hold values from -24 to 24
- defocus_bin: int32 [512], P(('grp', 'dev')), may hold values from 0 to 15
- candidates: int32 [512, 8], P(('grp', 'dev')), may hold values from 0 to 15, as said below
- projections: bfloat16 [16, 2, 6144], P('dev'), may hold values from -1 to 1
- ctf_table: bfloat16 [16, 6144], replicated, may hold values from -1 to 1
- inv_noise: float32 [6144], replicated, may hold values from 0.25 to 4
- line_slab: int32 [16, 48], P('dev'), may hold values from 0 to 3, as said below
- slab_owner: int32 [4], replicated, may hold values from 0 to 3, each once
Outputs:
- slab_data: float32 [4, 16, 2, 24, 128], P('grp', 'dev')
- slab_weight: float32 [4, 16, 24, 128], P('grp', 'dev')
Inputs may be any that keep to these rules, and one draw needn't show every extreme that they name: `candidates`: each particle lists 8 different projections. `line_slab`: no slab holds more than 24 lines of one projection, and for every projection one slab holds exactly 24 of them. `slab_owner`: each group owns exactly one slab.
All inputs are finite; a program needn't handle non-finite values.
Results may differ from a plain program's by a relative error of at most 0.02.
Values may be sent and summed in bfloat16 or wider, within the bound.
No kernel may reach another device: no remote copies, remote signals or barrier semaphores. Data moves between devices by JAX's collectives and lax.ppermute only.
A program may use at most 64 MiB of HBM per device.

v0:
```python
import math

import jax
import jax.numpy as jnp
from jax import lax
from jax.sharding import PartitionSpec as P

LINE_LEN = 128
PIXELS = 6144
SHIFTS = 9


two_pi = 2.0 * math.pi
exact = lax.Precision.HIGHEST
contract_rows = (((0,), (0,)), ((), ()))
contract_last = (((1,), (1,)), ((), ()))


def phase_tables():
    pixel_index = jnp.arange(PIXELS, dtype=jnp.int32)
    line_pos = (pixel_index // LINE_LEN).astype(jnp.float32)
    column = pixel_index % LINE_LEN
    frequency = jnp.where(column < LINE_LEN // 2, column, column - LINE_LEN).astype(jnp.float32)
    shift_index = jnp.arange(SHIFTS, dtype=jnp.int32)
    move_x = (shift_index // 3 - 1).astype(jnp.float32)
    move_y = (shift_index % 3 - 1).astype(jnp.float32)
    angles = (move_x[:, None] * line_pos[None, :] + move_y[:, None] * frequency[None, :]) * (
        two_pi / LINE_LEN
    )
    return (jnp.cos(angles), jnp.sin(angles))


def slot_tables(line_slab, slab_owner, groups):
    group_ids = jnp.arange(groups, dtype=jnp.int32)
    slab_hit = line_slab[:, :, None] == group_ids[None, None, :]
    owner_line = jnp.sum(jnp.where(slab_hit, slab_owner[None, None, :], 0), axis=2)
    line_ids = jnp.arange(line_slab.shape[1], dtype=jnp.int32)
    earlier = line_ids[None, :] < line_ids[:, None]
    same_owner = owner_line[:, :, None] == owner_line[:, None, :]
    line_rank = jnp.sum(jnp.logical_and(same_owner, earlier[None]), axis=2)
    return (owner_line, line_rank)


def route_lines(values, owner_line, line_rank, groups, capacity):
    group_ids = jnp.arange(groups, dtype=jnp.int32)
    slot_ids = jnp.arange(capacity, dtype=jnp.int32)
    selector = jnp.logical_and(
        owner_line[:, None, None, :] == group_ids[None, :, None, None],
        line_rank[:, None, None, :] == slot_ids[None, None, :, None],
    ).astype(jnp.float32)
    packed = jnp.einsum("jocl,jxlp->ojxcp", selector, values, precision=exact)
    return lax.psum_scatter(
        packed.astype(jnp.bfloat16), "grp", scatter_dimension=0, tiled=True
    ).astype(jnp.float32)[0]


def body(
    particles, defocus_bin, candidates, projections, ctf_table, inv_noise, line_slab, slab_owner
):
    part_dev = particles.shape[0]
    pixels = particles.shape[2]
    proj_dev = projections.shape[0]
    groups = lax.axis_size("grp")
    members = lax.axis_size("dev")
    proj_all = proj_dev * members
    line_count = line_slab.shape[1]
    line_len = pixels // line_count
    capacity = 2 * line_count // groups
    cosines, sine_table = phase_tables()
    table_values = ctf_table.astype(jnp.float32)
    ctf_square = table_values * table_values
    noisy_square = ctf_square * inv_noise[None, :]
    onehot = (
        defocus_bin[:, None] == jnp.arange(ctf_table.shape[0], dtype=jnp.int32)[None, :]
    ).astype(jnp.float32)
    ctf_rows = jnp.dot(onehot, table_values, precision=exact)
    weighted = (
        ((inv_noise[None, :] * ctf_rows)[:, None, :] * particles)
        .astype(jnp.bfloat16)
        .reshape(part_dev, 2 * pixels)
    )
    ctf_image = (
        (ctf_rows[:, None, :] * particles).astype(jnp.bfloat16).reshape(part_dev, 2 * pixels)
    )
    values = lax.all_gather(projections, "dev", axis=0, tiled=True).astype(jnp.float32)
    pix_power = values[:, 0] * values[:, 0] + values[:, 1] * values[:, 1]
    bin_power = lax.dot_general(noisy_square, pix_power, contract_last, precision=exact)
    quad_term = jnp.dot(onehot, bin_power, precision=exact)

    def one_shift(tables):
        cos_row, sin_row = tables
        real_part = values[:, 0] * cos_row[None, :] - values[:, 1] * sin_row[None, :]
        imag_part = values[:, 0] * sin_row[None, :] + values[:, 1] * cos_row[None, :]
        rotated = jnp.concatenate([real_part, imag_part], axis=1).astype(jnp.bfloat16)
        return lax.dot_general(weighted, rotated, contract_last, preferred_element_type=jnp.float32)

    scored = lax.map(one_shift, (cosines, sine_table))
    scores = jnp.transpose(scored, (1, 0, 2)) - 0.5 * quad_term[:, None, :]
    proj_ids = jnp.arange(proj_all, dtype=jnp.int32)
    listed = jnp.any(candidates[:, :, None] == proj_ids[None, None, :], axis=1)
    masked = jnp.where(listed[:, None, :], scores, -jnp.inf)
    row_peak = jnp.max(masked, axis=(1, 2), keepdims=True)
    exp_terms = jnp.exp(masked - row_peak)
    posterior = exp_terms / jnp.sum(exp_terms, axis=(1, 2), keepdims=True)
    by_shift = jnp.transpose(posterior.astype(jnp.bfloat16), (1, 0, 2))

    def add_shift(running, inputs):
        weights_now, cos_row, sin_row = inputs
        summed = lax.dot_general(
            weights_now, ctf_image, contract_rows, preferred_element_type=jnp.float32
        )
        real_sum = summed[:, :pixels]
        imag_sum = summed[:, pixels:]
        turned = jnp.stack(
            [
                real_sum * cos_row[None, :] + imag_sum * sin_row[None, :],
                imag_sum * cos_row[None, :] - real_sum * sin_row[None, :],
            ],
            axis=1,
        )
        return (running + turned, None)

    start_sum = jnp.zeros((proj_dev * lax.axis_size("dev"), 2, pixels), jnp.float32)
    result, _ = lax.scan(add_shift, start_sum, (by_shift, cosines, sine_table))
    data_part = lax.psum_scatter(
        result.astype(jnp.bfloat16), "dev", scatter_dimension=0, tiled=True
    ).astype(jnp.float32)
    proj_share = jnp.sum(posterior, axis=1)
    weight_scale = proj_all / (part_dev * groups * members)
    owner_line, line_rank = slot_tables(line_slab, slab_owner, groups)
    data_lines = data_part.reshape(proj_dev, 2, line_count, line_len)
    ctf_rows_sq = ctf_rows * ctf_rows
    weight_part = (
        lax.psum_scatter(
            lax.dot_general(
                proj_share,
                ctf_rows_sq,
                contract_rows,
                precision=exact,
                preferred_element_type=jnp.float32,
            ).astype(jnp.bfloat16),
            "dev",
            scatter_dimension=0,
            tiled=True,
        ).astype(jnp.float32)
        * weight_scale
    )
    stacked = jnp.concatenate(
        [data_lines, weight_part.reshape(proj_dev, 1, line_count, line_len)], axis=1
    )
    routed = route_lines(stacked, owner_line, line_rank, groups, capacity)
    return (routed[None, :, :2], routed[None, :, 2])


def solution(mesh):
    return jax.shard_map(
        body,
        mesh=mesh,
        in_specs=(
            P(("grp", "dev"), None, None),
            P(("grp", "dev")),
            P(("grp", "dev"), None),
            P("dev", None, None),
            P(),
            P(),
            P("dev", None),
            P(),
        ),
        out_specs=(P("grp", "dev", None, None, None), P("grp", "dev", None, None)),
        check_vma=False,
    )
```

profile of v0, /device:TPU:0, one launch (start us, length us, event | category | flops | bytes accessed | tf_op | source)
XLA Modules:
  0.0 171.1 jit_solution(4005252116136920779)
XLA Ops:
  7.2 0.6 fusion.43
  7.9 0.6 copy-done.10
  8.5 1.2 broadcast_multiply_fusion
  9.8 0.7 fusion.14
  10.5 0.9 copy.36
  11.3 11.0 %all_gather.3 = bf16[16,2,6144]{2,1,0:T(2,128)(2,1)S(1)} all-gather(bf16[2,2,6144]{2,1,0:T(2,128)(2,1)S(1)} %copy-done.7), channel_id=1, replica_groups=mesh['grp'=4,'dev'=8] {'dev'}, dimensions={0}, use_global_device_ids=true | all-gather | bytes 442368 | tf_op jit(solution)/shard_map/all_gather | solution.py:85
  22.8 0.5 fusion.15
  23.5 1.5 fusion.23
  25.0 25.9 %while.21 = (s32[]{:T(128)}, f32[9,16,16]{2,1,0:T(8,128)}, f32[16,2,6144]{2,1,0:T(2,128)S(1)}, f32[9,6144]{1,0:T(8,128)S(1)}, f32[9,6144]{1,0:T(8,128)S(1)}, /*index=5*/bf16[16,12288]{1,0:T(8,128)(2,1)}, s32[]{:T(128)}) while((s32[]{:T(128)}, f32[9,16,16]{2,1,0:T(8,128)}, f32[16,2,6144]{2,1,0:T(2,128)S(1)}, f32[9,6144]{1,0:T(8,128)S(1)}, ...), condition=%wide.region_2.3_spmd, body=%wide.region_1.2_spmd.sunk | while | flops 7864322 | bytes 6058605 | solution.py:97
  25.1 0.5 copy.54
  26.1 0.8 copy-done.1
  27.3 0.6 constant_dynamic-update-slice_fusion.2
  28.0 0.5 copy.54
  29.0 0.8 copy-done.1
  30.2 0.6 constant_dynamic-update-slice_fusion.2
  30.8 0.5 copy.54
  31.9 0.8 copy-done.1
  33.1 0.6 constant_dynamic-update-slice_fusion.2
  33.7 0.5 copy.54
  34.8 0.8 copy-done.1
  35.9 0.6 constant_dynamic-update-slice_fusion.2
  36.6 0.5 copy.54
  37.7 0.8 copy-done.1
  38.8 0.6 constant_dynamic-update-slice_fusion.2
  39.5 0.5 copy.54
  40.5 0.8 copy-done.1
  41.7 0.6 constant_dynamic-update-slice_fusion.2
  42.4 0.5 copy.54
  43.4 0.8 copy-done.1
  44.6 0.6 constant_dynamic-update-slice_fusion.2
  45.2 0.5 copy.54
  46.3 0.8 copy-done.1
  47.5 0.6 constant_dynamic-update-slice_fusion.2
  48.1 0.5 copy.54
  49.2 0.8 copy-done.1
  50.3 0.6 constant_dynamic-update-slice_fusion.2
  50.9 1.6 fusion.16
  52.9 0.5 copy-done
  53.8 0.7 fusion.54
  54.6 12.6 %while.22 = (s32[]{:T(128)}, f32[16,2,6144]{2,0,1:T(8,128)S(1)}, bf16[9,16,16]{2,1,0:T(8,128)(2,1)}, bf16[16,12288]{1,0:T(8,128)(2,1)S(1)}, f32[9,6144]{1,0:T(8,...) while((s32[]{:T(128)}, f32[16,2,6144]{2,0,1:T(8,128)S(1)}, ...), condition=%wide.region_6.7_spmd.clone, body=%wide.region_5.6_spmd.clone.sunk | while | flops 7471107 | bytes 5263971 | solution.py:124
  54.7 1.0 fusion.73
  56.1 1.0 fusion.73
  57.5 1.0 fusion.73
  58.9 1.0 fusion.73
  60.3 1.0 fusion.73
  61.7 1.0 fusion.73
  63.1 1.0 fusion.73
  64.5 1.0 fusion.73
  65.9 1.0 fusion.73
  67.2 0.8 convert_element_type.105
  68.1 1.2 convolution_convert_fusion
  69.4 0.6 copy-done.9
  70.2 0.6 copy-done.14
  70.8 0.6 dynamic-slice
  72.3 52.6 %all-reduce.9.cloned.1.call-done = (bf16[16,6144]{1,0:T(8,128)(2,1)}, bf16[16,2,6144]{2,0,1:T(8,128)(2,1)}) async-done(((bf16[16,6144]{1,0:T(8,128)(2,1)}, bf16[16,2,6144]{2,0,1:T(8,128)(2,1)}), (bf16[16,6144]{1,0:T(8,128)(2,1)}, bf16[16,2,6144]{2,0,1:T(8,128)(2,1)})) %all-reduce.9.cloned.1.call-update) | async-done | bytes 589840
  124.9 1.0 dynamic-slice_convert_fusion
  126.0 0.9 multiply_bitcast_fusion
  126.9 0.9 fusion.12
  127.9 0.6 copy-done.13
  128.5 0.6 dynamic-slice.4
  129.1 32.5 %all-reduce.7.cloned.1.call-done = bf16[4,2,3,24,128]{4,3,0,2,1:T(8,128)(2,1)} async-done(((bf16[4,2,3,24,128]{4,3,0,2,1:T(8,128)(2,1)}), bf16[4,2,3,24,128]{4,3,0,2,1:T(8,128)(2,1)}) %all-reduce.7.cloned.1.call-update) | async-done | bytes 147472
  161.6 1.4 fusion.40
  163.0 0.6 slice_bitcast_fusion.1
  163.6 0.6 slice_bitcast_fusion.2
  (126 shorter events, 14.0 us)
Async XLA Ops:
  7.2 0.7 copy-start.6
  7.2 117.7 %all-reduce.9.cloned.1.call-start = ((), (), s32[]{:S(2)}) async-start(), calls=%async_computation.1 | async-start | bytes 1179648
  7.9 0.7 copy-start.10
  8.5 1.2 copy-start.2
  10.5 0.9 copy-start.7
  22.8 0.7 copy-start.4
  22.8 0.7 copy-start.5
  26.0 1.0 copy-start.1
  28.8 1.0 copy-start.1
  31.7 1.0 copy-start.1
  34.6 1.0 copy-start.1
  37.5 1.0 copy-start.1
  40.4 1.0 copy-start.1
  43.2 1.0 copy-start.1
  46.1 1.0 copy-start.1
  49.0 1.0 copy-start.1
  50.9 1.6 copy-start.11
  50.9 1.8 %copy-start.8 = (s32[16,8]{0,1:T(8,128)S(1)}, s32[16,8]{0,1:T(8,128)}, u32[]{:S(2)}) copy-start(s32[16,8]{0,1:T(8,128)} %param.14) | copy-start | bytes 1540
  52.6 0.9 copy-start
  67.2 0.9 copy-start.3
  69.3 92.2 %all-reduce.7.cloned.1.call-start = ((), (), s32[]{:S(2)}) async-start(), calls=%async_computation | async-start | bytes 294912
  69.4 0.7 copy-start.9
  69.4 0.7 copy-start.12
  70.2 0.7 copy-start.14
  127.8 0.7 copy-start.13
Sparse Core Ops, SparseCore 0:
  69.5 55.3 all-reduce.8
  128.0 33.5 all-reduce.6
where the time goes:
time: 172 us; the launch traced here: 171 us
  waiting for transfers between devices  85.2 us (50%)
  local copies, waits for them, and re-layouts  29.2 us (17%)
  matrix products  16.3 us (9%)
  between operations  14.9 us (9%)
  other arithmetic  13.7 us (8%)
  blocking collectives  11 us (6%)
    unnamed x4, waiting for transfers between devices  85.2 us
    all_gather x1, blocking collectives, body(): lax.all_gather(projections, 'dev', axis=0, tiled=True).astype(jnp.float32)  11 us
    dot_general x9, matrix products, add_shift(): lax.dot_general(weights_now, ctf_image, contract_rows, preferred_element_...  8.81 us
    while x18, local copies, waits for them, and re-layouts  7.43 us
    dynamic_update_slice x18, local copies, waits for them, and re-layouts, body(): scored = lax.map(one_shift, (cosines, sine_table))  6.24 us
    unnamed x34, local copies, waits for them, and re-layouts  5.65 us
    another operation x9, local copies, waits for them, and re-layouts  4.14 us
    slice x9, local copies, waits for them, and re-layouts, one_shift(): values[:, 1] * sin_row[None, :]  3.67 us
  transfers between devices with their start and end apart: 2, of which 2 were waited for; matrix products, arithmetic and copies ran while one was open for 1% of the time, Pallas kernels for 0%

commit v1 on v0

v1 whole, which is shorter than its diff:
```python
import functools
import math

import jax
import jax.numpy as jnp
import numpy as np
from jax import lax
from jax.experimental import pallas as pl
from jax.experimental.pallas import tpu as pltpu
from jax.sharding import PartitionSpec as P

LINE_LEN = 128
VMEM_BYTES = 40 * 1024 * 1024
f32 = jnp.float32
bf16 = jnp.bfloat16
exact = lax.Precision.HIGHEST
last_last = (((1,), (1,)), ((), ()))
first_first = (((0,), (0,)), ((), ()))


def trig_rows(pixels):
    k = np.arange(pixels)
    line = k // LINE_LEN
    column = k % LINE_LEN
    freq = np.where(column < LINE_LEN // 2, column, column - LINE_LEN)
    step = 2.0 * math.pi / LINE_LEN
    rows = np.zeros((8, pixels), np.float32)
    rows[0] = np.cos(line * step)
    rows[1] = np.sin(line * step)
    rows[2] = np.cos(freq * step)
    rows[3] = np.sin(freq * step)
    return rows


def call(kernel, out_shape, flops=0, moved=0, **kw):
    return pl.pallas_call(
        kernel,
        out_shape=out_shape,
        compiler_params=pltpu.CompilerParams(vmem_limit_bytes=VMEM_BYTES),
        cost_estimate=pl.CostEstimate(flops=flops, bytes_accessed=moved, transcendentals=0),
        **kw,
    )


def split(x):
    hi = x.astype(bf16)
    return hi, (x - hi.astype(f32)).astype(bf16)


def prep_kernel(part_ref, ints_ref, table_ref, trig_ref, y_ref):
    n = ints_ref.shape[0]
    bins = table_ref.shape[0]
    pixels = part_ref.shape[1]
    hit = ints_ref[:, 0:1] == lax.broadcasted_iota(jnp.int32, (n, bins), 1)
    onehot = hit.astype(f32).astype(bf16)
    width = 1024
    for c in range(pixels // width):
        cols = slice(c * width, (c + 1) * width)
        ctf = jnp.dot(onehot, table_ref[:, cols], preferred_element_type=f32)
        for part in range(2):
            x = part_ref[part * n : (part + 1) * n, cols].astype(f32) * ctf
            base = part * n
            y_ref[base : base + n, cols] = x.astype(bf16)
            y_ref[2 * n + base : 3 * n + base, cols] = (x * trig_ref[0:1, cols]).astype(bf16)
            y_ref[4 * n + base : 5 * n + base, cols] = (x * trig_ref[1:2, cols]).astype(bf16)


def score_kernel(chunks, rows, *refs):
    p_refs = refs[:chunks]
    (y0_ref, y1_ref, i0_ref, i1_ref, table_ref, noise_ref, trig_ref, pid_ref) = refs[
        chunks : chunks + 8
    ]
    m0_ref, m1_ref, s_ref, stat_ref = refs[chunks + 8 : chunks + 12]
    r_ref, q_ref = refs[chunks + 12 :]
    n = i0_ref.shape[0]
    bins = table_ref.shape[0]
    pixels = table_ref.shape[1]
    wide = 4 * chunks
    width = 1024
    if rows > 5 * wide:
        r_ref[5 * wide :, :] = jnp.zeros((rows - 5 * wide, pixels), bf16)
    for c in range(pixels // width):
        cols = slice(c * width, (c + 1) * width)
        x = jnp.concatenate([p[:, cols].astype(f32) for p in p_refs], axis=0)
        one = x * noise_ref[:, cols]
        r_ref[0:wide, cols] = one.astype(bf16)
        r_ref[wide : 2 * wide, cols] = (one * trig_ref[2:3, cols]).astype(bf16)
        r_ref[2 * wide : 3 * wide, cols] = (one * trig_ref[3:4, cols]).astype(bf16)
        high, low = split(one * x)
        r_ref[3 * wide : 4 * wide, cols] = high
        r_ref[4 * wide : 5 * wide, cols] = low
        t = table_ref[:, cols].astype(f32)
        high, low = split(t * t)
        q_ref[0:bins, cols] = high
        q_ref[bins : 2 * bins, cols] = low
    g0 = lax.dot_general(y0_ref[...], r_ref[...], last_last, preferred_element_type=f32)
    g1 = lax.dot_general(y1_ref[...], r_ref[...], last_last, preferred_element_type=f32)
    gq = lax.dot_general(q_ref[...], r_ref[...], last_last, preferred_element_type=f32)

    def left(v, k):
        return pltpu.roll(v, rows - k, 1)

    def right(v, k):
        return pltpu.roll(v, k, 1)

    lane = lax.broadcasted_iota(jnp.int32, (1, rows), 1)
    is_real = (lane % 4) < 2
    block0 = jnp.logical_and(is_real, lane < wide)
    block1 = jnp.logical_and(is_real, jnp.logical_and(lane >= wide, lane < 2 * wide))
    power = gq[:bins] + gq[bins:]
    power = power + left(power, wide)
    power = power + left(power, 2)
    power = jnp.where(block0, left(power, 3 * wide), jnp.where(block1, left(power, 2 * wide), 0.0))

    def take(part, a):
        base = (2 * a + part) * n
        return jnp.concatenate([g0[base : base + n], g1[base : base + n]], axis=0)

    even, odd = [], []
    for a in range(3):
        real, imag = take(0, a), take(1, a)
        even.append(real + left(imag, 2))
        odd.append(imag - left(real, 2))
    ints = jnp.concatenate([i0_ref[...], i1_ref[...]], axis=0)
    onehot = (ints[:, 0:1] == lax.broadcasted_iota(jnp.int32, (2 * n, bins), 1)).astype(f32)
    quad = 0.5 * jnp.dot(onehot, power, precision=exact, preferred_element_type=f32)
    pid = pid_ref[...]
    listed = ints[:, 1:2] == pid
    for c in range(2, 9):
        listed = jnp.logical_or(listed, ints[:, c : c + 1] == pid)
    valid1 = jnp.logical_and(listed, block1)
    valid01 = jnp.logical_and(listed, jnp.logical_or(block0, block1))

    base = [even[0] - quad, even[1] + odd[2] - quad, even[1] - odd[2] - quad]
    turn = [left(odd[0], wide), left(odd[1] - even[2], wide), left(odd[1] + even[2], wide)]
    plus = [b + jnp.where(block1, d, 0.0) for b, d in zip(base, turn)]
    minus = [b - d for b, d in zip(base, turn)]
    low = -3.0e38
    plus = [jnp.where(valid01, v, low) for v in plus]
    minus = [jnp.where(valid1, v, low) for v in minus]
    peak = plus[0]
    for v in plus[1:] + minus:
        peak = jnp.maximum(peak, v)
    peak = jnp.max(peak, axis=1, keepdims=True)
    plus = [jnp.where(valid01, jnp.exp(v - peak), 0.0) for v in plus]
    minus = [jnp.where(valid1, jnp.exp(v - peak), 0.0) for v in minus]
    both = [u + v for u, v in zip(plus, minus)]
    diff = [jnp.where(block1, u - v, 0.0) for u, v in zip(plus, minus)]
    total = both[0] + both[1] + both[2]
    mass = jnp.sum(total, axis=1, keepdims=True)
    lanes = lax.broadcasted_iota(jnp.int32, (2 * n, LINE_LEN), 1)
    stat_ref[...] = jnp.where(lanes == 0, peak, jnp.where(lanes == 1, mass, 0.0))
    s_ref[...] = jnp.where(block0, total + left(total, wide), 0.0)
    alpha = [both[0], both[1] + both[2], right(diff[2] - diff[1], wide)]
    beta = [right(diff[0], wide), right(diff[1] + diff[2], wide), both[1] - both[2]]
    for a in range(3):
        real = alpha[a] - right(beta[a], 2)
        imag = beta[a] + right(alpha[a], 2)
        for h, ref in enumerate((m0_ref, m1_ref)):
            ref[(2 * a) * n : (2 * a + 1) * n] = real[h * n : (h + 1) * n]
            ref[(2 * a + 1) * n : (2 * a + 2) * n] = imag[h * n : (h + 1) * n]


def slice_kernel(chunks, *refs):
    (y0_ref, y1_ref, m0_ref, m1_ref, s_ref, stat_ref, other_ref, i0_ref, i1_ref, trig_ref) = refs[:10]
    outs = refs[10:]
    n = i0_ref.shape[0]
    pixels = y0_ref.shape[1]
    wide = 4 * chunks
    other = jnp.concatenate([other_ref[n:], other_ref[:n]], axis=0)
    peak0, mass0 = stat_ref[:, 0:1], stat_ref[:, 1:2]
    peak1, mass1 = other[:, 0:1], other[:, 1:2]
    peak = jnp.maximum(peak0, peak1)
    grow = jnp.exp(peak0 - peak)
    scale = grow / (mass0 * grow + mass1 * jnp.exp(peak1 - peak))
    ints = jnp.concatenate([i0_ref[...], i1_ref[...]], axis=0)
    onehot = (ints[:, 0:1] == lax.broadcasted_iota(jnp.int32, (2 * n, LINE_LEN), 1)).astype(f32)
    share = lax.dot_general(
        s_ref[...] * scale, onehot, first_first, precision=exact, preferred_element_type=f32
    )[:wide].astype(bf16)
    mats = []
    for h, ref in enumerate((m0_ref, m1_ref)):
        part = scale[h * n : (h + 1) * n]
        m = ref[...] * jnp.concatenate([part] * 6, axis=0)
        mats.append(jnp.transpose(m)[: 3 * wide].astype(bf16))
    width = 1024
    for c in range(pixels // width):
        cols = slice(c * width, (c + 1) * width)
        x = jnp.dot(mats[0], y0_ref[:, cols], preferred_element_type=f32)
        x = x + jnp.dot(mats[1], y1_ref[:, cols], preferred_element_type=f32)
        x = (
            x[:wide]
            + x[wide : 2 * wide] * trig_ref[2:3, cols]
            + x[2 * wide :] * trig_ref[3:4, cols]
        )
        for s in range(chunks):
            outs[s][:, cols] = x[4 * s : 4 * s + 4].astype(bf16)
    for s in range(chunks):
        outs[s][:, pixels:] = share[4 * s : 4 * s + 4]


def pack_kernel(chunks, lines, cap, idx_ref, *refs):
    p_refs = refs[:chunks]
    keep_ref, send_ref = refs[chunks : chunks + 2]
    (scr_ref,) = refs[chunks + 2 :]
    half = keep_ref.shape[0] - 16
    scr_ref[...] = jnp.zeros(scr_ref.shape, f32)
    for l in range(lines + 1):
        cols = slice(l * LINE_LEN, (l + 1) * LINE_LEN)
        x = p_refs[0][:, cols].astype(f32)
        for p in p_refs[1:]:
            x = x + p[:, cols].astype(f32)
        if l < lines:
            for j in range(2):
                row = idx_ref[j, l]
                scr_ref[pl.ds(row, 1), :] = x[j : j + 1]
                scr_ref[pl.ds(row + cap, 1), :] = x[2 + j : 3 + j]
        else:
            tail = jnp.concatenate([x, jnp.zeros((12, LINE_LEN), f32)], axis=0)
    keep_ref[:half] = scr_ref[:half]
    keep_ref[half:] = tail
    send_ref[:half] = scr_ref[half:].astype(bf16)
    send_ref[half:] = tail.astype(bf16)


def table_kernel(lines, cap, idx_ref, table_ref, sel_ref):
    bins = table_ref.shape[0]
    sel_ref[...] = jnp.zeros(sel_ref.shape, f32)
    for l in range(lines):
        t = table_ref[:, l * LINE_LEN : (l + 1) * LINE_LEN].astype(f32)
        t = t * t
        for j in range(2):
            slot = idx_ref[j, l]

            @pl.when(slot < 4 * cap)
            def _():
                sel_ref[j, pl.ds(slot - 2 * cap * j, 1)] = t[None]


def final_kernel(cap, scale, acc_ref, recv_ref, bins_ref, sel_ref, data_ref, weight_ref):
    rows = 4 * cap
    x = acc_ref[...] + recv_ref[:rows].astype(f32)
    data_ref[...] = x.reshape(data_ref.shape)
    b = (bins_ref[...] + recv_ref[rows:].astype(f32)) * scale
    bt = jnp.transpose(b)[: sel_ref.shape[2]]
    for j in range(2):
        weight_ref[0, j] = jnp.sum(sel_ref[j] * bt[:, j : j + 1][None], axis=1)


def body(
    particles, defocus_bin, candidates, projections, ctf_table, inv_noise, line_slab, slab_owner
):
    n, _, pixels = particles.shape
    groups = lax.axis_size("grp")
    members = lax.axis_size("dev")
    chunks = members // 2
    lines = line_slab.shape[1]
    cap = 2 * lines // groups
    bins = ctf_table.shape[0]
    wide = 4 * chunks
    rows = -(-5 * wide // 128) * 128
    dev = lax.axis_index("dev")
    grp = lax.axis_index("grp")
    trig = jnp.asarray(trig_rows(pixels))
    noise = inv_noise[None, :]

    def swap(x, axis, size, mask):
        return lax.ppermute(x, axis, [(i, i ^ mask) for i in range(size)])

    own = jnp.transpose(projections, (1, 0, 2)).reshape(4, pixels)
    proj = [own] + [swap(own, "dev", members, 2 * s) for s in range(1, chunks)]
    part0 = jnp.transpose(particles, (1, 0, 2)).reshape(2 * n, pixels)
    ints0 = jnp.concatenate([defocus_bin[:, None], candidates], axis=1)
    part1 = swap(part0, "dev", members, 1)
    ints1 = swap(ints0, "dev", members, 1)

    prep = call(
        prep_kernel,
        jax.ShapeDtypeStruct((6 * n, pixels), bf16),
        flops=10 * n * pixels,
        moved=16 * n * pixels,
    )
    y0 = prep(part0, ints0, ctf_table, trig)
    y1 = prep(part1, ints1, ctf_table, trig)

    lane = jnp.arange(rows, dtype=jnp.int32) % wide
    pid = 4 * ((dev // 2) ^ (lane // 4)) + 2 * (dev % 2) + lane % 2
    m0, m1, share, stat = call(
        functools.partial(score_kernel, chunks, rows),
        (
            jax.ShapeDtypeStruct((6 * n, rows), f32),
            jax.ShapeDtypeStruct((6 * n, rows), f32),
            jax.ShapeDtypeStruct((2 * n, rows), f32),
            jax.ShapeDtypeStruct((2 * n, LINE_LEN), f32),
        ),
        scratch_shapes=[pltpu.VMEM((rows, pixels), bf16), pltpu.VMEM((2 * bins, pixels), bf16)],
        flops=2 * 224 * rows * pixels,
        moved=30 * n * pixels,
    )(*proj, y0, y1, ints0, ints1, ctf_table, noise, trig, pid[None, :])
    other = swap(stat, "dev", members, 1)
    sums = call(
        functools.partial(slice_kernel, chunks),
        tuple(jax.ShapeDtypeStruct((4, pixels + LINE_LEN), bf16) for _ in range(chunks)),
        flops=2 * 192 * 3 * wide * pixels,
        moved=30 * n * pixels,
    )(y0, y1, m0, m1, share, stat, other, ints0, ints1, trig)
    parts = [sums[0]] + [swap(sums[s], "dev", members, 2 * s) for s in range(1, chunks)]

    group_ids = jnp.arange(groups, dtype=jnp.int32)
    slab_hit = line_slab[:, :, None] == group_ids[None, None, :]
    owner_line = jnp.sum(jnp.where(slab_hit, slab_owner[None, None, :], 0), axis=2)
    line_ids = jnp.arange(lines, dtype=jnp.int32)
    earlier = line_ids[None, :] < line_ids[:, None]
    same_owner = owner_line[:, :, None] == owner_line[:, None, :]
    line_rank = jnp.sum(jnp.logical_and(same_owner, earlier[None]), axis=2)
    rel = owner_line ^ grp
    place = jnp.zeros_like(rel)
    bits = groups.bit_length() - 1
    for b in range(bits):
        place = place + (((rel >> b) & 1) << (bits - 1 - b))
    idx = (4 * cap) * place + 2 * cap * jnp.arange(2, dtype=jnp.int32)[:, None] + line_rank
    idx = idx.astype(jnp.int32)

    sel = call(
        functools.partial(table_kernel, lines, cap),
        jax.ShapeDtypeStruct((2, cap, bins, LINE_LEN), f32),
        in_specs=[pl.BlockSpec(memory_space=pltpu.SMEM), pl.BlockSpec(memory_space=pltpu.VMEM)],
        flops=bins * pixels,
        moved=4 * bins * pixels,
    )(idx, ctf_table)
    half = groups // 2 * 4 * cap
    keep, send = call(
        functools.partial(pack_kernel, chunks, lines, cap),
        (
            jax.ShapeDtypeStruct((half + 16, LINE_LEN), f32),
            jax.ShapeDtypeStruct((half + 16, LINE_LEN), bf16),
        ),
        in_specs=[pl.BlockSpec(memory_space=pltpu.SMEM)]
        + [pl.BlockSpec(memory_space=pltpu.VMEM)] * chunks,
        scratch_shapes=[pltpu.VMEM((2 * half, LINE_LEN), f32)],
        flops=16 * pixels,
        moved=64 * pixels,
    )(idx, *parts)
    for b in range(bits - 1):
        total = keep + swap(send, "grp", groups, 1 << b).astype(f32)
        keep, send, tail = total[: half // 2], total[half // 2 : half], total[half:]
        half = half // 2
        send = jnp.concatenate([send, tail], axis=0).astype(bf16)
        if b < bits - 2:
            keep = jnp.concatenate([keep, tail], axis=0)
    recv = swap(send, "grp", groups, 1 << (bits - 1))
    weight_scale = 2 * members / (n * groups * members)
    return call(
        functools.partial(final_kernel, cap, weight_scale),
        (
            jax.ShapeDtypeStruct((1, 2, 2, cap, LINE_LEN), f32),
            jax.ShapeDtypeStruct((1, 2, cap, LINE_LEN), f32),
        ),
        flops=1000,
        moved=8 * 4 * cap * LINE_LEN,
    )(keep, recv, tail, sel)


def solution(mesh):
    return jax.shard_map(
        body,
        mesh=mesh,
        in_specs=(
            P(("grp", "dev"), None, None),
            P(("grp", "dev")),
            P(("grp", "dev"), None),
            P("dev", None, None),
            P(),
            P(),
            P("dev", None),
            P(),
        ),
        out_specs=(P("grp", "dev", None, None, None), P("grp", "dev", None, None)),
        check_vma=False,
    )
```

time: 172 us -> 35.1 us (0.20)
  waiting for transfers between devices: 85.2 us -> 9.27 us
  local copies, waits for them, and re-layouts: 29.2 us -> 3.87 us
  matrix products: 16.3 us -> 0 us
  between operations: 14.9 us -> 0.83 us
  starting transfers between devices: 0.08 us -> 13.2 us
  other arithmetic: 13.7 us -> 1.15 us
  blocking collectives: 11 us -> 0 us
  Pallas kernels: 0 us -> 6.47 us
    unnamed x4 -> x0, waiting for transfers between devices: 85.2 us -> none
    dot_general x23 -> x0, matrix products: 16.3 us -> none  [the longest x9 8.81 us: add_shift(): lax.dot_general(weights_now, ctf_image, contract_rows, preferred_element_...]
    ppermute x0 -> x11, starting transfers between devices: none -> 13.2 us  [swap(): return lax.ppermute(x, axis, [(i, i ^ mask) for i in range(size)])]
    all_gather x1 -> x0, blocking collectives: 11 us -> none  [body(): lax.all_gather(projections, 'dev', axis=0, tiled=True).astype(jnp.float32)]
    ppermute x0 -> x11, waiting for transfers between devices: none -> 9.27 us  [swap(): return lax.ppermute(x, axis, [(i, i ^ mask) for i in range(size)])]
    while x18 -> x0, local copies, waits for them, and re-layouts: 7.43 us -> none
    pallas_call x0 -> x7, Pallas kernels: none -> 6.47 us  [the longest x1 2.17 us: body(): call(functools.partial(score_kernel, chunks, rows), (jax.ShapeDtypeStruct...]
    dynamic_update_slice x18 -> x0, local copies, waits for them, and re-layouts: 6.24 us -> none  [body(): scored = lax.map(one_shift, (cosines, sine_table))]
  transfers between devices with their start and end apart: 2 -> 11, of which waited for: 2 -> 6; matrix products, arithmetic and copies ran while one was open for 1% -> 11% of each run, Pallas kernels for 0% -> 6%
where the time goes in v1:
time: 35.1 us; the launch traced here: 34.8 us
  starting transfers between devices  13.2 us (38%)
  waiting for transfers between devices  9.27 us (26%)
  Pallas kernels  6.47 us (18%)
  local copies, waits for them, and re-layouts  3.87 us (11%)
  other arithmetic  1.15 us (3%)
  between operations  0.83 us (2%)
    ppermute x11, starting transfers between devices, swap(): return lax.ppermute(x, axis, [(i, i ^ mask) for i in range(size)])  13.2 us
    ppermute x11, waiting for transfers between devices, swap(): return lax.ppermute(x, axis, [(i, i ^ mask) for i in range(size)])  9.27 us
    pallas_call x1, Pallas kernels, body(): call(functools.partial(score_kernel, chunks, rows), (jax.ShapeDtypeStruct...  2.17 us
    pallas_call x1, Pallas kernels, body(): call(functools.partial(table_kernel, lines, cap), jax.ShapeDtypeStruct((2...  1.34 us
    transpose x1, local copies, waits for them, and re-layouts, body(): part0 = jnp.transpose(particles, (1, 0, 2)).reshape(2 * n, pixels)  1.12 us
    unnamed x7, local copies, waits for them, and re-layouts  1.1 us
    transpose x1, local copies, waits for them, and re-layouts, body(): own = jnp.transpose(projections, (1, 0, 2)).reshape(4, pixels)  0.89 us
    pallas_call x1, Pallas kernels, body(): call(functools.partial(final_kernel, cap, weight_scale), (jax.ShapeDtypeS...  0.81 us
  transfers between devices with their start and end apart: 11, of which 6 were waited for; matrix products, arithmetic and copies ran while one was open for 11% of the time, Pallas kernels for 6%

profile of v1, /device:TPU:0, one launch (start us, length us, event | category | flops | bytes accessed | tf_op | source)
XLA Modules:
  0.0 34.8 jit_solution(19341460685529683)
XLA Ops:
  0.6 0.0 copy-start.1
  0.6 0.0 copy-start
  0.7 0.9 %copy.18 = bf16[2,2,6144]{2,1,0:T(2,128)(2,1)S(1)} copy(bf16[2,2,6144]{2,0,1:T(2,128)(2,1)} %bitcast.9) | data formatting | bytes 98304 | tf_op jit(solution)/shard_map/transpose | solution.py:270
  1.6 3.0 %collective-permute-start.2 = (bf16[4,6144]{1,0:T(4,128)(2,1)S(1)}, bf16[4,6144]{1,0:T(4,128)(2,1)S(1)}, u32[]{:S(2)}, u32[]{:S(2)}) collective-permute-start(bf16[4,6144]{1,0:T(4,128)(2,1)S(1)} %reshape.138.refs_0_), channel_id=1, source_target_pairs={{0,2},{1,3},{2,0},{3,1},{4,6},{5,7},{6,4},{7,5},{8,10},{9,11},{10,... | collective-permute-start | bytes 147464 | tf_op jit(solution)/shard_map/ppermute | solution.py:268
  4.6 1.5 %collective-permute-start.3 = (bf16[4,6144]{1,0:T(4,128)(2,1)S(1)}, bf16[4,6144]{1,0:T(4,128)(2,1)S(1)}, u32[]{:S(2)}, u32[]{:S(2)}) collective-permute-start(bf16[4,6144]{1,0:T(4,128)(2,1)S(1)} %reshape.138.refs_0_), channel_id=1, source_target_pairs={{0,4},{1,5},{2,6},{3,7},{4,0},{5,1},{6,2},{7,3},{8,12},{9,13},{10,... | collective-permute-start | bytes 147464 | tf_op jit(solution)/shard_map/ppermute | solution.py:268
  6.1 0.0 collective-permute-start.4
  6.1 0.7 %copy.16 = s32[16,1]{1,0:T(8,128)S(1)} copy(s32[16,1]{0,1:T(1,128)} %bitcast.10) | data formatting | bytes 128 | tf_op jit(solution)/shard_map/broadcast_in_dim | solution.py:273
  6.8 0.8 %copy.17 = s32[16,8]{1,0:T(8,128)S(1)} copy(s32[16,8]{0,1:T(8,128)} %param.11) | data formatting | bytes 1024 | tf_op args[2]
  7.6 0.1 pad_add_fusion.ints_ref.refs_6_.refs_7_
  7.7 0.0 collective-permute-start.1
  7.7 1.1 %copy.15 = bf16[2,16,6144]{2,1,0:T(8,128)(2,1)S(1)} copy(bf16[2,16,6144]{2,0,1:T(2,128)(2,1)} %bitcast.8) | data formatting | bytes 786432 | tf_op jit(solution)/shard_map/transpose | solution.py:272
  8.8 0.6 %collective-permute-start = (bf16[32,6144]{1,0:T(8,128)(2,1)S(1)}, bf16[32,6144]{1,0:T(8,128)(2,1)S(1)}, u32[]{:S(2)}, u32[]{:S(2)}) collective-permute-start(bf16[32,6144]{1,0:T(8,128)(2,1)S(1)} %bitcast.5), channel_id=1, source_target_pairs={{0,1},{1,0},{2,3},{3,2},{4,5},{5,4},{6,7},{7,6},{8,9},{9,8},{10,11... | collective-permute-start | bytes 1179656 | tf_op jit(solution)/shard_map/ppermute | solution.py:268
  9.4 0.8 %select_reduce_fusion = s32[2,48]{1,0:T(2,128)S(1)} fusion(s32[4]{0:T(128)} %param.16, s32[2,48]{1,0:T(2,128)} %param.15), kind=kLoop, calls=%fused_computation.5 | loop fusion | flops 1056 | bytes 784 | tf_op jit(solution)/shard_map/reduce_sum | solution.py:311
  10.2 0.2 convert_reduce_fusion
  10.4 0.0 copy-done.1
  10.4 0.0 copy-done
  10.4 0.3 shard_map.104.refs_4_.refs_0_
  10.8 0.0 copy-start.2
  10.8 0.0 collective-permute-done.1.ints_ref.refs_7_.refs_8_
  10.8 0.0 collective-permute-done.part_ref
  10.8 0.3 shard_map.105.refs_5_.refs_1_
  11.2 0.0 collective-permute-done.2.refs_1_
  11.2 0.0 collective-permute-done.3.refs_2_
  11.2 0.0 collective-permute-done.4.refs_3_
  11.2 0.3 copy-done.2
  11.5 2.2 %shard_map.106 = (f32[96,128]{1,0:T(8,128)S(1)}, f32[96,128]{1,0:T(8,128)S(1)}, f32[32,128]{1,0:T(8,128)S(1)}, f32[32,128]{1,0:T(8,128)S(1)}) custom-call(bf16[4,6144]{1,0:T(4,128)(2,1)S(1)} %reshape.138.refs_0_, bf16[4,6144]{1,0:T(4,128)(2,1)S(1)} %collective-permute-done.2.refs_1_, bf16[4,6144]{1,0:T(4,128)(2,1)S(1)} %collective-permute-done.3.refs_2_, ...), custom_call_target="tpu_custom_call" | custom-call | flops 352321536 | bytes 2949120 | tf_op jit(solution)/shard_map/pallas_call | solution.py:288
  13.7 0.1 collective-permute-start.5
  13.8 1.2 %collective-permute-done.5.refs_6_ = f32[32,128]{1,0:T(8,128)S(1)} collective-permute-done((f32[32,128]{1,0:T(8,128)S(1)}, f32[32,128]{1,0:T(8,128)S(1)}, u32[]{:S(2)}, u32[]{:S(2)}) %collective-permute-start.5) | collective-permute-done | bytes 16416 | tf_op jit(solution)/shard_map/ppermute | solution.py:268
  14.9 0.8 %shard_map.107 = (bf16[4,6272]{1,0:T(4,128)(2,1)S(1)}, bf16[4,6272]{1,0:T(4,128)(2,1)S(1)}, bf16[4,6272]{1,0:T(4,128)(2,1)S(1)}, bf16[4,6272]{1,0:T(4,128)(2,1)S(1)}) custom-call(bf16[96,6144]{1,0:T(8,128)(2,1)S(1)} %shard_map.104.refs_4_.refs_0_, bf16[96,6144]{1,0:T(8,128)(2,1)S(1)} %shard_map.105.refs_5_.refs_1_, f32[96,128]{1,0:T(8,128)S(1)} %get-tuple-element.12.refs_2_, ...), custom_call_target="tpu_custom_call" | custom-call | flops 113246208 | bytes 2949120 | tf_op jit(solution)/shard_map/pallas_call | solution.py:301
  15.7 2.0 %collective-permute-start.6 = (bf16[4,6272]{1,0:T(4,128)(2,1)S(1)}, bf16[4,6272]{1,0:T(4,128)(2,1)S(1)}, u32[]{:S(2)}, u32[]{:S(2)}) collective-permute-start(bf16[4,6272]{1,0:T(4,128)(2,1)S(1)} %get-tuple-element.17), channel_id=1, source_target_pairs={{0,2},{1,3},{2,0},{3,1},{4,6},{5,7},{6,4},{7,5},{8,10},{9,11},{10,... | collective-permute-start | bytes 150536 | tf_op jit(solution)/shard_map/ppermute | solution.py:268
  17.7 1.5 %collective-permute-start.7 = (bf16[4,6272]{1,0:T(4,128)(2,1)S(1)}, bf16[4,6272]{1,0:T(4,128)(2,1)S(1)}, u32[]{:S(2)}, u32[]{:S(2)}) collective-permute-start(bf16[4,6272]{1,0:T(4,128)(2,1)S(1)} %get-tuple-element.18), channel_id=1, source_target_pairs={{0,4},{1,5},{2,6},{3,7},{4,0},{5,1},{6,2},{7,3},{8,12},{9,13},{10,... | collective-permute-start | bytes 150536 | tf_op jit(solution)/shard_map/ppermute | solution.py:268
  19.3 0.0 collective-permute-start.8
  19.3 0.1 add_add_fusion.idx_ref
  19.3 0.5 %collective-permute-done.6.refs_1_ = bf16[4,6272]{1,0:T(4,128)(2,1)S(1)} collective-permute-done((bf16[4,6272]{1,0:T(4,128)(2,1)S(1)}, bf16[4,6272]{1,0:T(4,128)(2,1)S(1)}, u32[]{:S(2)}, u32[]{:S(2)}) %collective-permute-start.6) | collective-permute-done | bytes 50208 | tf_op jit(solution)/shard_map/ppermute | solution.py:268
  19.9 1.9 %collective-permute-done.7.refs_2_ = bf16[4,6272]{1,0:T(4,128)(2,1)S(1)} collective-permute-done((bf16[4,6272]{1,0:T(4,128)(2,1)S(1)}, bf16[4,6272]{1,0:T(4,128)(2,1)S(1)}, u32[]{:S(2)}, u32[]{:S(2)}) %collective-permute-start.7) | collective-permute-done | bytes 50208 | tf_op jit(solution)/shard_map/ppermute | solution.py:268
  21.8 2.4 %collective-permute-done.8.refs_3_ = bf16[4,6272]{1,0:T(4,128)(2,1)S(1)} collective-permute-done((bf16[4,6272]{1,0:T(4,128)(2,1)S(1)}, bf16[4,6272]{1,0:T(4,128)(2,1)S(1)}, u32[]{:S(2)}, u32[]{:S(2)}) %collective-permute-start.8) | collective-permute-done | bytes 50208 | tf_op jit(solution)/shard_map/ppermute | solution.py:268
  24.3 0.6 %shard_map.108 = (f32[208,128]{1,0:T(8,128)S(1)}, bf16[208,128]{1,0:T(8,128)(2,1)S(1)}) custom-call(s32[2,48]{1,0:T(2,128)S(1)} %add_add_fusion.idx_ref, bf16[4,6272]{1,0:T(4,128)(2,1)S(1)} %get-tuple-element.16.refs_0_, bf16[4,6272]{1,0:T(4,128)(2,1)S(1)} %collective-permute-done.6.refs_1_, bf16[4,6272]{1,0:T(4,128)(2,1)S(1)} %collective-permute-done.7.refs_2_, ...), custom_call_target="tpu_custom_call" | custom-call | flops 98304 | bytes 393216 | tf_op jit(solution)/shard_map/pallas_call | solution.py:332
  24.9 1.6 %collective-permute-start.9 = (bf16[208,128]{1,0:T(8,128)(2,1)S(1)}, bf16[208,128]{1,0:T(8,128)(2,1)S(1)}, u32[]{:S(2)}, u32[]{:S(2)}) collective-permute-start(bf16[208,128]{1,0:T(8,128)(2,1)S(1)} %get-tuple-element.21), channel_id=1, source_target_pairs={{0,8},{8,0},{16,24},{24,16},{1,9},{9,1},{17,25},{25,17},{2,10},{10... | collective-permute-start | bytes 159752 | tf_op jit(solution)/shard_map/ppermute | solution.py:268
  26.6 2.6 %collective-permute-done.9 = bf16[208,128]{1,0:T(8,128)(2,1)S(1)} collective-permute-done((bf16[208,128]{1,0:T(8,128)(2,1)S(1)}, bf16[208,128]{1,0:T(8,128)(2,1)S(1)}, u32[]{:S(2)}, u32[]{:S(2)}) %collective-permute-start.9) | collective-permute-done | bytes 53280 | tf_op jit(solution)/shard_map/ppermute | solution.py:268
  29.1 2.8 %collective-permute-start.10 = (bf16[112,128]{1,0:T(8,128)(2,1)S(1)}, bf16[112,128]{1,0:T(8,128)(2,1)S(1)}, u32[]{:S(2)}, u32[]{:S(2)}) collective-permute-start(bf16[112,128]{1,0:T(8,128)(2,1)S(1)} %concatenate.10), channel_id=1, source_target_pairs={{0,16},{8,24},{16,0},{24,8},{1,17},{9,25},{17,1},{25,9},{2,18},{10... | collective-permute-start | bytes 86024 | tf_op jit(solution)/shard_map/ppermute | solution.py:268
  32.0 1.3 %shard_map.109.sel_ref = f32[2,24,16,128]{3,2,1,0:T(8,128)S(1)} custom-call(s32[2,48]{1,0:T(2,128)S(1)} %add_add_fusion.idx_ref, bf16[16,6144]{1,0:T(8,128)(2,1)S(1)} %copy-done), custom_call_target="tpu_custom_call" | custom-call | flops 98304 | bytes 393216 | tf_op jit(solution)/shard_map/pallas_call | solution.py:324
  33.4 0.6 %collective-permute-done.10.recv_ref = bf16[112,128]{1,0:T(8,128)(2,1)S(1)} collective-permute-done((bf16[112,128]{1,0:T(8,128)(2,1)S(1)}, bf16[112,128]{1,0:T(8,128)(2,1)S(1)}, u32[]{:S(2)}, u32[]{:S(2)}) %collective-permute-start.10) | collective-permute-done | bytes 28704 | tf_op jit(solution)/shard_map/ppermute | solution.py:268
  34.0 0.8 %shard_map.110 = (f32[1,2,2,24,128]{4,3,2,1,0:T(8,128)}, f32[1,2,24,128]{3,2,1,0:T(8,128)}) custom-call(f32[96,128]{1,0:T(8,128)S(1)} %slice.11.acc_ref, bf16[112,128]{1,0:T(8,128)(2,1)S(1)} %collective-permute-done.10.recv_ref, f32[16,128]{1,0:T(8,128)S(1)} %slice.12.bins_ref, f32[2,24,16,128]{3,2,1,0:T(8,128)S(1)} %shard_map.109.sel_ref), custom_call_target="tpu_custom_call" | custom-call | flops 1000 | bytes 98304 | tf_op jit(solution)/shard_map/pallas_call | solution.py:353
  (8 shorter events, 0.1 us)
Async XLA Ops:
  0.6 9.8 %copy-start.1 = (f32[8,6144]{1,0:T(8,128)S(1)}, f32[8,6144]{1,0:T(8,128)}, u32[]{:S(2)}) copy-start(f32[8,6144]{1,0:T(8,128)} %constant.75.clone.trig_ref.refs_10_.refs_9_) | copy-start | bytes 589828
  0.6 9.8 %copy-start = (bf16[16,6144]{1,0:T(8,128)(2,1)S(1)}, bf16[16,6144]{1,0:T(8,128)(2,1)}, u32[]{:S(2)}) copy-start(bf16[16,6144]{1,0:T(8,128)(2,1)} %table_ref.5) | copy-start | bytes 589828
  1.6 9.6 %collective-permute-start.2 = (bf16[4,6144]{1,0:T(4,128)(2,1)S(1)}, bf16[4,6144]{1,0:T(4,128)(2,1)S(1)}, u32[]{:S(2)}, u32[]{:S(2)}) collective-permute-start(bf16[4,6144]{1,0:T(4,128)(2,1)S(1)} %reshape.138.refs_0_), channel_id=1, source_target_pairs={{0,2},{1,3},{2,0},{3,1},{4,6},{5,7},{6,4},{7,5},{8,10},{9,11},{10,... | collective-permute-start | bytes 147464 | tf_op jit(solution)/shard_map/ppermute | solution.py:268
  4.6 6.6 %collective-permute-start.3 = (bf16[4,6144]{1,0:T(4,128)(2,1)S(1)}, bf16[4,6144]{1,0:T(4,128)(2,1)S(1)}, u32[]{:S(2)}, u32[]{:S(2)}) collective-permute-start(bf16[4,6144]{1,0:T(4,128)(2,1)S(1)} %reshape.138.refs_0_), channel_id=1, source_target_pairs={{0,4},{1,5},{2,6},{3,7},{4,0},{5,1},{6,2},{7,3},{8,12},{9,13},{10,... | collective-permute-start | bytes 147464 | tf_op jit(solution)/shard_map/ppermute | solution.py:268
  6.1 5.1 %collective-permute-start.4 = (bf16[4,6144]{1,0:T(4,128)(2,1)S(1)}, bf16[4,6144]{1,0:T(4,128)(2,1)S(1)}, u32[]{:S(2)}, u32[]{:S(2)}) collective-permute-start(bf16[4,6144]{1,0:T(4,128)(2,1)S(1)} %reshape.138.refs_0_), channel_id=1, source_target_pairs={{0,6},{1,7},{2,4},{3,5},{4,2},{5,3},{6,0},{7,1},{8,14},{9,15},{10,... | collective-permute-start | bytes 147464 | tf_op jit(solution)/shard_map/ppermute | solution.py:268
  7.7 3.1 %collective-permute-start.1 = (s32[16,9]{1,0:T(8,128)S(1)}, s32[16,9]{1,0:T(8,128)S(1)}, u32[]{:S(2)}, u32[]{:S(2)}) collective-permute-start(s32[16,9]{1,0:T(8,128)S(1)} %pad_add_fusion.ints_ref.refs_6_.refs_7_), channel_id=1, source_target_pairs={{0,1},{1,0},{2,3},{3,2},{4,5},{5,4},{6,7},{7,6},{8,9},{9,8},{10,11... | collective-permute-start | bytes 1736 | tf_op jit(solution)/shard_map/ppermute | solution.py:268
  8.8 2.0 %collective-permute-start = (bf16[32,6144]{1,0:T(8,128)(2,1)S(1)}, bf16[32,6144]{1,0:T(8,128)(2,1)S(1)}, u32[]{:S(2)}, u32[]{:S(2)}) collective-permute-start(bf16[32,6144]{1,0:T(8,128)(2,1)S(1)} %bitcast.5), channel_id=1, source_target_pairs={{0,1},{1,0},{2,3},{3,2},{4,5},{5,4},{6,7},{7,6},{8,9},{9,8},{10,11... | collective-permute-start | bytes 1179656 | tf_op jit(solution)/shard_map/ppermute | solution.py:268
  10.8 0.7 %copy-start.2 = (f32[6144]{0:T(1024)S(1)}, f32[6144]{0:T(1024)}, u32[]{:S(2)}) copy-start(f32[6144]{0:T(1024)} %param.14) | copy-start | bytes 73732
  13.7 1.2 %collective-permute-start.5 = (f32[32,128]{1,0:T(8,128)S(1)}, f32[32,128]{1,0:T(8,128)S(1)}, u32[]{:S(2)}, u32[]{:S(2)}) collective-permute-start(f32[32,128]{1,0:T(8,128)S(1)} %get-tuple-element.15.refs_5_), channel_id=1, source_target_pairs={{0,1},{1,0},{2,3},{3,2},{4,5},{5,4},{6,7},{7,6},{8,9},{9,8},{10,11... | collective-permute-start | bytes 49160 | tf_op jit(solution)/shard_map/ppermute | solution.py:268
  15.7 4.2 %collective-permute-start.6 = (bf16[4,6272]{1,0:T(4,128)(2,1)S(1)}, bf16[4,6272]{1,0:T(4,128)(2,1)S(1)}, u32[]{:S(2)}, u32[]{:S(2)}) collective-permute-start(bf16[4,6272]{1,0:T(4,128)(2,1)S(1)} %get-tuple-element.17), channel_id=1, source_target_pairs={{0,2},{1,3},{2,0},{3,1},{4,6},{5,7},{6,4},{7,5},{8,10},{9,11},{10,... | collective-permute-start | bytes 150536 | tf_op jit(solution)/shard_map/ppermute | solution.py:268
  17.7 4.1 %collective-permute-start.7 = (bf16[4,6272]{1,0:T(4,128)(2,1)S(1)}, bf16[4,6272]{1,0:T(4,128)(2,1)S(1)}, u32[]{:S(2)}, u32[]{:S(2)}) collective-permute-start(bf16[4,6272]{1,0:T(4,128)(2,1)S(1)} %get-tuple-element.18), channel_id=1, source_target_pairs={{0,4},{1,5},{2,6},{3,7},{4,0},{5,1},{6,2},{7,3},{8,12},{9,13},{10,... | collective-permute-start | bytes 150536 | tf_op jit(solution)/shard_map/ppermute | solution.py:268
  19.3 5.0 %collective-permute-start.8 = (bf16[4,6272]{1,0:T(4,128)(2,1)S(1)}, bf16[4,6272]{1,0:T(4,128)(2,1)S(1)}, u32[]{:S(2)}, u32[]{:S(2)}) collective-permute-start(bf16[4,6272]{1,0:T(4,128)(2,1)S(1)} %get-tuple-element.19), channel_id=1, source_target_pairs={{0,6},{1,7},{2,4},{3,5},{4,2},{5,3},{6,0},{7,1},{8,14},{9,15},{10,... | collective-permute-start | bytes 150536 | tf_op jit(solution)/shard_map/ppermute | solution.py:268
  24.9 4.2 %collective-permute-start.9 = (bf16[208,128]{1,0:T(8,128)(2,1)S(1)}, bf16[208,128]{1,0:T(8,128)(2,1)S(1)}, u32[]{:S(2)}, u32[]{:S(2)}) collective-permute-start(bf16[208,128]{1,0:T(8,128)(2,1)S(1)} %get-tuple-element.21), channel_id=1, source_target_pairs={{0,8},{8,0},{16,24},{24,16},{1,9},{9,1},{17,25},{25,17},{2,10},{10... | collective-permute-start | bytes 159752 | tf_op jit(solution)/shard_map/ppermute | solution.py:268
  29.1 4.8 %collective-permute-start.10 = (bf16[112,128]{1,0:T(8,128)(2,1)S(1)}, bf16[112,128]{1,0:T(8,128)(2,1)S(1)}, u32[]{:S(2)}, u32[]{:S(2)}) collective-permute-start(bf16[112,128]{1,0:T(8,128)(2,1)S(1)} %concatenate.10), channel_id=1, source_target_pairs={{0,16},{8,24},{16,0},{24,8},{1,17},{9,25},{17,1},{25,9},{2,18},{10... | collective-permute-start | bytes 86024 | tf_op jit(solution)/shard_map/ppermute | solution.py:268

commit v2 on v1

v2 whole, which is shorter than its diff:
```python
import functools
import math

import jax
import jax.numpy as jnp
import numpy as np
from jax import lax
from jax.experimental import pallas as pl
from jax.experimental.pallas import tpu as pltpu
from jax.sharding import PartitionSpec as P

LINE_LEN = 128
STEP = 2.0 * math.pi / LINE_LEN
VMEM_BYTES = 40 * 1024 * 1024
f32 = jnp.float32
bf16 = jnp.bfloat16
exact = lax.Precision.HIGHEST
last_last = (((1,), (1,)), ((), ()))
first_first = (((0,), (0,)), ((), ()))


def trig_rows():
    column = np.arange(LINE_LEN)
    freq = np.where(column < LINE_LEN // 2, column, column - LINE_LEN)
    rows = np.zeros((8, LINE_LEN), np.float32)
    rows[0] = np.cos(freq * STEP)
    rows[1] = np.sin(freq * STEP)
    return rows


def far_first(count):
    return reversed(range(1, count))


def call(kernel, out_shape, flops=0, moved=0, **kw):
    return pl.pallas_call(
        kernel,
        out_shape=out_shape,
        compiler_params=pltpu.CompilerParams(vmem_limit_bytes=VMEM_BYTES),
        cost_estimate=pl.CostEstimate(flops=flops, bytes_accessed=moved, transcendentals=0),
        **kw,
    )


def spread(first, second):
    rows, n = first.shape
    rest = jnp.full((rows, LINE_LEN - 2 * n), -1, jnp.int32)
    return jnp.concatenate([first, second, rest], axis=1)


def onehot_of(d0_ref, d1_ref, bins):
    row = spread(d0_ref[...], d1_ref[...])
    return (row == lax.broadcasted_iota(jnp.int32, (bins, LINE_LEN), 0)).astype(f32)


def prep_half(h, part, defocus, tab_ref, y_ref, scr_ref, ctf_ref):
    n = defocus.shape[1]
    bins, pixels = tab_ref.shape
    lines = pixels // LINE_LEN
    onehot = (defocus == lax.broadcasted_iota(jnp.int32, (bins, n), 0)).astype(f32)
    scr_ref[...] = part.astype(f32)
    ctf_ref[...] = lax.dot_general(
        onehot.astype(bf16), tab_ref[...], first_first, preferred_element_type=f32
    )
    for l in range(lines):
        cols = slice(l * LINE_LEN, (l + 1) * LINE_LEN)
        ctf = ctf_ref[:, cols]
        for part in range(2):
            x = scr_ref[pl.ds(2 * l + part, n, stride=2 * lines), :] * ctf
            base = (2 * part + h) * n
            y_ref[base : base + n, cols] = x.astype(bf16)
            base += 4 * n
            y_ref[base : base + n, cols] = (x * math.cos(l * STEP)).astype(bf16)
            base += 4 * n
            y_ref[base : base + n, cols] = (x * math.sin(l * STEP)).astype(bf16)


def own_kernel(p_hbm, t_hbm, d_hbm, y_ref, tab_ref, raw_ref, d_ref, scr_ref, ctf_ref, sems):
    copies = [
        pltpu.make_async_copy(src, dst, sems.at[i])
        for i, (src, dst) in enumerate(((t_hbm, tab_ref), (p_hbm, raw_ref), (d_hbm, d_ref)))
    ]
    for copy in copies:
        copy.start()
    for copy in copies:
        copy.wait()
    prep_half(0, raw_ref[...], d_ref[...], tab_ref, y_ref, scr_ref, ctf_ref)


def partner_kernel(p_ref, tab_ref, d_ref, half_ref, y_ref, scr_ref, ctf_ref):
    prep_half(1, p_ref[...], d_ref[...], tab_ref, y_ref, scr_ref, ctf_ref)


def score_kernel(chunks, *refs):
    p_refs = refs[:chunks]
    y_ref, tab_ref, d0_ref, d1_ref, c0_ref, c1_ref, noise_ref, trig_ref, pid_ref = refs[
        chunks : chunks + 9
    ]
    m_ref, s_ref, stat_ref = refs[chunks + 9 : chunks + 12]
    scr_ref, r_ref, g_ref = refs[chunks + 12 :]
    n = d0_ref.shape[1]
    bins, pixels = tab_ref.shape
    lines = pixels // LINE_LEN
    half = 2 * chunks
    wide = 2 * half
    size = 4 * lines
    for s, p in enumerate(p_refs):
        scr_ref[s * size : (s + 1) * size] = p[...].astype(f32)
    cos_row, sin_row = trig_ref[0:1], trig_ref[1:2]
    power = [None] * half
    for l in range(lines):
        cols = slice(l * LINE_LEN, (l + 1) * LINE_LEN)
        x = jnp.concatenate(
            [scr_ref[pl.ds(2 * l + part, half, stride=2 * lines), :] for part in range(2)], axis=0
        )
        one = x * noise_ref[:, cols]
        r_ref[0:wide, cols] = one.astype(bf16)
        r_ref[wide : 2 * wide, cols] = (one * cos_row).astype(bf16)
        r_ref[2 * wide : 3 * wide, cols] = (one * sin_row).astype(bf16)
        square = one * x
        square = square[:half] + square[half:]
        t = tab_ref[:, cols].astype(f32)
        t = t * t
        for j in range(half):
            term = t * square[j : j + 1]
            power[j] = term if l == 0 else power[j] + term
    g_ref[:, : y_ref.shape[0]] = lax.dot_general(
        r_ref[...], y_ref[...], last_last, preferred_element_type=f32
    )
    step = 2 * n

    def left(v, k):
        return pltpu.roll(v, LINE_LEN - k, 1) if k else v

    def right(v, k):
        return pltpu.roll(v, k, 1) if k else v

    def block(k):
        at = k * step // LINE_LEN * LINE_LEN
        return left(g_ref[: 3 * wide, at : at + LINE_LEN], k * step - at)

    even, odd = [], []
    for a in range(3):
        real, imag = block(2 * a), block(2 * a + 1)
        row = [(v * wide, v * wide + half, (v + 1) * wide) for v in range(3)]
        even.append([real[i:j] + imag[j:k] for i, j, k in row])
        odd.append([imag[i:j] - real[j:k] for i, j, k in row])
    onehot = onehot_of(d0_ref, d1_ref, bins)
    quad = 0.5 * jnp.concatenate(
        [
            jnp.sum(onehot * jnp.sum(p, axis=1, keepdims=True), axis=0, keepdims=True)
            for p in power
        ],
        axis=0,
    )
    pid = pid_ref[...]
    cand = spread(c0_ref[...], c1_ref[...])
    listed = cand[0:1] == pid
    for c in range(1, cand.shape[0]):
        listed = jnp.logical_or(listed, cand[c : c + 1] == pid)

    scores = []
    for a, sign in ((0, 0), (1, 1), (1, -1)):
        still, base, turn = even[a][0], even[a][1], odd[a][2]
        if sign == 1:
            still, base, turn = still + odd[2][0], base + odd[2][1], turn - even[2][2]
        if sign == -1:
            still, base, turn = still - odd[2][0], base - odd[2][1], turn + even[2][2]
        still, base = still - quad, base - quad
        scores.append([jnp.where(listed, v, -3.0e38) for v in (still, base + turn, base - turn)])
    peak = scores[0][0]
    for v in scores[0][1:] + scores[1] + scores[2]:
        peak = jnp.maximum(peak, v)
    peak = jnp.max(peak, axis=0, keepdims=True)
    terms = [[jnp.where(listed, jnp.exp(v - peak), 0.0) for v in group] for group in scores]
    both = [p + m for _, p, m in terms]
    diff = [p - m for _, p, m in terms]
    still = [s for s, _, _ in terms]
    total = (still[0] + both[0]) + (still[1] + both[1]) + (still[2] + both[2])
    s_ref[...] = total
    mass = jnp.sum(total, axis=0, keepdims=True)
    stat_ref[...] = jnp.concatenate([peak, mass, jnp.zeros((6, LINE_LEN), f32)], axis=0)
    alpha = [
        [still[0], both[0], None],
        [still[1] + still[2], both[1] + both[2], None],
        [None, None, diff[2] - diff[1]],
    ]
    beta = [
        [None, None, diff[0]],
        [None, None, diff[1] + diff[2]],
        [still[1] - still[2], both[1] - both[2], None],
    ]
    zero = jnp.zeros((half, LINE_LEN), f32)
    for b in range(3):
        for at in range(0, 2 * LINE_LEN, LINE_LEN):
            real, imag = zero, zero
            for a in range(3):
                for part in range(2):
                    k = (2 * a + part) * step - at
                    if not 0 <= k < LINE_LEN:
                        continue
                    if alpha[a][b] is not None:
                        if part == 0:
                            real = real + right(alpha[a][b], k)
                        else:
                            imag = imag + right(alpha[a][b], k)
                    elif part == 0:
                        imag = imag - right(beta[a][b], k)
                    else:
                        real = real + right(beta[a][b], k)
            m_ref[b * wide : (b + 1) * wide, at : at + LINE_LEN] = by_chunk(real, imag)


def by_chunk(real, imag):
    pieces = []
    for s in range(real.shape[0] // 2):
        pieces += [real[2 * s : 2 * s + 2], imag[2 * s : 2 * s + 2]]
    return jnp.concatenate(pieces, axis=0)


def slice_kernel(
    y_ref, m_ref, s_ref, stat_ref, other_ref, d0_ref, d1_ref, trig_ref, keep_ref, *send_refs
):
    n = d0_ref.shape[1]
    pixels = y_ref.shape[1]
    half = s_ref.shape[0]
    wide = 2 * half
    lane = lax.broadcasted_iota(jnp.int32, (1, LINE_LEN), 1)
    other = other_ref[...]
    other = jnp.where(lane < n, pltpu.roll(other, LINE_LEN - n, 1), pltpu.roll(other, n, 1))
    peak0, mass0 = stat_ref[0:1], stat_ref[1:2]
    peak1, mass1 = other[0:1], other[1:2]
    peak = jnp.maximum(peak0, peak1)
    grow = jnp.exp(peak0 - peak)
    scale = grow / (mass0 * grow + mass1 * jnp.exp(peak1 - peak))
    scale = jnp.where(lane < 2 * n, scale, 0.0)
    share = lax.dot_general(
        s_ref[...] * scale,
        onehot_of(d0_ref, d1_ref, LINE_LEN),
        last_last,
        precision=exact,
        preferred_element_type=f32,
    )
    share = by_chunk(share, jnp.zeros_like(share))
    scales = scale
    for k in range(2 * n, LINE_LEN, 2 * n):
        scales = scales + pltpu.roll(scale, k, 1)
    m = m_ref[...] * jnp.concatenate([scales, scales], axis=1)
    m = m.astype(bf16)[:, : 12 * n]
    width = 1024
    cos_row = jnp.concatenate([trig_ref[0:1]] * (width // LINE_LEN), axis=1)
    sin_row = jnp.concatenate([trig_ref[1:2]] * (width // LINE_LEN), axis=1)
    for c in range(pixels // width):
        cols = slice(c * width, (c + 1) * width)
        x = jnp.dot(m, y_ref[:, cols], preferred_element_type=f32)
        x = x[:wide] + x[wide : 2 * wide] * cos_row + x[2 * wide :] * sin_row
        keep_ref[:, cols] = x[:4]
        for s, ref in enumerate(send_refs, 1):
            ref[:, cols] = x[4 * s : 4 * s + 4].astype(bf16)
    keep_ref[:, pixels:] = share[:4]
    for s, ref in enumerate(send_refs, 1):
        ref[:, pixels:] = share[4 * s : 4 * s + 4].astype(bf16)


def pack_kernel(lines, cap, groups, chunks, idx_ref, own_ref, *refs):
    recv_refs = refs[: chunks - 1]
    keep_ref, *send_refs, scr_ref = refs[chunks - 1 :]
    size = 4 * cap
    scr_ref[...] = jnp.zeros(scr_ref.shape, f32)
    for l in range(lines + 1):
        cols = slice(l * LINE_LEN, (l + 1) * LINE_LEN)
        x = own_ref[:, cols]
        for ref in recv_refs:
            x = x + ref[:, cols].astype(f32)
        if l < lines:
            for j in range(2):
                row = idx_ref[j, l]
                scr_ref[pl.ds(row, 1), :] = x[j : j + 1]
                scr_ref[pl.ds(row + cap, 1), :] = x[2 + j : 3 + j]
        else:
            tail = jnp.concatenate([x, jnp.zeros((12, LINE_LEN), f32)], axis=0)
    keep_ref[:size] = scr_ref[:size]
    keep_ref[size:] = tail
    for r, ref in enumerate(send_refs, 1):
        ref[:size] = scr_ref[r * size : (r + 1) * size].astype(bf16)
        ref[size:] = tail.astype(bf16)


def table_kernel(lines, cap, idx_ref, table_ref, sel_ref):
    bins = table_ref.shape[0]
    sel_ref[...] = jnp.zeros(sel_ref.shape, f32)
    for l in range(lines):
        t = table_ref[:, l * LINE_LEN : (l + 1) * LINE_LEN].astype(f32)
        t = t * t
        for j in range(2):
            slot = idx_ref[j, l]

            @pl.when(slot < 4 * cap)
            def _():
                sel_ref[j, pl.ds(slot - 2 * cap * j, 1)] = t[None]


def final_kernel(cap, scale, own_ref, *refs):
    *recv_refs, sel_ref, data_ref, weight_ref = refs
    x = own_ref[...]
    for ref in recv_refs:
        x = x + ref[...].astype(f32)
    data_ref[...] = x[: 4 * cap].reshape(data_ref.shape)
    bt = jnp.transpose(x[4 * cap :] * scale)[: sel_ref.shape[2]]
    for j in range(2):
        weight_ref[0, j] = jnp.sum(sel_ref[j] * bt[:, j : j + 1][None], axis=1)


def body(
    particles, defocus_bin, candidates, projections, ctf_table, inv_noise, line_slab, slab_owner
):
    n, _, pixels = particles.shape
    groups = lax.axis_size("grp")
    members = lax.axis_size("dev")
    chunks = members // 2
    chip_bits = chunks.bit_length() - 1
    lines = line_slab.shape[1]
    cap = 2 * lines // groups
    bins = ctf_table.shape[0]
    wide = 4 * chunks
    dev = lax.axis_index("dev")
    grp = lax.axis_index("grp")
    trig = jnp.asarray(trig_rows())
    noise = inv_noise[None, :]

    def swap(x, axis, size, mask):
        return lax.ppermute(x, axis, [(i, i ^ mask) for i in range(size)])

    def turned(t):
        k = chip_bits // 2
        return ((t << k) | (t >> (chip_bits - k))) & (chunks - 1)

    def to_place(x, t):
        return lax.ppermute(
            x, "dev", [(i, i ^ (2 * (turned(t) if i % 2 else t))) for i in range(members)]
        )

    def as_lines(x):
        count = x.shape[0]
        x = x.reshape(count, 2, lines, LINE_LEN)
        return jnp.transpose(x, (0, 2, 1, 3)).reshape(2 * count * lines, LINE_LEN)

    part0, part1 = as_lines(particles), as_lines(swap(particles, "dev", members, 1))
    def0, def1 = defocus_bin[None, :], swap(defocus_bin, "dev", members, 1)[None, :]
    cand0, cand1 = candidates.T, swap(candidates, "dev", members, 1).T
    proj = {t: to_place(projections, t) for t in far_first(chunks)}
    proj = [as_lines(p) for p in [projections] + [proj[t] for t in range(1, chunks)]]

    def in_hbm(x):
        return pltpu.with_memory_space_constraint(x, pltpu.HBM)

    vmem = pl.BlockSpec(memory_space=pltpu.VMEM)
    hbm = pl.BlockSpec(memory_space=pl.ANY)
    scratch = [pltpu.VMEM((2 * n * lines, LINE_LEN), f32), pltpu.VMEM((n, pixels), f32)]
    y, table = call(
        own_kernel,
        (
            jax.ShapeDtypeStruct((12 * n, pixels), bf16),
            jax.ShapeDtypeStruct((bins, pixels), bf16),
        ),
        in_specs=[hbm] * 3,
        scratch_shapes=[
            pltpu.VMEM((2 * n * lines, LINE_LEN), bf16),
            pltpu.VMEM((1, n), jnp.int32),
            *scratch,
            pltpu.SemaphoreType.DMA((3,)),
        ],
        flops=20 * n * pixels,
        moved=32 * n * pixels,
    )(in_hbm(part0), in_hbm(ctf_table), in_hbm(def0))
    y = call(
        partner_kernel,
        jax.ShapeDtypeStruct((12 * n, pixels), bf16),
        in_specs=[vmem, vmem, vmem, hbm],
        scratch_shapes=scratch,
        input_output_aliases={3: 0},
        flops=20 * n * pixels,
        moved=32 * n * pixels,
    )(part1, table, def1, y)

    row = lax.broadcasted_iota(jnp.int32, (2 * chunks, LINE_LEN), 0)
    far = jnp.where(dev % 2 == 0, row // 2, turned(row // 2))
    pid = 4 * ((dev // 2) ^ far) + 2 * (dev % 2) + row % 2
    m, share, stat = call(
        functools.partial(score_kernel, chunks),
        (
            jax.ShapeDtypeStruct((3 * wide, 2 * LINE_LEN), f32),
            jax.ShapeDtypeStruct((2 * chunks, LINE_LEN), f32),
            jax.ShapeDtypeStruct((8, LINE_LEN), f32),
        ),
        scratch_shapes=[
            pltpu.VMEM((4 * lines * chunks, LINE_LEN), f32),
            pltpu.VMEM((3 * wide, pixels), bf16),
            pltpu.VMEM((3 * wide, 2 * LINE_LEN), f32),
        ],
        flops=2 * 192 * 3 * wide * pixels,
        moved=30 * n * pixels,
    )(*proj, y, table, def0, def1, cand0, cand1, noise, trig, pid)
    line_slab, stat = lax.optimization_barrier((line_slab, stat))
    other = swap(stat, "dev", members, 1)
    own, *send = call(
        slice_kernel,
        (jax.ShapeDtypeStruct((4, pixels + LINE_LEN), f32),)
        + (jax.ShapeDtypeStruct((4, pixels + LINE_LEN), bf16),) * (chunks - 1),
        flops=2 * 192 * 3 * wide * pixels,
        moved=30 * n * pixels,
    )(y, m, share, stat, other, def0, def1, trig)
    got = [to_place(send[t - 1], t) for t in far_first(chunks)]

    group_ids = jnp.arange(groups, dtype=jnp.int32)
    slab_hit = line_slab[:, :, None] == group_ids[None, None, :]
    owner_line = jnp.sum(jnp.where(slab_hit, slab_owner[None, None, :], 0), axis=2)
    line_ids = jnp.arange(lines, dtype=jnp.int32)
    earlier = line_ids[None, :] < line_ids[:, None]
    same_owner = owner_line[:, :, None] == owner_line[:, None, :]
    line_rank = jnp.sum(jnp.logical_and(same_owner, earlier[None]), axis=2)
    rel = owner_line ^ grp
    idx = (4 * cap) * rel + 2 * cap * jnp.arange(2, dtype=jnp.int32)[:, None] + line_rank
    idx = idx.astype(jnp.int32)

    sel = call(
        functools.partial(table_kernel, lines, cap),
        jax.ShapeDtypeStruct((2, cap, bins, LINE_LEN), f32),
        in_specs=[pl.BlockSpec(memory_space=pltpu.SMEM), pl.BlockSpec(memory_space=pltpu.VMEM)],
        flops=bins * pixels,
        moved=4 * bins * pixels,
    )(idx, table)
    size = 4 * cap + 16
    keep, *send = call(
        functools.partial(pack_kernel, lines, cap, groups, chunks),
        (jax.ShapeDtypeStruct((size, LINE_LEN), f32),)
        + (jax.ShapeDtypeStruct((size, LINE_LEN), bf16),) * (groups - 1),
        in_specs=[pl.BlockSpec(memory_space=pltpu.SMEM)] + [vmem] * chunks,
        scratch_shapes=[pltpu.VMEM((4 * cap * groups, LINE_LEN), f32)],
        flops=16 * pixels,
        moved=64 * pixels,
    )(idx, own, *got)
    recv = [swap(send[r - 1], "grp", groups, r) for r in far_first(groups)]
    weight_scale = 2 * members / (n * groups * members)
    return call(
        functools.partial(final_kernel, cap, weight_scale),
        (
            jax.ShapeDtypeStruct((1, 2, 2, cap, LINE_LEN), f32),
            jax.ShapeDtypeStruct((1, 2, cap, LINE_LEN), f32),
        ),
        flops=1000,
        moved=8 * 4 * cap * LINE_LEN,
    )(keep, *recv, sel)


def solution(mesh):
    return jax.shard_map(
        body,
        mesh=mesh,
        in_specs=(
            P(("grp", "dev"), None, None),
            P(("grp", "dev")),
            P(("grp", "dev"), None),
            P("dev", None, None),
            P(),
            P(),
            P("dev", None),
            P(),
        ),
        out_specs=(P("grp", "dev", None, None, None), P("grp", "dev", None, None)),
        check_vma=False,
    )
```

time: 35.1 us -> 30.1 us (0.86)
  local copies, waits for them, and re-layouts: 3.87 us -> 0.04 us
  waiting for transfers between devices: 9.27 us -> 7.93 us
  Pallas kernels: 6.47 us -> 7.47 us
  other arithmetic: 1.15 us -> 0.45 us
    ppermute x0 -> x6, starting transfers between devices: none -> 8.16 us  [to_place(): lax.ppermute(x, 'dev', [(i, i ^ 2 * (turned(t) if i % 2 else t)) for i in...]
    ppermute x11 -> x7, starting transfers between devices: 13.2 us -> 5.11 us  [swap(): return lax.ppermute(x, axis, [(i, i ^ mask) for i in range(size)])]
    ppermute x11 -> x7, waiting for transfers between devices: 9.27 us -> 4.01 us  [swap(): return lax.ppermute(x, axis, [(i, i ^ mask) for i in range(size)])]
    ppermute x0 -> x6, waiting for transfers between devices: none -> 3.92 us  [to_place(): lax.ppermute(x, 'dev', [(i, i ^ 2 * (turned(t) if i % 2 else t)) for i in...]
    transpose x2 -> x0, local copies, waits for them, and re-layouts: 2 us -> none  [the longest x1 1.12 us: body(): part0 = jnp.transpose(particles, (1, 0, 2)).reshape(2 * n, pixels)]
    unnamed x7 -> x14, local copies, waits for them, and re-layouts: 1.1 us -> 0.04 us
    pallas_call x5, Pallas kernels: 4.32 us -> 5.3 us  [the longest x1 1.88 us: body(): call(own_kernel, (jax.ShapeDtypeStruct((12 * n, pixels), bf16), jax.Shape...]
    broadcast_in_dim x1 -> x0, local copies, waits for them, and re-layouts: 0.73 us -> none  [body(): ints0 = jnp.concatenate([defocus_bin[:, None], candidates], axis=1)]
  transfers between devices with their start and end apart: 11 -> 13, of which waited for: 6 -> 7; matrix products, arithmetic and copies ran while one was open for 11% -> 1% of each run, Pallas kernels for 6% -> 13%
where the time goes in v2:
time: 30.1 us; the launch traced here: 30 us
  starting transfers between devices  13.3 us (44%)
  waiting for transfers between devices  7.93 us (26%)
  Pallas kernels  7.47 us (25%)
  between operations  0.84 us (3%)
  other arithmetic  0.45 us (1%)
    ppermute x6, starting transfers between devices, to_place(): lax.ppermute(x, 'dev', [(i, i ^ 2 * (turned(t) if i % 2 else t)) for i in...  8.16 us
    ppermute x7, starting transfers between devices, swap(): return lax.ppermute(x, axis, [(i, i ^ mask) for i in range(size)])  5.11 us
    ppermute x7, waiting for transfers between devices, swap(): return lax.ppermute(x, axis, [(i, i ^ mask) for i in range(size)])  4.01 us
    ppermute x6, waiting for transfers between devices, to_place(): lax.ppermute(x, 'dev', [(i, i ^ 2 * (turned(t) if i % 2 else t)) for i in...  3.92 us
    pallas_call x1, Pallas kernels, body(): call(own_kernel, (jax.ShapeDtypeStruct((12 * n, pixels), bf16), jax.Shape...  1.88 us
    pallas_call x1, Pallas kernels, body(): call(functools.partial(table_kernel, lines, cap), jax.ShapeDtypeStruct((2...  1.35 us
    pallas_call x1, Pallas kernels, body(): call(functools.partial(score_kernel, chunks), (jax.ShapeDtypeStruct((3 *...  1.29 us
    pallas_call x1, Pallas kernels, body(): call(functools.partial(final_kernel, cap, weight_scale), (jax.ShapeDtypeS...  0.81 us
  transfers between devices with their start and end apart: 13, of which 7 were waited for; matrix products, arithmetic and copies ran while one was open for 1% of the time, Pallas kernels for 13%

profile of v2, /device:TPU:0, one launch (start us, length us, event | category | flops | bytes accessed | tf_op | source)
XLA Modules:
  0.0 30.0 jit_solution(6681484989870465940)
XLA Ops:
  0.6 4.0 %collective-permute-start.2 = (bf16[2,2,6144]{2,1,0:T(2,128)(2,1)}, bf16[2,2,6144]{2,1,0:T(2,128)(2,1)S(1)}, u32[]{:S(2)}, u32[]{:S(2)}) collective-permute-start(bf16[2,2,6144]{2,1,0:T(2,128)(2,1)} %param.12), channel_id=1, source_target_pairs={{0,6},{1,7},{2,4},{3,5},{4,2},{5,3},{6,0},{7,1},{8,14},{9,15},{10,... | collective-permute-start | bytes 147464 | tf_op jit(solution)/shard_map/ppermute | solution.py:339
  4.6 0.5 %collective-permute-start = (bf16[2,2,6144]{2,1,0:T(2,128)(2,1)}, bf16[2,2,6144]{2,1,0:T(2,128)(2,1)S(1)}, u32[]{:S(2)}, u32[]{:S(2)}) collective-permute-start(bf16[2,2,6144]{2,1,0:T(2,128)(2,1)} %param.12), channel_id=1, source_target_pairs={{0,2},{1,5},{2,0},{3,7},{4,6},{5,1},{6,4},{7,3},{8,10},{9,13},{10,... | collective-permute-start | bytes 147464 | tf_op jit(solution)/shard_map/ppermute | solution.py:339
  5.1 0.1 collective-permute-start.1
  5.2 0.0 collective-permute-start.4
  5.2 0.5 %collective-permute-start.3 = (bf16[16,2,6144]{2,1,0:T(2,128)(2,1)}, bf16[16,2,6144]{2,1,0:T(2,128)(2,1)S(1)}, u32[]{:S(2)}, u32[]{:S(2)}) collective-permute-start(bf16[16,2,6144]{2,1,0:T(2,128)(2,1)} %param.9), channel_id=1, source_target_pairs={{0,1},{1,0},{2,3},{3,2},{4,5},{5,4},{6,7},{7,6},{8,9},{9,8},{10,11... | collective-permute-start | bytes 1179656 | tf_op jit(solution)/shard_map/ppermute | solution.py:332
  5.8 0.1 fusion.5.refs_12_
  5.9 1.9 %shard_map.104 = (bf16[192,6144]{1,0:T(8,128)(2,1)S(1)}, bf16[16,6144]{1,0:T(8,128)(2,1)S(1)}) custom-call(bf16[1536,128]{1,0:T(8,128)(2,1)} %bitcast.49, bf16[16,6144]{1,0:T(8,128)(2,1)} %t_hbm.1, s32[1,16]{1,0:T(1,128)} %bitcast.44), custom_call_target="tpu_custom_call" | custom-call | flops 1966080 | bytes 3145728 | tf_op jit(solution)/shard_map/pallas_call | solution.py:360
  7.8 0.0 collective-permute-done.4
  7.8 0.1 collective-permute-start.5
  7.9 0.0 collective-permute-done.3
  7.9 0.0 copy-start
  7.9 0.0 copy-start.1
  7.9 0.0 copy-start.2
  7.9 0.0 copy-start.3
  7.9 0.0 copy-start.4
  7.9 0.7 %shard_map.105.refs_4_.y_ref = bf16[192,6144]{1,0:T(8,128)(2,1)S(1)} custom-call(bf16[1536,128]{1,0:T(8,128)(2,1)S(1)} %bitcast.35, bf16[16,6144]{1,0:T(8,128)(2,1)S(1)} %get-tuple-element.17.tab_ref.refs_5_.table_ref, s32[1,16]{1,0:T(1,128)S(1)} %bitcast.41, bf16[192,6144]{1,0:T(8,128)(2,1)S(1)} %get-tuple-element.18.half_ref), custom_call_target="tpu_custom_call", output_to_operand_aliasing={{}: (3, {})} | custom-call | flops 1966080 | bytes 3145728 | tf_op jit(solution)/shard_map/pallas_call | solution.py:376
  8.7 0.0 copy-start.5
  8.7 0.0 copy-start.6
  8.7 0.5 %collective-permute-done.5 = s32[16,8]{0,1:T(8,128)S(1)} collective-permute-done((s32[16,8]{0,1:T(8,128)}, s32[16,8]{0,1:T(8,128)S(1)}, u32[]{:S(2)}, u32[]{:S(2)}) %collective-permute-start.5) | collective-permute-done | bytes 544 | tf_op jit(solution)/shard_map/ppermute | solution.py:332
  9.2 0.0 collective-permute-done.2
  9.2 0.0 collective-permute-done
  9.2 0.2 collective-permute-done.1
  9.4 0.0 copy-done
  9.4 0.0 copy-done.1
  9.4 0.0 copy-done.2
  9.4 0.0 copy-done.3
  9.4 0.0 copy-done.4
  9.5 1.3 %shard_map.106 = (f32[48,256]{1,0:T(8,128)S(1)}, f32[8,128]{1,0:T(8,128)S(1)}, f32[8,128]{1,0:T(8,128)S(1)}) custom-call(bf16[192,128]{1,0:T(8,128)(2,1)S(1)} %bitcast.36, bf16[192,128]{1,0:T(8,128)(2,1)S(1)} %bitcast.38, bf16[192,128]{1,0:T(8,128)(2,1)S(1)} %bitcast.39, bf16[192,128]{1,0:T(8,128)(2,1)S(1)} %bitcast.37, ...), custom_call_target="tpu_custom_call" | custom-call | flops 113246208 | bytes 2949120 | tf_op jit(solution)/shard_map/pallas_call | solution.py:389
  10.8 0.1 collective-permute-start.6
  10.8 0.0 copy-done.5
  10.8 0.0 copy-done.6
  10.9 0.1 select_reduce_fusion
  10.9 0.2 convert_reduce_fusion
  11.1 0.9 %collective-permute-done.6.other_ref = f32[8,128]{1,0:T(8,128)S(1)} collective-permute-done((f32[8,128]{1,0:T(8,128)S(1)}, f32[8,128]{1,0:T(8,128)S(1)}, u32[]{:S(2)}, u32[]{:S(2)}) %collective-permute-start.6) | collective-permute-done | bytes 4128 | tf_op jit(solution)/shard_map/ppermute | solution.py:332
  12.0 0.7 %shard_map.107 = (f32[4,6272]{1,0:T(4,128)S(1)}, bf16[4,6272]{1,0:T(4,128)(2,1)S(1)}, bf16[4,6272]{1,0:T(4,128)(2,1)S(1)}, bf16[4,6272]{1,0:T(4,128)(2,1)S(1)}) custom-call(bf16[192,6144]{1,0:T(8,128)(2,1)S(1)} %shard_map.105.refs_4_.y_ref, f32[48,256]{1,0:T(8,128)S(1)} %get-tuple-element.21.m_ref, f32[8,128]{1,0:T(8,128)S(1)} %get-tuple-element.22.s_ref, ...), custom_call_target="tpu_custom_call" | custom-call | flops 113246208 | bytes 2949120 | tf_op jit(solution)/shard_map/pallas_call | solution.py:406
  12.7 2.8 %collective-permute-start.7 = (bf16[4,6272]{1,0:T(4,128)(2,1)S(1)}, bf16[4,6272]{1,0:T(4,128)(2,1)S(1)}, u32[]{:S(2)}, u32[]{:S(2)}) collective-permute-start(bf16[4,6272]{1,0:T(4,128)(2,1)S(1)} %get-tuple-element.25), channel_id=1, source_target_pairs={{0,6},{1,7},{2,4},{3,5},{4,2},{5,3},{6,0},{7,1},{8,14},{9,15},{10,... | collective-permute-start | bytes 150536 | tf_op jit(solution)/shard_map/ppermute | solution.py:339
  15.5 0.5 %collective-permute-start.8 = (bf16[4,6272]{1,0:T(4,128)(2,1)S(1)}, bf16[4,6272]{1,0:T(4,128)(2,1)S(1)}, u32[]{:S(2)}, u32[]{:S(2)}) collective-permute-start(bf16[4,6272]{1,0:T(4,128)(2,1)S(1)} %get-tuple-element.26), channel_id=1, source_target_pairs={{0,4},{1,3},{2,6},{3,1},{4,0},{5,7},{6,2},{7,5},{8,12},{9,11},{10,... | collective-permute-start | bytes 150536 | tf_op jit(solution)/shard_map/ppermute | solution.py:339
  16.0 0.3 collective-permute-start.9
  16.3 0.1 add_add_fusion.idx_ref
  16.4 1.4 %collective-permute-done.7.refs_0_ = bf16[4,6272]{1,0:T(4,128)(2,1)S(1)} collective-permute-done((bf16[4,6272]{1,0:T(4,128)(2,1)S(1)}, bf16[4,6272]{1,0:T(4,128)(2,1)S(1)}, u32[]{:S(2)}, u32[]{:S(2)}) %collective-permute-start.7) | collective-permute-done | bytes 50208 | tf_op jit(solution)/shard_map/ppermute | solution.py:339
  17.8 1.8 %collective-permute-done.8.refs_1_ = bf16[4,6272]{1,0:T(4,128)(2,1)S(1)} collective-permute-done((bf16[4,6272]{1,0:T(4,128)(2,1)S(1)}, bf16[4,6272]{1,0:T(4,128)(2,1)S(1)}, u32[]{:S(2)}, u32[]{:S(2)}) %collective-permute-start.8) | collective-permute-done | bytes 50208 | tf_op jit(solution)/shard_map/ppermute | solution.py:339
  19.6 0.5 %collective-permute-done.9.refs_2_ = bf16[4,6272]{1,0:T(4,128)(2,1)S(1)} collective-permute-done((bf16[4,6272]{1,0:T(4,128)(2,1)S(1)}, bf16[4,6272]{1,0:T(4,128)(2,1)S(1)}, u32[]{:S(2)}, u32[]{:S(2)}) %collective-permute-start.9) | collective-permute-done | bytes 50208 | tf_op jit(solution)/shard_map/ppermute | solution.py:339
  20.1 0.7 %shard_map.108 = (f32[112,128]{1,0:T(8,128)S(1)}, bf16[112,128]{1,0:T(8,128)(2,1)S(1)}, bf16[112,128]{1,0:T(8,128)(2,1)S(1)}, bf16[112,128]{1,0:T(8,128)(2,1)S(1)}) custom-call(s32[2,48]{1,0:T(2,128)S(1)} %add_add_fusion.idx_ref, f32[4,6272]{1,0:T(4,128)S(1)} %get-tuple-element.24.own_ref, bf16[4,6272]{1,0:T(4,128)(2,1)S(1)} %collective-permute-done.7.refs_0_, ...), custom_call_target="tpu_custom_call" | custom-call | flops 98304 | bytes 393216 | tf_op jit(solution)/shard_map/pallas_call | solution.py:434
  20.8 3.7 %collective-permute-start.10 = (bf16[112,128]{1,0:T(8,128)(2,1)S(1)}, bf16[112,128]{1,0:T(8,128)(2,1)S(1)}, u32[]{:S(2)}, u32[]{:S(2)}) collective-permute-start(bf16[112,128]{1,0:T(8,128)(2,1)S(1)} %get-tuple-element.29), channel_id=1, source_target_pairs={{0,24},{8,16},{16,8},{24,0},{1,25},{9,17},{17,9},{25,1},{2,26},{10... | collective-permute-start | bytes 86024 | tf_op jit(solution)/shard_map/ppermute | solution.py:332
  24.4 0.0 collective-permute-start.11
  24.4 0.8 %collective-permute-start.12 = (bf16[112,128]{1,0:T(8,128)(2,1)S(1)}, bf16[112,128]{1,0:T(8,128)(2,1)S(1)}, u32[]{:S(2)}, u32[]{:S(2)}) collective-permute-start(bf16[112,128]{1,0:T(8,128)(2,1)S(1)} %get-tuple-element.31), channel_id=1, source_target_pairs={{0,8},{8,0},{16,24},{24,16},{1,9},{9,1},{17,25},{25,17},{2,10},{10... | collective-permute-start | bytes 86024 | tf_op jit(solution)/shard_map/ppermute | solution.py:332
  25.2 1.4 %shard_map.109.refs_3_ = f32[2,24,16,128]{3,2,1,0:T(8,128)S(1)} custom-call(s32[2,48]{1,0:T(2,128)S(1)} %add_add_fusion.idx_ref, bf16[16,6144]{1,0:T(8,128)(2,1)S(1)} %get-tuple-element.17.tab_ref.refs_5_.table_ref), custom_call_target="tpu_custom_call" | custom-call | flops 98304 | bytes 393216 | tf_op jit(solution)/shard_map/pallas_call | solution.py:426
  26.6 0.0 collective-permute-done.10.refs_0_
  26.6 2.6 %collective-permute-done.11.refs_1_ = bf16[112,128]{1,0:T(8,128)(2,1)S(1)} collective-permute-done((bf16[112,128]{1,0:T(8,128)(2,1)S(1)}, bf16[112,128]{1,0:T(8,128)(2,1)S(1)}, u32[]{:S(2)}, u32[]{:S(2)}) %collective-permute-start.11) | collective-permute-done | bytes 28704 | tf_op jit(solution)/shard_map/ppermute | solution.py:332
  29.2 0.0 collective-permute-done.12.refs_2_
  29.2 0.8 %shard_map.110 = (f32[1,2,2,24,128]{4,3,2,1,0:T(8,128)}, f32[1,2,24,128]{3,2,1,0:T(8,128)}) custom-call(f32[112,128]{1,0:T(8,128)S(1)} %get-tuple-element.28.own_ref, bf16[112,128]{1,0:T(8,128)(2,1)S(1)} %collective-permute-done.10.refs_0_, bf16[112,128]{1,0:T(8,128)(2,1)S(1)} %collective-permute-done.11.refs_1_, ...), custom_call_target="tpu_custom_call" | custom-call | flops 1000 | bytes 98304 | tf_op jit(solution)/shard_map/pallas_call | solution.py:445
  (5 shorter events, 0.0 us)
Async XLA Ops:
  0.6 8.6 %collective-permute-start.2 = (bf16[2,2,6144]{2,1,0:T(2,128)(2,1)}, bf16[2,2,6144]{2,1,0:T(2,128)(2,1)S(1)}, u32[]{:S(2)}, u32[]{:S(2)}) collective-permute-start(bf16[2,2,6144]{2,1,0:T(2,128)(2,1)} %param.12), channel_id=1, source_target_pairs={{0,6},{1,7},{2,4},{3,5},{4,2},{5,3},{6,0},{7,1},{8,14},{9,15},{10,... | collective-permute-start | bytes 147464 | tf_op jit(solution)/shard_map/ppermute | solution.py:339
  4.6 4.7 %collective-permute-start = (bf16[2,2,6144]{2,1,0:T(2,128)(2,1)}, bf16[2,2,6144]{2,1,0:T(2,128)(2,1)S(1)}, u32[]{:S(2)}, u32[]{:S(2)}) collective-permute-start(bf16[2,2,6144]{2,1,0:T(2,128)(2,1)} %param.12), channel_id=1, source_target_pairs={{0,2},{1,5},{2,0},{3,7},{4,6},{5,1},{6,4},{7,3},{8,10},{9,13},{10,... | collective-permute-start | bytes 147464 | tf_op jit(solution)/shard_map/ppermute | solution.py:339
  5.1 4.3 %collective-permute-start.1 = (bf16[2,2,6144]{2,1,0:T(2,128)(2,1)}, bf16[2,2,6144]{2,1,0:T(2,128)(2,1)S(1)}, u32[]{:S(2)}, u32[]{:S(2)}) collective-permute-start(bf16[2,2,6144]{2,1,0:T(2,128)(2,1)} %param.12), channel_id=1, source_target_pairs={{0,4},{1,3},{2,6},{3,1},{4,0},{5,7},{6,2},{7,5},{8,12},{9,11},{10,... | collective-permute-start | bytes 147464 | tf_op jit(solution)/shard_map/ppermute | solution.py:339
  5.2 2.6 %collective-permute-start.4 = (s32[16]{0:T(128)}, s32[16]{0:T(128)S(1)}, u32[]{:S(2)}, u32[]{:S(2)}) collective-permute-start(s32[16]{0:T(128)} %param.10), channel_id=1, source_target_pairs={{0,1},{1,0},{2,3},{3,2},{4,5},{5,4},{6,7},{7,6},{8,9},{9,8},{10,11... | collective-permute-start | bytes 200 | tf_op jit(solution)/shard_map/ppermute | solution.py:332
  5.2 2.6 %collective-permute-start.3 = (bf16[16,2,6144]{2,1,0:T(2,128)(2,1)}, bf16[16,2,6144]{2,1,0:T(2,128)(2,1)S(1)}, u32[]{:S(2)}, u32[]{:S(2)}) collective-permute-start(bf16[16,2,6144]{2,1,0:T(2,128)(2,1)} %param.9), channel_id=1, source_target_pairs={{0,1},{1,0},{2,3},{3,2},{4,5},{5,4},{6,7},{7,6},{8,9},{9,8},{10,11... | collective-permute-start | bytes 1179656 | tf_op jit(solution)/shard_map/ppermute | solution.py:332
  7.8 1.4 %collective-permute-start.5 = (s32[16,8]{0,1:T(8,128)}, s32[16,8]{0,1:T(8,128)S(1)}, u32[]{:S(2)}, u32[]{:S(2)}) collective-permute-start(s32[16,8]{0,1:T(8,128)} %param.11), channel_id=1, source_target_pairs={{0,1},{1,0},{2,3},{3,2},{4,5},{5,4},{6,7},{7,6},{8,9},{9,8},{10,11... | collective-permute-start | bytes 1544 | tf_op jit(solution)/shard_map/ppermute | solution.py:332
  7.9 1.5 %copy-start = (bf16[2,2,6144]{2,1,0:T(2,128)(2,1)S(1)}, bf16[2,2,6144]{2,1,0:T(2,128)(2,1)}, u32[]{:S(2)}) copy-start(bf16[2,2,6144]{2,1,0:T(2,128)(2,1)} %param.12) | copy-start | bytes 147460
  7.9 1.5 %copy-start.1 = (f32[6144]{0:T(1024)S(1)}, f32[6144]{0:T(1024)}, u32[]{:S(2)}) copy-start(f32[6144]{0:T(1024)} %param.14) | copy-start | bytes 73732
  7.9 1.5 %copy-start.2 = (f32[8,128]{1,0:T(8,128)S(1)}, f32[8,128]{1,0:T(8,128)}, u32[]{:S(2)}) copy-start(f32[8,128]{1,0:T(8,128)} %constant.70.clone.refs_11_.trig_ref) | copy-start | bytes 12292
  7.9 1.5 %copy-start.3 = (s32[16]{0:T(128)S(1)}, s32[16]{0:T(128)}, u32[]{:S(2)}) copy-start(s32[16]{0:T(128)} %param.10) | copy-start | bytes 196
  7.9 1.5 %copy-start.4 = (s32[16,8]{0,1:T(8,128)S(1)}, s32[16,8]{0,1:T(8,128)}, u32[]{:S(2)}) copy-start(s32[16,8]{0,1:T(8,128)} %param.11) | copy-start | bytes 1540
  8.7 2.1 %copy-start.5 = (s32[2,48]{1,0:T(2,128)S(1)}, s32[2,48]{1,0:T(2,128)}, u32[]{:S(2)}) copy-start(s32[2,48]{1,0:T(2,128)} %param.15) | copy-start | bytes 1156
  8.7 2.1 %copy-start.6 = (s32[4]{0:T(128)S(1)}, s32[4]{0:T(128)}, u32[]{:S(2)}) copy-start(s32[4]{0:T(128)} %param.16) | copy-start | bytes 52
  10.8 1.2 %collective-permute-start.6 = (f32[8,128]{1,0:T(8,128)S(1)}, f32[8,128]{1,0:T(8,128)S(1)}, u32[]{:S(2)}, u32[]{:S(2)}) collective-permute-start(f32[8,128]{1,0:T(8,128)S(1)} %get-tuple-element.23.stat_ref), channel_id=1, source_target_pairs={{0,1},{1,0},{2,3},{3,2},{4,5},{5,4},{6,7},{7,6},{8,9},{9,8},{10,11... | collective-permute-start | bytes 12296 | tf_op jit(solution)/shard_map/ppermute | solution.py:332
  12.7 5.1 %collective-permute-start.7 = (bf16[4,6272]{1,0:T(4,128)(2,1)S(1)}, bf16[4,6272]{1,0:T(4,128)(2,1)S(1)}, u32[]{:S(2)}, u32[]{:S(2)}) collective-permute-start(bf16[4,6272]{1,0:T(4,128)(2,1)S(1)} %get-tuple-element.25), channel_id=1, source_target_pairs={{0,6},{1,7},{2,4},{3,5},{4,2},{5,3},{6,0},{7,1},{8,14},{9,15},{10,... | collective-permute-start | bytes 150536 | tf_op jit(solution)/shard_map/ppermute | solution.py:339
  15.5 4.1 %collective-permute-start.8 = (bf16[4,6272]{1,0:T(4,128)(2,1)S(1)}, bf16[4,6272]{1,0:T(4,128)(2,1)S(1)}, u32[]{:S(2)}, u32[]{:S(2)}) collective-permute-start(bf16[4,6272]{1,0:T(4,128)(2,1)S(1)} %get-tuple-element.26), channel_id=1, source_target_pairs={{0,4},{1,3},{2,6},{3,1},{4,0},{5,7},{6,2},{7,5},{8,12},{9,11},{10,... | collective-permute-start | bytes 150536 | tf_op jit(solution)/shard_map/ppermute | solution.py:339
  16.0 4.1 %collective-permute-start.9 = (bf16[4,6272]{1,0:T(4,128)(2,1)S(1)}, bf16[4,6272]{1,0:T(4,128)(2,1)S(1)}, u32[]{:S(2)}, u32[]{:S(2)}) collective-permute-start(bf16[4,6272]{1,0:T(4,128)(2,1)S(1)} %get-tuple-element.27), channel_id=1, source_target_pairs={{0,2},{1,5},{2,0},{3,7},{4,6},{5,1},{6,4},{7,3},{8,10},{9,13},{10,... | collective-permute-start | bytes 150536 | tf_op jit(solution)/shard_map/ppermute | solution.py:339
  20.8 5.8 %collective-permute-start.10 = (bf16[112,128]{1,0:T(8,128)(2,1)S(1)}, bf16[112,128]{1,0:T(8,128)(2,1)S(1)}, u32[]{:S(2)}, u32[]{:S(2)}) collective-permute-start(bf16[112,128]{1,0:T(8,128)(2,1)S(1)} %get-tuple-element.29), channel_id=1, source_target_pairs={{0,24},{8,16},{16,8},{24,0},{1,25},{9,17},{17,9},{25,1},{2,26},{10... | collective-permute-start | bytes 86024 | tf_op jit(solution)/shard_map/ppermute | solution.py:332
  24.4 4.8 %collective-permute-start.11 = (bf16[112,128]{1,0:T(8,128)(2,1)S(1)}, bf16[112,128]{1,0:T(8,128)(2,1)S(1)}, u32[]{:S(2)}, u32[]{:S(2)}) collective-permute-start(bf16[112,128]{1,0:T(8,128)(2,1)S(1)} %get-tuple-element.30), channel_id=1, source_target_pairs={{0,16},{8,24},{16,0},{24,8},{1,17},{9,25},{17,1},{25,9},{2,18},{10... | collective-permute-start | bytes 86024 | tf_op jit(solution)/shard_map/ppermute | solution.py:332
  24.4 4.8 %collective-permute-start.12 = (bf16[112,128]{1,0:T(8,128)(2,1)S(1)}, bf16[112,128]{1,0:T(8,128)(2,1)S(1)}, u32[]{:S(2)}, u32[]{:S(2)}) collective-permute-start(bf16[112,128]{1,0:T(8,128)(2,1)S(1)} %get-tuple-element.31), channel_id=1, source_target_pairs={{0,8},{8,0},{16,24},{24,16},{1,9},{9,1},{17,25},{25,17},{2,10},{10... | collective-permute-start | bytes 86024 | tf_op jit(solution)/shard_map/ppermute | solution.py:332

commit v3 on v2

--- a/solution.py
+++ b/solution.py
@@ -29,7 +29,12 @@
 
 
 def far_first(count):
-    return reversed(range(1, count))
+    return list(range(count - 1, 0, -1))
+
+
+def nearest_first_then_far(count):
+    order = far_first(count)
+    return order[-1:] + order[:-1]
 
 
 def call(kernel, out_shape, flops=0, moved=0, **kw):
@@ -48,8 +53,8 @@
     return jnp.concatenate([first, second, rest], axis=1)
 
 
-def onehot_of(d0_ref, d1_ref, bins):
-    row = spread(d0_ref[...], d1_ref[...])
+def onehot_of(i0_ref, i1_ref, bins):
+    row = spread(i0_ref[8:9], i1_ref[8:9])
     return (row == lax.broadcasted_iota(jnp.int32, (bins, LINE_LEN), 0)).astype(f32)
 
 
@@ -75,30 +80,35 @@
             y_ref[base : base + n, cols] = (x * math.sin(l * STEP)).astype(bf16)
 
 
-def own_kernel(p_hbm, t_hbm, d_hbm, y_ref, tab_ref, raw_ref, d_ref, scr_ref, ctf_ref, sems):
+def load_kernel(p_hbm, t_hbm, c_hbm, d_hbm, raw_ref, tab_ref, ints_ref, c_ref, d_ref, sems):
     copies = [
         pltpu.make_async_copy(src, dst, sems.at[i])
-        for i, (src, dst) in enumerate(((t_hbm, tab_ref), (p_hbm, raw_ref), (d_hbm, d_ref)))
+        for i, (src, dst) in enumerate(
+            ((p_hbm, raw_ref), (t_hbm, tab_ref), (c_hbm, c_ref), (d_hbm, d_ref))
+        )
     ]
     for copy in copies:
         copy.start()
     for copy in copies:
         copy.wait()
-    prep_half(0, raw_ref[...], d_ref[...], tab_ref, y_ref, scr_ref, ctf_ref)
+    ints_ref[0:8] = c_ref[...]
+    ints_ref[8:] = jnp.broadcast_to(d_ref[...], (8, d_ref.shape[1]))
+
+
+def own_kernel(p_ref, tab_ref, d_ref, y_ref, scr_ref, ctf_ref):
+    prep_half(0, p_ref[...], d_ref[8:9], tab_ref, y_ref, scr_ref, ctf_ref)
 
 
 def partner_kernel(p_ref, tab_ref, d_ref, half_ref, y_ref, scr_ref, ctf_ref):
-    prep_half(1, p_ref[...], d_ref[...], tab_ref, y_ref, scr_ref, ctf_ref)
+    prep_half(1, p_ref[...], d_ref[8:9], tab_ref, y_ref, scr_ref, ctf_ref)
 
 
 def score_kernel(chunks, *refs):
     p_refs = refs[:chunks]
-    y_ref, tab_ref, d0_ref, d1_ref, c0_ref, c1_ref, noise_ref, trig_ref, pid_ref = refs[
-        chunks : chunks + 9
-    ]
-    m_ref, s_ref, stat_ref = refs[chunks + 9 : chunks + 12]
-    scr_ref, r_ref, g_ref = refs[chunks + 12 :]
-    n = d0_ref.shape[1]
+    y_ref, tab_ref, i0_ref, i1_ref, noise_ref, trig_ref, pid_ref = refs[chunks : chunks + 7]
+    m_ref, s_ref, stat_ref = refs[chunks + 7 : chunks + 10]
+    scr_ref, r_ref, g_ref = refs[chunks + 10 :]
+    n = i0_ref.shape[1]
     bins, pixels = tab_ref.shape
     lines = pixels // LINE_LEN
     half = 2 * chunks
@@ -145,7 +155,7 @@
         row = [(v * wide, v * wide + half, (v + 1) * wide) for v in range(3)]
         even.append([real[i:j] + imag[j:k] for i, j, k in row])
         odd.append([imag[i:j] - real[j:k] for i, j, k in row])
-    onehot = onehot_of(d0_ref, d1_ref, bins)
+    onehot = onehot_of(i0_ref, i1_ref, bins)
     quad = 0.5 * jnp.concatenate(
         [
             jnp.sum(onehot * jnp.sum(p, axis=1, keepdims=True), axis=0, keepdims=True)
@@ -154,7 +164,7 @@
         axis=0,
     )
     pid = pid_ref[...]
-    cand = spread(c0_ref[...], c1_ref[...])
+    cand = spread(i0_ref[0:8], i1_ref[0:8])
     listed = cand[0:1] == pid
     for c in range(1, cand.shape[0]):
         listed = jnp.logical_or(listed, cand[c : c + 1] == pid)
@@ -219,9 +229,9 @@
 
 
 def slice_kernel(
-    y_ref, m_ref, s_ref, stat_ref, other_ref, d0_ref, d1_ref, trig_ref, keep_ref, *send_refs
+    y_ref, m_ref, s_ref, stat_ref, other_ref, i0_ref, i1_ref, trig_ref, keep_ref, *send_refs
 ):
-    n = d0_ref.shape[1]
+    n = i0_ref.shape[1]
     pixels = y_ref.shape[1]
     half = s_ref.shape[0]
     wide = 2 * half
@@ -236,7 +246,7 @@
     scale = jnp.where(lane < 2 * n, scale, 0.0)
     share = lax.dot_general(
         s_ref[...] * scale,
-        onehot_of(d0_ref, d1_ref, LINE_LEN),
+        onehot_of(i0_ref, i1_ref, LINE_LEN),
         last_last,
         precision=exact,
         preferred_element_type=f32,
@@ -262,11 +272,10 @@
         ref[:, pixels:] = share[4 * s : 4 * s + 4].astype(bf16)
 
 
-def pack_kernel(lines, cap, groups, chunks, idx_ref, own_ref, *refs):
+def pack_kernel(lines, cap, chunks, slot_ref, own_ref, *refs):
     recv_refs = refs[: chunks - 1]
     keep_ref, *send_refs, scr_ref = refs[chunks - 1 :]
-    size = 4 * cap
-    scr_ref[...] = jnp.zeros(scr_ref.shape, f32)
+    size = 2 * cap
     for l in range(lines + 1):
         cols = slice(l * LINE_LEN, (l + 1) * LINE_LEN)
         x = own_ref[:, cols]
@@ -274,41 +283,60 @@
             x = x + ref[:, cols].astype(f32)
         if l < lines:
             for j in range(2):
-                row = idx_ref[j, l]
-                scr_ref[pl.ds(row, 1), :] = x[j : j + 1]
-                scr_ref[pl.ds(row + cap, 1), :] = x[2 + j : 3 + j]
+                row = j * lines + l
+                scr_ref[row : row + 1, :LINE_LEN] = x[j : j + 1]
+                scr_ref[row : row + 1, LINE_LEN:] = x[2 + j : 3 + j]
         else:
-            tail = jnp.concatenate([x, jnp.zeros((12, LINE_LEN), f32)], axis=0)
-    keep_ref[:size] = scr_ref[:size]
-    keep_ref[size:] = tail
-    for r, ref in enumerate(send_refs, 1):
-        ref[:size] = scr_ref[r * size : (r + 1) * size].astype(bf16)
-        ref[size:] = tail.astype(bf16)
-
-
-def table_kernel(lines, cap, idx_ref, table_ref, sel_ref):
+            tail = jnp.concatenate([x, jnp.zeros((4, LINE_LEN), f32)], axis=0)
+    slots = jnp.concatenate([slot_ref[0:1], slot_ref[1:2]], axis=1)
+    rows = size * (len(send_refs) + 1)
+    pick = slots == lax.broadcasted_iota(jnp.int32, (rows, 2 * lines), 0)
+    packed = jnp.dot(
+        pick.astype(f32).astype(bf16), scr_ref[...].astype(bf16), preferred_element_type=f32
+    )
+    for r, ref in enumerate([keep_ref] + send_refs):
+        for part in range(2):
+            piece = packed[r * size : (r + 1) * size, part * LINE_LEN : (part + 1) * LINE_LEN]
+            ref[part * size : (part + 1) * size] = piece.astype(ref.dtype)
+        ref[2 * size :] = tail.astype(ref.dtype)
+
+
+def table_kernel(lines, cap, slot_ref, table_ref, sel_ref):
     bins = table_ref.shape[0]
     sel_ref[...] = jnp.zeros(sel_ref.shape, f32)
     for l in range(lines):
         t = table_ref[:, l * LINE_LEN : (l + 1) * LINE_LEN].astype(f32)
         t = t * t
         for j in range(2):
-            slot = idx_ref[j, l]
-
-            @pl.when(slot < 4 * cap)
+            slot = slot_ref[j, l]
+
+            @pl.when(slot < 2 * cap)
             def _():
-                sel_ref[j, pl.ds(slot - 2 * cap * j, 1)] = t[None]
-
-
-def final_kernel(cap, scale, own_ref, *refs):
-    *recv_refs, sel_ref, data_ref, weight_ref = refs
+                sel_ref[j, pl.ds(slot - cap * j, bins, stride=cap), :] = t
+
+
+def final_kernel(cap, bins, scale, own_ref, *refs):
+    *recv_refs, sel_ref, data_hbm, weight_hbm, data_ref, weight_ref, sems = refs
     x = own_ref[...]
     for ref in recv_refs:
         x = x + ref[...].astype(f32)
-    data_ref[...] = x[: 4 * cap].reshape(data_ref.shape)
-    bt = jnp.transpose(x[4 * cap :] * scale)[: sel_ref.shape[2]]
+    for part in range(2):
+        for j in range(2):
+            row = (2 * part + j) * cap
+            data_ref[0, j, part] = x[row : row + cap]
+    data_copy = pltpu.make_async_copy(data_ref, data_hbm, sems.at[0])
+    data_copy.start()
+    tail = x[4 * cap :] * scale
     for j in range(2):
-        weight_ref[0, j] = jnp.sum(sel_ref[j] * bt[:, j : j + 1][None], axis=1)
+        total = None
+        for b in range(bins):
+            term = sel_ref[j, b * cap : (b + 1) * cap] * tail[j : j + 1, b : b + 1]
+            total = term if b == 0 else total + term
+        weight_ref[0, j] = total
+    weight_copy = pltpu.make_async_copy(weight_ref, weight_hbm, sems.at[1])
+    weight_copy.start()
+    data_copy.wait()
+    weight_copy.wait()
 
 
 def body(
@@ -346,8 +374,6 @@
         return jnp.transpose(x, (0, 2, 1, 3)).reshape(2 * count * lines, LINE_LEN)
 
     part0, part1 = as_lines(particles), as_lines(swap(particles, "dev", members, 1))
-    def0, def1 = defocus_bin[None, :], swap(defocus_bin, "dev", members, 1)[None, :]
-    cand0, cand1 = candidates.T, swap(candidates, "dev", members, 1).T
     proj = {t: to_place(projections, t) for t in far_first(chunks)}
     proj = [as_lines(p) for p in [projections] + [proj[t] for t in range(1, chunks)]]
 
@@ -357,22 +383,29 @@
     vmem = pl.BlockSpec(memory_space=pltpu.VMEM)
     hbm = pl.BlockSpec(memory_space=pl.ANY)
     scratch = [pltpu.VMEM((2 * n * lines, LINE_LEN), f32), pltpu.VMEM((n, pixels), f32)]
-    y, table = call(
+    raw, table, ints0 = call(
+        load_kernel,
+        (
+            jax.ShapeDtypeStruct(part0.shape, bf16),
+            jax.ShapeDtypeStruct((bins, pixels), bf16),
+            jax.ShapeDtypeStruct((16, n), jnp.int32),
+        ),
+        in_specs=[hbm] * 4,
+        scratch_shapes=[
+            pltpu.VMEM((8, n), jnp.int32),
+            pltpu.VMEM((1, n), jnp.int32),
+            pltpu.SemaphoreType.DMA((4,)),
+        ],
+        moved=32 * n * pixels,
+    )(in_hbm(part0), in_hbm(ctf_table), in_hbm(candidates.T), in_hbm(defocus_bin[None, :]))
+    ints1 = swap(ints0, "dev", members, 1)
+    y = call(
         own_kernel,
-        (
-            jax.ShapeDtypeStruct((12 * n, pixels), bf16),
-            jax.ShapeDtypeStruct((bins, pixels), bf16),
-        ),
-        in_specs=[hbm] * 3,
-        scratch_shapes=[
-            pltpu.VMEM((2 * n * lines, LINE_LEN), bf16),
-            pltpu.VMEM((1, n), jnp.int32),
-            *scratch,
-            pltpu.SemaphoreType.DMA((3,)),
-        ],
+        jax.ShapeDtypeStruct((12 * n, pixels), bf16),
+        scratch_shapes=scratch,
         flops=20 * n * pixels,
         moved=32 * n * pixels,
-    )(in_hbm(part0), in_hbm(ctf_table), in_hbm(def0))
+    )(raw, table, ints0)
     y = call(
         partner_kernel,
         jax.ShapeDtypeStruct((12 * n, pixels), bf16),
@@ -381,7 +414,7 @@
         input_output_aliases={3: 0},
         flops=20 * n * pixels,
         moved=32 * n * pixels,
-    )(part1, table, def1, y)
+    )(part1, table, ints1, y)
 
     row = lax.broadcasted_iota(jnp.int32, (2 * chunks, LINE_LEN), 0)
     far = jnp.where(dev % 2 == 0, row // 2, turned(row // 2))
@@ -400,7 +433,7 @@
         ],
         flops=2 * 192 * 3 * wide * pixels,
         moved=30 * n * pixels,
-    )(*proj, y, table, def0, def1, cand0, cand1, noise, trig, pid)
+    )(*proj, y, table, ints0, ints1, noise, trig, pid)
     line_slab, stat = lax.optimization_barrier((line_slab, stat))
     other = swap(stat, "dev", members, 1)
     own, *send = call(
@@ -409,7 +442,7 @@
         + (jax.ShapeDtypeStruct((4, pixels + LINE_LEN), bf16),) * (chunks - 1),
         flops=2 * 192 * 3 * wide * pixels,
         moved=30 * n * pixels,
-    )(y, m, share, stat, other, def0, def1, trig)
+    )(y, m, share, stat, other, ints0, ints1, trig)
     got = [to_place(send[t - 1], t) for t in far_first(chunks)]
 
     group_ids = jnp.arange(groups, dtype=jnp.int32)
@@ -420,34 +453,38 @@
     same_owner = owner_line[:, :, None] == owner_line[:, None, :]
     line_rank = jnp.sum(jnp.logical_and(same_owner, earlier[None]), axis=2)
     rel = owner_line ^ grp
-    idx = (4 * cap) * rel + 2 * cap * jnp.arange(2, dtype=jnp.int32)[:, None] + line_rank
-    idx = idx.astype(jnp.int32)
+    slot = (2 * cap) * rel + cap * jnp.arange(2, dtype=jnp.int32)[:, None] + line_rank
+    slot = slot.astype(jnp.int32)
 
     sel = call(
         functools.partial(table_kernel, lines, cap),
-        jax.ShapeDtypeStruct((2, cap, bins, LINE_LEN), f32),
-        in_specs=[pl.BlockSpec(memory_space=pltpu.SMEM), pl.BlockSpec(memory_space=pltpu.VMEM)],
+        jax.ShapeDtypeStruct((2, bins * cap, LINE_LEN), f32),
+        in_specs=[pl.BlockSpec(memory_space=pltpu.SMEM), vmem],
         flops=bins * pixels,
         moved=4 * bins * pixels,
-    )(idx, table)
-    size = 4 * cap + 16
+    )(slot, table)
+    size = 4 * cap + 8
     keep, *send = call(
-        functools.partial(pack_kernel, lines, cap, groups, chunks),
+        functools.partial(pack_kernel, lines, cap, chunks),
         (jax.ShapeDtypeStruct((size, LINE_LEN), f32),)
         + (jax.ShapeDtypeStruct((size, LINE_LEN), bf16),) * (groups - 1),
-        in_specs=[pl.BlockSpec(memory_space=pltpu.SMEM)] + [vmem] * chunks,
-        scratch_shapes=[pltpu.VMEM((4 * cap * groups, LINE_LEN), f32)],
+        scratch_shapes=[pltpu.VMEM((2 * lines, 2 * LINE_LEN), f32)],
         flops=16 * pixels,
         moved=64 * pixels,
-    )(idx, own, *got)
-    recv = [swap(send[r - 1], "grp", groups, r) for r in far_first(groups)]
+    )(slot, own, *got)
+    recv = [swap(send[r - 1], "grp", groups, r) for r in nearest_first_then_far(groups)]
     weight_scale = 2 * members / (n * groups * members)
+    data, weight = (1, 2, 2, cap, LINE_LEN), (1, 2, cap, LINE_LEN)
     return call(
-        functools.partial(final_kernel, cap, weight_scale),
-        (
-            jax.ShapeDtypeStruct((1, 2, 2, cap, LINE_LEN), f32),
-            jax.ShapeDtypeStruct((1, 2, cap, LINE_LEN), f32),
-        ),
+        functools.partial(final_kernel, cap, bins, weight_scale),
+        (jax.ShapeDtypeStruct(data, f32), jax.ShapeDtypeStruct(weight, f32)),
+        in_specs=[vmem] * (groups + 1),
+        out_specs=(hbm, hbm),
+        scratch_shapes=[
+            pltpu.VMEM(data, f32),
+            pltpu.VMEM(weight, f32),
+            pltpu.SemaphoreType.DMA((2,)),
+        ],
         flops=1000,
         moved=8 * 4 * cap * LINE_LEN,
     )(keep, *recv, sel)

time: 30.1 us -> 29.5 us (0.980)
  Pallas kernels: 7.47 us -> 7 us
    ppermute x7 -> x6, waiting for transfers between devices: 4.01 us -> 3.5 us  [swap(): return lax.ppermute(x, axis, [(i, i ^ mask) for i in range(size)])]
    pallas_call x3 -> x4, Pallas kernels: 3.34 us -> 2.85 us  [the longest x1 1.08 us: body(): call(load_kernel, (jax.ShapeDtypeStruct(part0.shape, bf16), jax.ShapeDtyp...]
    ppermute x6, waiting for transfers between devices: 3.92 us -> 4.28 us  [to_place(): lax.ppermute(x, 'dev', [(i, i ^ 2 * (turned(t) if i % 2 else t)) for i in...]
    ppermute x7 -> x6, starting transfers between devices: 5.11 us -> 5.1 us  [swap(): return lax.ppermute(x, axis, [(i, i ^ mask) for i in range(size)])]
  transfers between devices with their start and end apart: 13 -> 12, of which waited for: 7 -> 7; matrix products, arithmetic and copies ran while one was open for 1% -> 2% of each run, Pallas kernels for 13% -> 13%
where the time goes in v3:
time: 29.5 us; the launch traced here: 29.3 us
  starting transfers between devices  13.3 us (45%)
  waiting for transfers between devices  7.78 us (26%)
  Pallas kernels  7 us (24%)
  between operations  0.83 us (3%)
  other arithmetic  0.45 us (2%)
    ppermute x6, starting transfers between devices, to_place(): lax.ppermute(x, 'dev', [(i, i ^ 2 * (turned(t) if i % 2 else t)) for i in...  8.16 us
    ppermute x6, starting transfers between devices, swap(): return lax.ppermute(x, axis, [(i, i ^ mask) for i in range(size)])  5.1 us
    ppermute x6, waiting for transfers between devices, to_place(): lax.ppermute(x, 'dev', [(i, i ^ 2 * (turned(t) if i % 2 else t)) for i in...  4.28 us
    ppermute x6, waiting for transfers between devices, swap(): return lax.ppermute(x, axis, [(i, i ^ mask) for i in range(size)])  3.5 us
    pallas_call x1, Pallas kernels, body(): call(functools.partial(table_kernel, lines, cap), jax.ShapeDtypeStruct((2...  1.33 us
    pallas_call x1, Pallas kernels, body(): call(functools.partial(score_kernel, chunks), (jax.ShapeDtypeStruct((3 *...  1.32 us
    pallas_call x1, Pallas kernels, body(): call(load_kernel, (jax.ShapeDtypeStruct(part0.shape, bf16), jax.ShapeDtyp...  1.08 us
    pallas_call x1, Pallas kernels, body(): call(functools.partial(final_kernel, cap, bins, weight_scale), (jax.Shape...  0.78 us
  transfers between devices with their start and end apart: 12, of which 7 were waited for; matrix products, arithmetic and copies ran while one was open for 2% of the time, Pallas kernels for 13%

profile of v3, /device:TPU:0, one launch (start us, length us, event | category | flops | bytes accessed | tf_op | source)
XLA Modules:
  0.0 29.3 jit_solution(14014369219756203831)
XLA Ops:
  0.6 4.0 %collective-permute-start.2 = (bf16[2,2,6144]{2,1,0:T(2,128)(2,1)}, bf16[2,2,6144]{2,1,0:T(2,128)(2,1)S(1)}, u32[]{:S(2)}, u32[]{:S(2)}) collective-permute-start(bf16[2,2,6144]{2,1,0:T(2,128)(2,1)} %param.12), channel_id=1, source_target_pairs={{0,6},{1,7},{2,4},{3,5},{4,2},{5,3},{6,0},{7,1},{8,14},{9,15},{10,... | collective-permute-start | bytes 147464 | tf_op jit(solution)/shard_map/ppermute | solution.py:367
  4.6 0.5 %collective-permute-start = (bf16[2,2,6144]{2,1,0:T(2,128)(2,1)}, bf16[2,2,6144]{2,1,0:T(2,128)(2,1)S(1)}, u32[]{:S(2)}, u32[]{:S(2)}) collective-permute-start(bf16[2,2,6144]{2,1,0:T(2,128)(2,1)} %param.12), channel_id=1, source_target_pairs={{0,2},{1,5},{2,0},{3,7},{4,6},{5,1},{6,4},{7,3},{8,10},{9,13},{10,... | collective-permute-start | bytes 147464 | tf_op jit(solution)/shard_map/ppermute | solution.py:367
  5.1 0.1 collective-permute-start.1
  5.2 0.0 collective-permute-start.3
  5.2 1.1 %shard_map.104 = (bf16[1536,128]{1,0:T(8,128)(2,1)S(1)}, bf16[16,6144]{1,0:T(8,128)(2,1)S(1)}, s32[16,16]{1,0:T(8,128)S(1)}) custom-call(bf16[1536,128]{1,0:T(8,128)(2,1)} %bitcast.39, bf16[16,6144]{1,0:T(8,128)(2,1)} %t_hbm.1, s32[8,16]{1,0:T(8,128)} %bitcast.40, s32[1,16]{1,0:T(1,128)} %bitcast.41), custom_call_target="tpu_custom_call" | custom-call | bytes 3145728 | tf_op jit(solution)/shard_map/pallas_call | solution.py:386
  6.3 0.6 %collective-permute-start.4 = (s32[16,16]{1,0:T(8,128)S(1)}, s32[16,16]{1,0:T(8,128)S(1)}, u32[]{:S(2)}, u32[]{:S(2)}) collective-permute-start(s32[16,16]{1,0:T(8,128)S(1)} %get-tuple-element.19.d_ref.refs_6_.i0_ref), channel_id=1, source_target_pairs={{0,1},{1,0},{2,3},{3,2},{4,5},{5,4},{6,7},{7,6},{8,9},{9,8},{10,11... | collective-permute-start | bytes 3080 | tf_op jit(solution)/shard_map/ppermute | solution.py:360
  7.0 0.1 fusion.5.refs_10_
  7.1 0.7 %shard_map.105.half_ref = bf16[192,6144]{1,0:T(8,128)(2,1)S(1)} custom-call(bf16[1536,128]{1,0:T(8,128)(2,1)S(1)} %get-tuple-element.20.p_ref, bf16[16,6144]{1,0:T(8,128)(2,1)S(1)} %get-tuple-element.18.tab_ref.refs_5_.table_ref, s32[16,16]{1,0:T(8,128)S(1)} %get-tuple-element.19.d_ref.refs_6_.i0_ref), custom_call_target="tpu_custom_call" | custom-call | flops 1966080 | bytes 3145728 | tf_op jit(solution)/shard_map/pallas_call | solution.py:402
  7.8 0.0 collective-permute-done.4.d_ref.refs_7_.i1_ref
  7.8 0.0 collective-permute-done.3
  7.8 0.0 copy-start
  7.8 0.0 copy-start.1
  7.8 0.0 copy-start.2
  7.9 0.7 %shard_map.106.refs_4_.y_ref = bf16[192,6144]{1,0:T(8,128)(2,1)S(1)} custom-call(bf16[1536,128]{1,0:T(8,128)(2,1)S(1)} %bitcast.33, bf16[16,6144]{1,0:T(8,128)(2,1)S(1)} %get-tuple-element.18.tab_ref.refs_5_.table_ref, s32[16,16]{1,0:T(8,128)S(1)} %collective-permute-done.4.d_ref.refs_7_.i1_ref, ...), custom_call_target="tpu_custom_call", output_to_operand_aliasing={{}: (3, {})} | custom-call | flops 1966080 | bytes 3145728 | tf_op jit(solution)/shard_map/pallas_call | solution.py:409
  8.6 0.0 copy-start.3
  8.6 0.0 copy-start.4
  8.6 0.0 collective-permute-done.2
  8.6 0.3 collective-permute-done
  8.9 0.5 %collective-permute-done.1 = bf16[2,2,6144]{2,1,0:T(2,128)(2,1)S(1)} collective-permute-done((bf16[2,2,6144]{2,1,0:T(2,128)(2,1)}, bf16[2,2,6144]{2,1,0:T(2,128)(2,1)S(1)}, u32[]{:S(2)}, u32[]{:S(2)}) %collective-permute-start.1) | collective-permute-done | bytes 49184 | tf_op jit(solution)/shard_map/ppermute | solution.py:367
  9.4 0.0 copy-done
  9.4 0.0 copy-done.1
  9.4 0.0 copy-done.2
  9.4 1.3 %shard_map.107 = (f32[48,256]{1,0:T(8,128)S(1)}, f32[8,128]{1,0:T(8,128)S(1)}, f32[8,128]{1,0:T(8,128)S(1)}) custom-call(bf16[192,128]{1,0:T(8,128)(2,1)S(1)} %bitcast.34, bf16[192,128]{1,0:T(8,128)(2,1)S(1)} %bitcast.36, bf16[192,128]{1,0:T(8,128)(2,1)S(1)} %bitcast.37, bf16[192,128]{1,0:T(8,128)(2,1)S(1)} %bitcast.35, ...), custom_call_target="tpu_custom_call" | custom-call | flops 113246208 | bytes 2949120 | tf_op jit(solution)/shard_map/pallas_call | solution.py:422
  10.8 0.1 collective-permute-start.5
  10.8 0.0 copy-done.3
  10.9 0.0 copy-done.4
  10.9 0.1 select_reduce_fusion
  11.0 0.2 convert_reduce_fusion
  11.1 0.9 %collective-permute-done.5.other_ref = f32[8,128]{1,0:T(8,128)S(1)} collective-permute-done((f32[8,128]{1,0:T(8,128)S(1)}, f32[8,128]{1,0:T(8,128)S(1)}, u32[]{:S(2)}, u32[]{:S(2)}) %collective-permute-start.5) | collective-permute-done | bytes 4128 | tf_op jit(solution)/shard_map/ppermute | solution.py:360
  12.0 0.8 %shard_map.108 = (f32[4,6272]{1,0:T(4,128)S(1)}, bf16[4,6272]{1,0:T(4,128)(2,1)S(1)}, bf16[4,6272]{1,0:T(4,128)(2,1)S(1)}, bf16[4,6272]{1,0:T(4,128)(2,1)S(1)}) custom-call(bf16[192,6144]{1,0:T(8,128)(2,1)S(1)} %shard_map.106.refs_4_.y_ref, f32[48,256]{1,0:T(8,128)S(1)} %get-tuple-element.23.m_ref, f32[8,128]{1,0:T(8,128)S(1)} %get-tuple-element.24.s_ref, ...), custom_call_target="tpu_custom_call" | custom-call | flops 113246208 | bytes 2949120 | tf_op jit(solution)/shard_map/pallas_call | solution.py:439
  12.8 2.2 %collective-permute-start.6 = (bf16[4,6272]{1,0:T(4,128)(2,1)S(1)}, bf16[4,6272]{1,0:T(4,128)(2,1)S(1)}, u32[]{:S(2)}, u32[]{:S(2)}) collective-permute-start(bf16[4,6272]{1,0:T(4,128)(2,1)S(1)} %get-tuple-element.27), channel_id=1, source_target_pairs={{0,6},{1,7},{2,4},{3,5},{4,2},{5,3},{6,0},{7,1},{8,14},{9,15},{10,... | collective-permute-start | bytes 150536 | tf_op jit(solution)/shard_map/ppermute | solution.py:367
  14.9 0.9 %collective-permute-start.7 = (bf16[4,6272]{1,0:T(4,128)(2,1)S(1)}, bf16[4,6272]{1,0:T(4,128)(2,1)S(1)}, u32[]{:S(2)}, u32[]{:S(2)}) collective-permute-start(bf16[4,6272]{1,0:T(4,128)(2,1)S(1)} %get-tuple-element.28), channel_id=1, source_target_pairs={{0,4},{1,3},{2,6},{3,1},{4,0},{5,7},{6,2},{7,5},{8,12},{9,11},{10,... | collective-permute-start | bytes 150536 | tf_op jit(solution)/shard_map/ppermute | solution.py:367
  15.8 0.5 %collective-permute-start.8 = (bf16[4,6272]{1,0:T(4,128)(2,1)S(1)}, bf16[4,6272]{1,0:T(4,128)(2,1)S(1)}, u32[]{:S(2)}, u32[]{:S(2)}) collective-permute-start(bf16[4,6272]{1,0:T(4,128)(2,1)S(1)} %get-tuple-element.29), channel_id=1, source_target_pairs={{0,2},{1,5},{2,0},{3,7},{4,6},{5,1},{6,4},{7,3},{8,10},{9,13},{10,... | collective-permute-start | bytes 150536 | tf_op jit(solution)/shard_map/ppermute | solution.py:367
  16.3 0.1 add_add_fusion.slot_ref
  16.4 1.7 %collective-permute-done.6.refs_0_ = bf16[4,6272]{1,0:T(4,128)(2,1)S(1)} collective-permute-done((bf16[4,6272]{1,0:T(4,128)(2,1)S(1)}, bf16[4,6272]{1,0:T(4,128)(2,1)S(1)}, u32[]{:S(2)}, u32[]{:S(2)}) %collective-permute-start.6) | collective-permute-done | bytes 50208 | tf_op jit(solution)/shard_map/ppermute | solution.py:367
  18.0 1.0 %collective-permute-done.7.refs_1_ = bf16[4,6272]{1,0:T(4,128)(2,1)S(1)} collective-permute-done((bf16[4,6272]{1,0:T(4,128)(2,1)S(1)}, bf16[4,6272]{1,0:T(4,128)(2,1)S(1)}, u32[]{:S(2)}, u32[]{:S(2)}) %collective-permute-start.7) | collective-permute-done | bytes 50208 | tf_op jit(solution)/shard_map/ppermute | solution.py:367
  19.0 0.9 %collective-permute-done.8.refs_2_ = bf16[4,6272]{1,0:T(4,128)(2,1)S(1)} collective-permute-done((bf16[4,6272]{1,0:T(4,128)(2,1)S(1)}, bf16[4,6272]{1,0:T(4,128)(2,1)S(1)}, u32[]{:S(2)}, u32[]{:S(2)}) %collective-permute-start.8) | collective-permute-done | bytes 50208 | tf_op jit(solution)/shard_map/ppermute | solution.py:367
  19.9 0.3 shard_map.109
  20.1 3.7 %collective-permute-start.10 = (bf16[104,128]{1,0:T(8,128)(2,1)S(1)}, bf16[104,128]{1,0:T(8,128)(2,1)S(1)}, u32[]{:S(2)}, u32[]{:S(2)}) collective-permute-start(bf16[104,128]{1,0:T(8,128)(2,1)S(1)} %get-tuple-element.32), channel_id=1, source_target_pairs={{0,24},{8,16},{16,8},{24,0},{1,25},{9,17},{17,9},{25,1},{2,26},{10... | collective-permute-start | bytes 79880 | tf_op jit(solution)/shard_map/ppermute | solution.py:360
  23.8 0.0 collective-permute-start.11
  23.8 0.8 %collective-permute-start.9 = (bf16[104,128]{1,0:T(8,128)(2,1)S(1)}, bf16[104,128]{1,0:T(8,128)(2,1)S(1)}, u32[]{:S(2)}, u32[]{:S(2)}) collective-permute-start(bf16[104,128]{1,0:T(8,128)(2,1)S(1)} %get-tuple-element.31), channel_id=1, source_target_pairs={{0,8},{8,0},{16,24},{24,16},{1,9},{9,1},{17,25},{25,17},{2,10},{10... | collective-permute-start | bytes 79880 | tf_op jit(solution)/shard_map/ppermute | solution.py:360
  24.6 1.3 %shard_map.110.refs_3_ = f32[2,384,128]{2,1,0:T(8,128)S(1)} custom-call(s32[2,48]{1,0:T(2,128)S(1)} %add_add_fusion.slot_ref, bf16[16,6144]{1,0:T(8,128)(2,1)S(1)} %get-tuple-element.18.tab_ref.refs_5_.table_ref), custom_call_target="tpu_custom_call" | custom-call | flops 98304 | bytes 393216 | tf_op jit(solution)/shard_map/pallas_call | solution.py:459
  25.9 0.0 collective-permute-done.10.refs_1_
  25.9 2.6 %collective-permute-done.11.refs_2_ = bf16[104,128]{1,0:T(8,128)(2,1)S(1)} collective-permute-done((bf16[104,128]{1,0:T(8,128)(2,1)S(1)}, bf16[104,128]{1,0:T(8,128)(2,1)S(1)}, u32[]{:S(2)}, u32[]{:S(2)}) %collective-permute-start.11) | collective-permute-done | bytes 26656 | tf_op jit(solution)/shard_map/ppermute | solution.py:360
  28.6 0.0 collective-permute-done.9.refs_0_
  28.6 0.8 %shard_map.111 = (f32[1,2,2,24,128]{4,3,2,1,0:T(8,128)}, f32[1,2,24,128]{3,2,1,0:T(8,128)}) custom-call(f32[104,128]{1,0:T(8,128)S(1)} %get-tuple-element.30.own_ref, bf16[104,128]{1,0:T(8,128)(2,1)S(1)} %collective-permute-done.9.refs_0_, bf16[104,128]{1,0:T(8,128)(2,1)S(1)} %collective-permute-done.10.refs_1_, ...), custom_call_target="tpu_custom_call" | custom-call | flops 1000 | bytes 98304 | tf_op jit(solution)/shard_map/pallas_call | solution.py:478
  (5 shorter events, 0.0 us)
Async XLA Ops:
  0.6 8.0 %collective-permute-start.2 = (bf16[2,2,6144]{2,1,0:T(2,128)(2,1)}, bf16[2,2,6144]{2,1,0:T(2,128)(2,1)S(1)}, u32[]{:S(2)}, u32[]{:S(2)}) collective-permute-start(bf16[2,2,6144]{2,1,0:T(2,128)(2,1)} %param.12), channel_id=1, source_target_pairs={{0,6},{1,7},{2,4},{3,5},{4,2},{5,3},{6,0},{7,1},{8,14},{9,15},{10,... | collective-permute-start | bytes 147464 | tf_op jit(solution)/shard_map/ppermute | solution.py:367
  4.6 4.3 %collective-permute-start = (bf16[2,2,6144]{2,1,0:T(2,128)(2,1)}, bf16[2,2,6144]{2,1,0:T(2,128)(2,1)S(1)}, u32[]{:S(2)}, u32[]{:S(2)}) collective-permute-start(bf16[2,2,6144]{2,1,0:T(2,128)(2,1)} %param.12), channel_id=1, source_target_pairs={{0,2},{1,5},{2,0},{3,7},{4,6},{5,1},{6,4},{7,3},{8,10},{9,13},{10,... | collective-permute-start | bytes 147464 | tf_op jit(solution)/shard_map/ppermute | solution.py:367
  5.1 4.3 %collective-permute-start.1 = (bf16[2,2,6144]{2,1,0:T(2,128)(2,1)}, bf16[2,2,6144]{2,1,0:T(2,128)(2,1)S(1)}, u32[]{:S(2)}, u32[]{:S(2)}) collective-permute-start(bf16[2,2,6144]{2,1,0:T(2,128)(2,1)} %param.12), channel_id=1, source_target_pairs={{0,4},{1,3},{2,6},{3,1},{4,0},{5,7},{6,2},{7,5},{8,12},{9,11},{10,... | collective-permute-start | bytes 147464 | tf_op jit(solution)/shard_map/ppermute | solution.py:367
  5.2 2.6 %collective-permute-start.3 = (bf16[16,2,6144]{2,1,0:T(2,128)(2,1)}, bf16[16,2,6144]{2,1,0:T(2,128)(2,1)S(1)}, u32[]{:S(2)}, u32[]{:S(2)}) collective-permute-start(bf16[16,2,6144]{2,1,0:T(2,128)(2,1)} %param.9), channel_id=1, source_target_pairs={{0,1},{1,0},{2,3},{3,2},{4,5},{5,4},{6,7},{7,6},{8,9},{9,8},{10,11... | collective-permute-start | bytes 1179656 | tf_op jit(solution)/shard_map/ppermute | solution.py:360
  6.3 1.5 %collective-permute-start.4 = (s32[16,16]{1,0:T(8,128)S(1)}, s32[16,16]{1,0:T(8,128)S(1)}, u32[]{:S(2)}, u32[]{:S(2)}) collective-permute-start(s32[16,16]{1,0:T(8,128)S(1)} %get-tuple-element.19.d_ref.refs_6_.i0_ref), channel_id=1, source_target_pairs={{0,1},{1,0},{2,3},{3,2},{4,5},{5,4},{6,7},{7,6},{8,9},{9,8},{10,11... | collective-permute-start | bytes 3080 | tf_op jit(solution)/shard_map/ppermute | solution.py:360
  7.8 1.6 %copy-start = (bf16[2,2,6144]{2,1,0:T(2,128)(2,1)S(1)}, bf16[2,2,6144]{2,1,0:T(2,128)(2,1)}, u32[]{:S(2)}) copy-start(bf16[2,2,6144]{2,1,0:T(2,128)(2,1)} %param.12) | copy-start | bytes 147460
  7.8 1.6 %copy-start.1 = (f32[6144]{0:T(1024)S(1)}, f32[6144]{0:T(1024)}, u32[]{:S(2)}) copy-start(f32[6144]{0:T(1024)} %param.14) | copy-start | bytes 73732
  7.8 1.6 %copy-start.2 = (f32[8,128]{1,0:T(8,128)S(1)}, f32[8,128]{1,0:T(8,128)}, u32[]{:S(2)}) copy-start(f32[8,128]{1,0:T(8,128)} %constant.70.clone.refs_9_.trig_ref) | copy-start | bytes 12292
  8.6 2.2 %copy-start.3 = (s32[2,48]{1,0:T(2,128)S(1)}, s32[2,48]{1,0:T(2,128)}, u32[]{:S(2)}) copy-start(s32[2,48]{1,0:T(2,128)} %param.15) | copy-start | bytes 1156
  8.6 2.2 %copy-start.4 = (s32[4]{0:T(128)S(1)}, s32[4]{0:T(128)}, u32[]{:S(2)}) copy-start(s32[4]{0:T(128)} %param.16) | copy-start | bytes 52
  10.8 1.2 %collective-permute-start.5 = (f32[8,128]{1,0:T(8,128)S(1)}, f32[8,128]{1,0:T(8,128)S(1)}, u32[]{:S(2)}, u32[]{:S(2)}) collective-permute-start(f32[8,128]{1,0:T(8,128)S(1)} %get-tuple-element.25.stat_ref), channel_id=1, source_target_pairs={{0,1},{1,0},{2,3},{3,2},{4,5},{5,4},{6,7},{7,6},{8,9},{9,8},{10,11... | collective-permute-start | bytes 12296 | tf_op jit(solution)/shard_map/ppermute | solution.py:360
  12.8 5.3 %collective-permute-start.6 = (bf16[4,6272]{1,0:T(4,128)(2,1)S(1)}, bf16[4,6272]{1,0:T(4,128)(2,1)S(1)}, u32[]{:S(2)}, u32[]{:S(2)}) collective-permute-start(bf16[4,6272]{1,0:T(4,128)(2,1)S(1)} %get-tuple-element.27), channel_id=1, source_target_pairs={{0,6},{1,7},{2,4},{3,5},{4,2},{5,3},{6,0},{7,1},{8,14},{9,15},{10,... | collective-permute-start | bytes 150536 | tf_op jit(solution)/shard_map/ppermute | solution.py:367
  14.9 4.1 %collective-permute-start.7 = (bf16[4,6272]{1,0:T(4,128)(2,1)S(1)}, bf16[4,6272]{1,0:T(4,128)(2,1)S(1)}, u32[]{:S(2)}, u32[]{:S(2)}) collective-permute-start(bf16[4,6272]{1,0:T(4,128)(2,1)S(1)} %get-tuple-element.28), channel_id=1, source_target_pairs={{0,4},{1,3},{2,6},{3,1},{4,0},{5,7},{6,2},{7,5},{8,12},{9,11},{10,... | collective-permute-start | bytes 150536 | tf_op jit(solution)/shard_map/ppermute | solution.py:367
  15.8 4.1 %collective-permute-start.8 = (bf16[4,6272]{1,0:T(4,128)(2,1)S(1)}, bf16[4,6272]{1,0:T(4,128)(2,1)S(1)}, u32[]{:S(2)}, u32[]{:S(2)}) collective-permute-start(bf16[4,6272]{1,0:T(4,128)(2,1)S(1)} %get-tuple-element.29), channel_id=1, source_target_pairs={{0,2},{1,5},{2,0},{3,7},{4,6},{5,1},{6,4},{7,3},{8,10},{9,13},{10,... | collective-permute-start | bytes 150536 | tf_op jit(solution)/shard_map/ppermute | solution.py:367
  20.1 5.8 %collective-permute-start.10 = (bf16[104,128]{1,0:T(8,128)(2,1)S(1)}, bf16[104,128]{1,0:T(8,128)(2,1)S(1)}, u32[]{:S(2)}, u32[]{:S(2)}) collective-permute-start(bf16[104,128]{1,0:T(8,128)(2,1)S(1)} %get-tuple-element.32), channel_id=1, source_target_pairs={{0,24},{8,16},{16,8},{24,0},{1,25},{9,17},{17,9},{25,1},{2,26},{10... | collective-permute-start | bytes 79880 | tf_op jit(solution)/shard_map/ppermute | solution.py:360
  23.8 4.7 %collective-permute-start.11 = (bf16[104,128]{1,0:T(8,128)(2,1)S(1)}, bf16[104,128]{1,0:T(8,128)(2,1)S(1)}, u32[]{:S(2)}, u32[]{:S(2)}) collective-permute-start(bf16[104,128]{1,0:T(8,128)(2,1)S(1)} %get-tuple-element.33), channel_id=1, source_target_pairs={{0,16},{8,24},{16,0},{24,8},{1,17},{9,25},{17,1},{25,9},{2,18},{10... | collective-permute-start | bytes 79880 | tf_op jit(solution)/shard_map/ppermute | solution.py:360
  23.8 4.7 %collective-permute-start.9 = (bf16[104,128]{1,0:T(8,128)(2,1)S(1)}, bf16[104,128]{1,0:T(8,128)(2,1)S(1)}, u32[]{:S(2)}, u32[]{:S(2)}) collective-permute-start(bf16[104,128]{1,0:T(8,128)(2,1)S(1)} %get-tuple-element.31), channel_id=1, source_target_pairs={{0,8},{8,0},{16,24},{24,16},{1,9},{9,1},{17,25},{25,17},{2,10},{10... | collective-permute-start | bytes 79880 | tf_op jit(solution)/shard_map/ppermute | solution.py:360

commit v4 on v3

--- a/solution.py
+++ b/solution.py
@@ -28,13 +28,21 @@
     return rows
 
 
-def far_first(count):
-    return list(range(count - 1, 0, -1))
-
-
-def nearest_first_then_far(count):
-    order = far_first(count)
-    return order[-1:] + order[:-1]
+CHIP_ROUTES = [[[3, 2, 1, 0], [2, 3, 0, 1], [1, 0, 3, 2]], [[3, 2, 1, 0], [1, 3, 0, 2], [2, 0, 3, 1]]]
+GROUP_ROUTES = [[[2, 3, 1, 0], [3, 2, 0, 1], [1, 0, 3, 2]], [[2, 3, 1, 0], [3, 2, 0, 1], [1, 0, 3, 2]]]
+
+
+def routes(count, chosen):
+    if count == 4:
+        return chosen
+    return [[[i ^ t for i in range(count)] for t in range(count - 1, 0, -1)]] * 2
+
+
+def lookup(index, table):
+    found = table[0]
+    for i in range(1, len(table)):
+        found = jnp.where(index == i, table[i], found)
+    return found
 
 
 def call(kernel, out_shape, flops=0, moved=0, **kw):
@@ -106,8 +114,8 @@
 def score_kernel(chunks, *refs):
     p_refs = refs[:chunks]
     y_ref, tab_ref, i0_ref, i1_ref, noise_ref, trig_ref, pid_ref = refs[chunks : chunks + 7]
-    m_ref, s_ref, stat_ref = refs[chunks + 7 : chunks + 10]
-    scr_ref, r_ref, g_ref = refs[chunks + 10 :]
+    e_ref, stat_ref = refs[chunks + 7 : chunks + 9]
+    scr_ref, r_ref, g_ref = refs[chunks + 9 :]
     n = i0_ref.shape[1]
     bins, pixels = tab_ref.shape
     lines = pixels // LINE_LEN
@@ -142,9 +150,6 @@
     def left(v, k):
         return pltpu.roll(v, LINE_LEN - k, 1) if k else v
 
-    def right(v, k):
-        return pltpu.roll(v, k, 1) if k else v
-
     def block(k):
         at = k * step // LINE_LEN * LINE_LEN
         return left(g_ref[: 3 * wide, at : at + LINE_LEN], k * step - at)
@@ -183,13 +188,28 @@
         peak = jnp.maximum(peak, v)
     peak = jnp.max(peak, axis=0, keepdims=True)
     terms = [[jnp.where(listed, jnp.exp(v - peak), 0.0) for v in group] for group in scores]
+    total = 0.0
+    for k, v in enumerate(terms[0] + terms[1] + terms[2]):
+        total = total + v
+        e_ref[k * half : (k + 1) * half] = v
+    mass = jnp.sum(total, axis=0, keepdims=True)
+    stat_ref[...] = jnp.concatenate([peak, mass, jnp.zeros((6, LINE_LEN), f32)], axis=0)
+
+
+def coef_kernel(n, e_ref, m_ref, s_ref):
+    half = e_ref.shape[0] // 9
+    wide = 2 * half
+    step = 2 * n
+
+    def right(v, k):
+        return pltpu.roll(v, k, 1) if k else v
+
+    flat = [e_ref[k * half : (k + 1) * half] for k in range(9)]
+    terms = [flat[0:3], flat[3:6], flat[6:9]]
     both = [p + m for _, p, m in terms]
     diff = [p - m for _, p, m in terms]
     still = [s for s, _, _ in terms]
-    total = (still[0] + both[0]) + (still[1] + both[1]) + (still[2] + both[2])
-    s_ref[...] = total
-    mass = jnp.sum(total, axis=0, keepdims=True)
-    stat_ref[...] = jnp.concatenate([peak, mass, jnp.zeros((6, LINE_LEN), f32)], axis=0)
+    s_ref[...] = (still[0] + both[0]) + (still[1] + both[1]) + (still[2] + both[2])
     alpha = [
         [still[0], both[0], None],
         [still[1] + still[2], both[1] + both[2], None],
@@ -346,7 +366,6 @@
     groups = lax.axis_size("grp")
     members = lax.axis_size("dev")
     chunks = members // 2
-    chip_bits = chunks.bit_length() - 1
     lines = line_slab.shape[1]
     cap = 2 * lines // groups
     bins = ctf_table.shape[0]
@@ -356,25 +375,43 @@
     trig = jnp.asarray(trig_rows())
     noise = inv_noise[None, :]
 
-    def swap(x, axis, size, mask):
-        return lax.ppermute(x, axis, [(i, i ^ mask) for i in range(size)])
-
-    def turned(t):
-        k = chip_bits // 2
-        return ((t << k) | (t >> (chip_bits - k))) & (chunks - 1)
+    core = dev % 2
+    chip_routes = routes(chunks, CHIP_ROUTES)
+    group_routes = routes(groups, GROUP_ROUTES)
+
+    def swap(x):
+        return lax.ppermute(x, "dev", [(i, i ^ 1) for i in range(members)])
+
+    def chip_pairs(t):
+        return [(i, 2 * chip_routes[i % 2][t - 1][i // 2] + i % 2) for i in range(members)]
+
+    def from_place(x, t):
+        return lax.ppermute(x, "dev", [(j, i) for i, j in chip_pairs(t)])
 
     def to_place(x, t):
+        return lax.ppermute(x, "dev", chip_pairs(t))
+
+    def to_group(x, r):
         return lax.ppermute(
-            x, "dev", [(i, i ^ (2 * (turned(t) if i % 2 else t))) for i in range(members)]
+            x,
+            ("grp", "dev"),
+            [
+                (g * members + i, group_routes[i % 2][r - 1][g] * members + i)
+                for g in range(groups)
+                for i in range(members)
+            ],
         )
+
+    def at_place(t, index, table):
+        return jnp.where(core == 0, lookup(index, table[0][t - 1]), lookup(index, table[1][t - 1]))
 
     def as_lines(x):
         count = x.shape[0]
         x = x.reshape(count, 2, lines, LINE_LEN)
         return jnp.transpose(x, (0, 2, 1, 3)).reshape(2 * count * lines, LINE_LEN)
 
-    part0, part1 = as_lines(particles), as_lines(swap(particles, "dev", members, 1))
-    proj = {t: to_place(projections, t) for t in far_first(chunks)}
+    part0, part1 = as_lines(particles), as_lines(swap(particles))
+    proj = {t: from_place(projections, t) for t in range(1, chunks)}
     proj = [as_lines(p) for p in [projections] + [proj[t] for t in range(1, chunks)]]
 
     def in_hbm(x):
@@ -398,7 +435,7 @@
         ],
         moved=32 * n * pixels,
     )(in_hbm(part0), in_hbm(ctf_table), in_hbm(candidates.T), in_hbm(defocus_bin[None, :]))
-    ints1 = swap(ints0, "dev", members, 1)
+    ints1 = swap(ints0)
     y = call(
         own_kernel,
         jax.ShapeDtypeStruct((12 * n, pixels), bf16),
@@ -417,13 +454,14 @@
     )(part1, table, ints1, y)
 
     row = lax.broadcasted_iota(jnp.int32, (2 * chunks, LINE_LEN), 0)
-    far = jnp.where(dev % 2 == 0, row // 2, turned(row // 2))
-    pid = 4 * ((dev // 2) ^ far) + 2 * (dev % 2) + row % 2
-    m, share, stat = call(
+    chip = jnp.full(row.shape, dev // 2, jnp.int32)
+    for t in range(1, chunks):
+        chip = jnp.where(row // 2 == t, at_place(t, dev // 2, chip_routes), chip)
+    pid = 4 * chip + 2 * core + row % 2
+    terms, stat = call(
         functools.partial(score_kernel, chunks),
         (
-            jax.ShapeDtypeStruct((3 * wide, 2 * LINE_LEN), f32),
-            jax.ShapeDtypeStruct((2 * chunks, LINE_LEN), f32),
+            jax.ShapeDtypeStruct((18 * chunks, LINE_LEN), f32),
             jax.ShapeDtypeStruct((8, LINE_LEN), f32),
         ),
         scratch_shapes=[
@@ -435,7 +473,16 @@
         moved=30 * n * pixels,
     )(*proj, y, table, ints0, ints1, noise, trig, pid)
     line_slab, stat = lax.optimization_barrier((line_slab, stat))
-    other = swap(stat, "dev", members, 1)
+    other = swap(stat)
+    m, share = call(
+        functools.partial(coef_kernel, n),
+        (
+            jax.ShapeDtypeStruct((3 * wide, 2 * LINE_LEN), f32),
+            jax.ShapeDtypeStruct((2 * chunks, LINE_LEN), f32),
+        ),
+        flops=100000,
+        moved=100000,
+    )(terms)
     own, *send = call(
         slice_kernel,
         (jax.ShapeDtypeStruct((4, pixels + LINE_LEN), f32),)
@@ -443,7 +490,7 @@
         flops=2 * 192 * 3 * wide * pixels,
         moved=30 * n * pixels,
     )(y, m, share, stat, other, ints0, ints1, trig)
-    got = [to_place(send[t - 1], t) for t in far_first(chunks)]
+    got = [to_place(send[t - 1], t) for t in range(1, chunks)]
 
     group_ids = jnp.arange(groups, dtype=jnp.int32)
     slab_hit = line_slab[:, :, None] == group_ids[None, None, :]
@@ -452,8 +499,10 @@
     earlier = line_ids[None, :] < line_ids[:, None]
     same_owner = owner_line[:, :, None] == owner_line[:, None, :]
     line_rank = jnp.sum(jnp.logical_and(same_owner, earlier[None]), axis=2)
-    rel = owner_line ^ grp
-    slot = (2 * cap) * rel + cap * jnp.arange(2, dtype=jnp.int32)[:, None] + line_rank
+    place = jnp.zeros_like(owner_line)
+    for r in range(1, groups):
+        place = jnp.where(owner_line == at_place(r, grp, group_routes), r, place)
+    slot = (2 * cap) * place + cap * jnp.arange(2, dtype=jnp.int32)[:, None] + line_rank
     slot = slot.astype(jnp.int32)
 
     sel = call(
@@ -472,7 +521,7 @@
         flops=16 * pixels,
         moved=64 * pixels,
     )(slot, own, *got)
-    recv = [swap(send[r - 1], "grp", groups, r) for r in nearest_first_then_far(groups)]
+    recv = [to_group(send[r - 1], r) for r in [groups - 1, *range(1, groups - 1)]]
     weight_scale = 2 * members / (n * groups * members)
     data, weight = (1, 2, 2, cap, LINE_LEN), (1, 2, cap, LINE_LEN)
     return call(

time: 29.5 us -> 28.7 us (0.973)
  waiting for transfers between devices: 7.78 us -> 7.24 us
  starting transfers between devices: 13.3 us -> 13 us
    ppermute x12, waiting for transfers between devices: 7.78 us -> 7.24 us  [the longest x3 3.51 us: to_place(): return lax.ppermute(x, 'dev', chip_pairs(t))]
    ppermute x12, starting transfers between devices: 13.3 us -> 13 us  [the longest x3 4.53 us: from_place(): return lax.ppermute(x, 'dev', [(j, i) for i, j in chip_pairs(t)])]
    pallas_call x1 -> x2, Pallas kernels: 1.32 us -> 1.34 us  [the longest x1 1.25 us: body(): call(functools.partial(score_kernel, chunks), (jax.ShapeDtypeStruct((18 *...]
  transfers between devices with their start and end apart: 12 -> 12, of which waited for: 7 -> 10; matrix products, arithmetic and copies ran while one was open for 2% -> 2% of each run, Pallas kernels for 13% -> 14%
where the time goes in v4:
time: 28.7 us; the launch traced here: 28.6 us
  starting transfers between devices  13 us (45%)
  waiting for transfers between devices  7.24 us (25%)
  Pallas kernels  7.04 us (25%)
  between operations  0.86 us (3%)
  other arithmetic  0.45 us (2%)
    ppermute x3, starting transfers between devices, from_place(): return lax.ppermute(x, 'dev', [(j, i) for i, j in chip_pairs(t)])  4.53 us
    ppermute x3, starting transfers between devices, to_group(): lax.ppermute(x, ('grp', 'dev'), [(g * members + i, group_routes[i % 2][r...  4.22 us
    ppermute x3, starting transfers between devices, to_place(): return lax.ppermute(x, 'dev', chip_pairs(t))  3.55 us
    ppermute x3, waiting for transfers between devices, to_place(): return lax.ppermute(x, 'dev', chip_pairs(t))  3.51 us
    ppermute x3, waiting for transfers between devices, to_group(): lax.ppermute(x, ('grp', 'dev'), [(g * members + i, group_routes[i % 2][r...  2.14 us
    pallas_call x1, Pallas kernels, body(): call(functools.partial(table_kernel, lines, cap), jax.ShapeDtypeStruct((2...  1.35 us
    pallas_call x1, Pallas kernels, body(): call(functools.partial(score_kernel, chunks), (jax.ShapeDtypeStruct((18 *...  1.25 us
    pallas_call x1, Pallas kernels, body(): call(load_kernel, (jax.ShapeDtypeStruct(part0.shape, bf16), jax.ShapeDtyp...  1.08 us
  transfers between devices with their start and end apart: 12, of which 10 were waited for; matrix products, arithmetic and copies ran while one was open for 2% of the time, Pallas kernels for 14%

profile of v4, /device:TPU:0, one launch (start us, length us, event | category | flops | bytes accessed | tf_op | source)
XLA Modules:
  0.0 28.6 jit_solution(17938951264093630543)
XLA Ops:
  0.6 3.0 %collective-permute-start.2 = (bf16[2,2,6144]{2,1,0:T(2,128)(2,1)}, bf16[2,2,6144]{2,1,0:T(2,128)(2,1)S(1)}, u32[]{:S(2)}, u32[]{:S(2)}) collective-permute-start(bf16[2,2,6144]{2,1,0:T(2,128)(2,1)} %param.12), channel_id=1, source_target_pairs={{2,0},{5,1},{0,2},{1,3},{6,4},{7,5},{4,6},{3,7},{10,8},{13,9},{8,1... | collective-permute-start | bytes 147464 | tf_op jit(solution)/shard_map/ppermute | solution.py:389
  3.6 1.5 %collective-permute-start = (bf16[2,2,6144]{2,1,0:T(2,128)(2,1)}, bf16[2,2,6144]{2,1,0:T(2,128)(2,1)S(1)}, u32[]{:S(2)}, u32[]{:S(2)}) collective-permute-start(bf16[2,2,6144]{2,1,0:T(2,128)(2,1)} %param.12), channel_id=1, source_target_pairs={{6,0},{7,1},{4,2},{5,3},{2,4},{3,5},{0,6},{1,7},{14,8},{15,9},{12,... | collective-permute-start | bytes 147464 | tf_op jit(solution)/shard_map/ppermute | solution.py:389
  5.1 0.1 collective-permute-start.1
  5.2 0.4 %collective-permute-start.3 = (bf16[16,2,6144]{2,1,0:T(2,128)(2,1)}, bf16[16,2,6144]{2,1,0:T(2,128)(2,1)S(1)}, u32[]{:S(2)}, u32[]{:S(2)}) collective-permute-start(bf16[16,2,6144]{2,1,0:T(2,128)(2,1)} %param.9), channel_id=1, source_target_pairs={{0,1},{1,0},{2,3},{3,2},{4,5},{5,4},{6,7},{7,6},{8,9},{9,8},{10,11... | collective-permute-start | bytes 1179656 | tf_op jit(solution)/shard_map/ppermute | solution.py:383
  5.6 1.1 %shard_map.104 = (bf16[1536,128]{1,0:T(8,128)(2,1)S(1)}, bf16[16,6144]{1,0:T(8,128)(2,1)S(1)}, s32[16,16]{1,0:T(8,128)S(1)}) custom-call(bf16[1536,128]{1,0:T(8,128)(2,1)} %bitcast.39, bf16[16,6144]{1,0:T(8,128)(2,1)} %t_hbm.1, s32[8,16]{1,0:T(8,128)} %bitcast.40, s32[1,16]{1,0:T(1,128)} %bitcast.41), custom_call_target="tpu_custom_call" | custom-call | bytes 3145728 | tf_op jit(solution)/shard_map/pallas_call | solution.py:423
  6.7 0.1 collective-permute-start.4
  6.9 0.1 select_add_fusion.refs_10_
  7.0 0.7 %shard_map.105.half_ref = bf16[192,6144]{1,0:T(8,128)(2,1)S(1)} custom-call(bf16[1536,128]{1,0:T(8,128)(2,1)S(1)} %get-tuple-element.21.p_ref, bf16[16,6144]{1,0:T(8,128)(2,1)S(1)} %get-tuple-element.19.tab_ref.refs_5_.table_ref, s32[16,16]{1,0:T(8,128)S(1)} %get-tuple-element.20.d_ref.refs_6_.i0_ref), custom_call_target="tpu_custom_call" | custom-call | flops 1966080 | bytes 3145728 | tf_op jit(solution)/shard_map/pallas_call | solution.py:439
  7.8 0.1 collective-permute-done.4.d_ref.refs_7_.i1_ref
  7.9 0.0 collective-permute-done.3
  7.9 0.0 copy-start
  7.9 0.0 copy-start.1
  7.9 0.0 copy-start.2
  7.9 0.7 %shard_map.106.refs_4_.y_ref = bf16[192,6144]{1,0:T(8,128)(2,1)S(1)} custom-call(bf16[1536,128]{1,0:T(8,128)(2,1)S(1)} %bitcast.33, bf16[16,6144]{1,0:T(8,128)(2,1)S(1)} %get-tuple-element.19.tab_ref.refs_5_.table_ref, s32[16,16]{1,0:T(8,128)S(1)} %collective-permute-done.4.d_ref.refs_7_.i1_ref, ...), custom_call_target="tpu_custom_call", output_to_operand_aliasing={{}: (3, {})} | custom-call | flops 1966080 | bytes 3145728 | tf_op jit(solution)/shard_map/pallas_call | solution.py:446
  8.7 0.0 copy-start.3
  8.7 0.0 copy-start.4
  8.7 0.0 collective-permute-done.2
  8.7 0.1 collective-permute-done
  8.8 0.6 %collective-permute-done.1 = bf16[2,2,6144]{2,1,0:T(2,128)(2,1)S(1)} collective-permute-done((bf16[2,2,6144]{2,1,0:T(2,128)(2,1)}, bf16[2,2,6144]{2,1,0:T(2,128)(2,1)S(1)}, u32[]{:S(2)}, u32[]{:S(2)}) %collective-permute-start.1) | collective-permute-done | bytes 49184 | tf_op jit(solution)/shard_map/ppermute | solution.py:389
  9.4 0.0 copy-done
  9.4 0.0 copy-done.1
  9.4 0.0 copy-done.2
  9.4 1.3 %shard_map.107 = (f32[72,128]{1,0:T(8,128)S(1)}, f32[8,128]{1,0:T(8,128)S(1)}) custom-call(bf16[192,128]{1,0:T(8,128)(2,1)S(1)} %bitcast.34, bf16[192,128]{1,0:T(8,128)(2,1)S(1)} %bitcast.36, bf16[192,128]{1,0:T(8,128)(2,1)S(1)} %bitcast.37, bf16[192,128]{1,0:T(8,128)(2,1)S(1)} %bitcast.35, bf16[192,6144]{1,0:T(8,128)(2,1)S(1)} %shard_map.106.refs_4_.y_ref, ...), custom_call_target="tpu_custom_call" | custom-call | flops 113246208 | bytes 2949120 | tf_op jit(solution)/shard_map/pallas_call | solution.py:461
  10.7 0.1 collective-permute-start.5
  10.8 0.0 copy-done.3
  10.8 0.0 copy-done.4
  10.8 0.1 select_reduce_fusion
  10.9 0.2 convert_reduce_fusion
  11.0 0.1 shard_map.108
  11.1 0.8 %collective-permute-done.5.other_ref = f32[8,128]{1,0:T(8,128)S(1)} collective-permute-done((f32[8,128]{1,0:T(8,128)S(1)}, f32[8,128]{1,0:T(8,128)S(1)}, u32[]{:S(2)}, u32[]{:S(2)}) %collective-permute-start.5) | collective-permute-done | bytes 4128 | tf_op jit(solution)/shard_map/ppermute | solution.py:383
  11.9 0.8 %shard_map.109 = (f32[4,6272]{1,0:T(4,128)S(1)}, bf16[4,6272]{1,0:T(4,128)(2,1)S(1)}, bf16[4,6272]{1,0:T(4,128)(2,1)S(1)}, bf16[4,6272]{1,0:T(4,128)(2,1)S(1)}) custom-call(bf16[192,6144]{1,0:T(8,128)(2,1)S(1)} %shard_map.106.refs_4_.y_ref, f32[48,256]{1,0:T(8,128)S(1)} %get-tuple-element.25.m_ref, f32[8,128]{1,0:T(8,128)S(1)} %get-tuple-element.26.s_ref, ...), custom_call_target="tpu_custom_call" | custom-call | flops 113246208 | bytes 2949120 | tf_op jit(solution)/shard_map/pallas_call | solution.py:486
  12.7 2.2 %collective-permute-start.6 = (bf16[4,6272]{1,0:T(4,128)(2,1)S(1)}, bf16[4,6272]{1,0:T(4,128)(2,1)S(1)}, u32[]{:S(2)}, u32[]{:S(2)}) collective-permute-start(bf16[4,6272]{1,0:T(4,128)(2,1)S(1)} %get-tuple-element.29), channel_id=1, source_target_pairs={{0,6},{1,7},{2,4},{3,5},{4,2},{5,3},{6,0},{7,1},{8,14},{9,15},{10,... | collective-permute-start | bytes 150536 | tf_op jit(solution)/shard_map/ppermute | solution.py:392
  14.9 0.8 %collective-permute-start.7 = (bf16[4,6272]{1,0:T(4,128)(2,1)S(1)}, bf16[4,6272]{1,0:T(4,128)(2,1)S(1)}, u32[]{:S(2)}, u32[]{:S(2)}) collective-permute-start(bf16[4,6272]{1,0:T(4,128)(2,1)S(1)} %get-tuple-element.30), channel_id=1, source_target_pairs={{0,4},{1,3},{2,6},{3,7},{4,0},{5,1},{6,2},{7,5},{8,12},{9,11},{10,... | collective-permute-start | bytes 150536 | tf_op jit(solution)/shard_map/ppermute | solution.py:392
  15.7 0.5 %collective-permute-start.8 = (bf16[4,6272]{1,0:T(4,128)(2,1)S(1)}, bf16[4,6272]{1,0:T(4,128)(2,1)S(1)}, u32[]{:S(2)}, u32[]{:S(2)}) collective-permute-start(bf16[4,6272]{1,0:T(4,128)(2,1)S(1)} %get-tuple-element.31), channel_id=1, source_target_pairs={{0,2},{1,5},{2,0},{3,1},{4,6},{5,7},{6,4},{7,3},{8,10},{9,13},{10,... | collective-permute-start | bytes 150536 | tf_op jit(solution)/shard_map/ppermute | solution.py:392
  16.2 0.1 fusion.2.slot_ref
  16.3 1.6 %collective-permute-done.6.refs_0_ = bf16[4,6272]{1,0:T(4,128)(2,1)S(1)} collective-permute-done((bf16[4,6272]{1,0:T(4,128)(2,1)S(1)}, bf16[4,6272]{1,0:T(4,128)(2,1)S(1)}, u32[]{:S(2)}, u32[]{:S(2)}) %collective-permute-start.6) | collective-permute-done | bytes 50208 | tf_op jit(solution)/shard_map/ppermute | solution.py:392
  17.9 1.1 %collective-permute-done.7.refs_1_ = bf16[4,6272]{1,0:T(4,128)(2,1)S(1)} collective-permute-done((bf16[4,6272]{1,0:T(4,128)(2,1)S(1)}, bf16[4,6272]{1,0:T(4,128)(2,1)S(1)}, u32[]{:S(2)}, u32[]{:S(2)}) %collective-permute-start.7) | collective-permute-done | bytes 50208 | tf_op jit(solution)/shard_map/ppermute | solution.py:392
  19.0 0.8 %collective-permute-done.8.refs_2_ = bf16[4,6272]{1,0:T(4,128)(2,1)S(1)} collective-permute-done((bf16[4,6272]{1,0:T(4,128)(2,1)S(1)}, bf16[4,6272]{1,0:T(4,128)(2,1)S(1)}, u32[]{:S(2)}, u32[]{:S(2)}) %collective-permute-start.8) | collective-permute-done | bytes 50208 | tf_op jit(solution)/shard_map/ppermute | solution.py:392
  19.8 0.3 shard_map.110
  20.1 2.6 %collective-permute-start.10 = (bf16[104,128]{1,0:T(8,128)(2,1)S(1)}, bf16[104,128]{1,0:T(8,128)(2,1)S(1)}, u32[]{:S(2)}, u32[]{:S(2)}) collective-permute-start(bf16[104,128]{1,0:T(8,128)(2,1)S(1)} %get-tuple-element.34), channel_id=1, source_target_pairs={{0,16},{1,17},{2,18},{3,19},{4,20},{5,21},{6,22},{7,23},{8,24},{9,... | collective-permute-start | bytes 79880 | tf_op jit(solution)/shard_map/ppermute | solution.py:395
  22.7 1.2 %collective-permute-start.11 = (bf16[104,128]{1,0:T(8,128)(2,1)S(1)}, bf16[104,128]{1,0:T(8,128)(2,1)S(1)}, u32[]{:S(2)}, u32[]{:S(2)}) collective-permute-start(bf16[104,128]{1,0:T(8,128)(2,1)S(1)} %get-tuple-element.35), channel_id=1, source_target_pairs={{0,24},{1,25},{2,26},{3,27},{4,28},{5,29},{6,30},{7,31},{8,16},{9,... | collective-permute-start | bytes 79880 | tf_op jit(solution)/shard_map/ppermute | solution.py:395
  23.9 0.3 %collective-permute-start.9 = (bf16[104,128]{1,0:T(8,128)(2,1)S(1)}, bf16[104,128]{1,0:T(8,128)(2,1)S(1)}, u32[]{:S(2)}, u32[]{:S(2)}) collective-permute-start(bf16[104,128]{1,0:T(8,128)(2,1)S(1)} %get-tuple-element.33), channel_id=1, source_target_pairs={{0,8},{1,9},{2,10},{3,11},{4,12},{5,13},{6,14},{7,15},{8,0},{9,1},... | collective-permute-start | bytes 79880 | tf_op jit(solution)/shard_map/ppermute | solution.py:395
  24.3 1.4 %shard_map.111.refs_3_ = f32[2,384,128]{2,1,0:T(8,128)S(1)} custom-call(s32[2,48]{1,0:T(2,128)S(1)} %fusion.2.slot_ref, bf16[16,6144]{1,0:T(8,128)(2,1)S(1)} %get-tuple-element.19.tab_ref.refs_5_.table_ref), custom_call_target="tpu_custom_call" | custom-call | flops 98304 | bytes 393216 | tf_op jit(solution)/shard_map/pallas_call | solution.py:508
  25.6 0.4 %collective-permute-done.10.refs_1_ = bf16[104,128]{1,0:T(8,128)(2,1)S(1)} collective-permute-done((bf16[104,128]{1,0:T(8,128)(2,1)S(1)}, bf16[104,128]{1,0:T(8,128)(2,1)S(1)}, u32[]{:S(2)}, u32[]{:S(2)}) %collective-permute-start.10) | collective-permute-done | bytes 26656 | tf_op jit(solution)/shard_map/ppermute | solution.py:395
  26.0 1.4 %collective-permute-done.11.refs_2_ = bf16[104,128]{1,0:T(8,128)(2,1)S(1)} collective-permute-done((bf16[104,128]{1,0:T(8,128)(2,1)S(1)}, bf16[104,128]{1,0:T(8,128)(2,1)S(1)}, u32[]{:S(2)}, u32[]{:S(2)}) %collective-permute-start.11) | collective-permute-done | bytes 26656 | tf_op jit(solution)/shard_map/ppermute | solution.py:395
  27.5 0.3 %collective-permute-done.9.refs_0_ = bf16[104,128]{1,0:T(8,128)(2,1)S(1)} collective-permute-done((bf16[104,128]{1,0:T(8,128)(2,1)S(1)}, bf16[104,128]{1,0:T(8,128)(2,1)S(1)}, u32[]{:S(2)}, u32[]{:S(2)}) %collective-permute-start.9) | collective-permute-done | bytes 26656 | tf_op jit(solution)/shard_map/ppermute | solution.py:395
  27.8 0.8 %shard_map.112 = (f32[1,2,2,24,128]{4,3,2,1,0:T(8,128)}, f32[1,2,24,128]{3,2,1,0:T(8,128)}) custom-call(f32[104,128]{1,0:T(8,128)S(1)} %get-tuple-element.32.own_ref, bf16[104,128]{1,0:T(8,128)(2,1)S(1)} %collective-permute-done.9.refs_0_, bf16[104,128]{1,0:T(8,128)(2,1)S(1)} %collective-permute-done.10.refs_1_, ...), custom_call_target="tpu_custom_call" | custom-call | flops 1000 | bytes 98304 | tf_op jit(solution)/shard_map/pallas_call | solution.py:527
  (5 shorter events, 0.0 us)
Async XLA Ops:
  0.6 8.1 %collective-permute-start.2 = (bf16[2,2,6144]{2,1,0:T(2,128)(2,1)}, bf16[2,2,6144]{2,1,0:T(2,128)(2,1)S(1)}, u32[]{:S(2)}, u32[]{:S(2)}) collective-permute-start(bf16[2,2,6144]{2,1,0:T(2,128)(2,1)} %param.12), channel_id=1, source_target_pairs={{2,0},{5,1},{0,2},{1,3},{6,4},{7,5},{4,6},{3,7},{10,8},{13,9},{8,1... | collective-permute-start | bytes 147464 | tf_op jit(solution)/shard_map/ppermute | solution.py:389
  3.6 5.2 %collective-permute-start = (bf16[2,2,6144]{2,1,0:T(2,128)(2,1)}, bf16[2,2,6144]{2,1,0:T(2,128)(2,1)S(1)}, u32[]{:S(2)}, u32[]{:S(2)}) collective-permute-start(bf16[2,2,6144]{2,1,0:T(2,128)(2,1)} %param.12), channel_id=1, source_target_pairs={{6,0},{7,1},{4,2},{5,3},{2,4},{3,5},{0,6},{1,7},{14,8},{15,9},{12,... | collective-permute-start | bytes 147464 | tf_op jit(solution)/shard_map/ppermute | solution.py:389
  5.1 4.3 %collective-permute-start.1 = (bf16[2,2,6144]{2,1,0:T(2,128)(2,1)}, bf16[2,2,6144]{2,1,0:T(2,128)(2,1)S(1)}, u32[]{:S(2)}, u32[]{:S(2)}) collective-permute-start(bf16[2,2,6144]{2,1,0:T(2,128)(2,1)} %param.12), channel_id=1, source_target_pairs={{4,0},{3,1},{6,2},{7,3},{0,4},{1,5},{2,6},{5,7},{12,8},{11,9},{14,... | collective-permute-start | bytes 147464 | tf_op jit(solution)/shard_map/ppermute | solution.py:389
  5.2 2.8 %collective-permute-start.3 = (bf16[16,2,6144]{2,1,0:T(2,128)(2,1)}, bf16[16,2,6144]{2,1,0:T(2,128)(2,1)S(1)}, u32[]{:S(2)}, u32[]{:S(2)}) collective-permute-start(bf16[16,2,6144]{2,1,0:T(2,128)(2,1)} %param.9), channel_id=1, source_target_pairs={{0,1},{1,0},{2,3},{3,2},{4,5},{5,4},{6,7},{7,6},{8,9},{9,8},{10,11... | collective-permute-start | bytes 1179656 | tf_op jit(solution)/shard_map/ppermute | solution.py:383
  6.7 1.2 %collective-permute-start.4 = (s32[16,16]{1,0:T(8,128)S(1)}, s32[16,16]{1,0:T(8,128)S(1)}, u32[]{:S(2)}, u32[]{:S(2)}) collective-permute-start(s32[16,16]{1,0:T(8,128)S(1)} %get-tuple-element.20.d_ref.refs_6_.i0_ref), channel_id=1, source_target_pairs={{0,1},{1,0},{2,3},{3,2},{4,5},{5,4},{6,7},{7,6},{8,9},{9,8},{10,11... | collective-permute-start | bytes 3080 | tf_op jit(solution)/shard_map/ppermute | solution.py:383
  7.9 1.5 %copy-start = (bf16[2,2,6144]{2,1,0:T(2,128)(2,1)S(1)}, bf16[2,2,6144]{2,1,0:T(2,128)(2,1)}, u32[]{:S(2)}) copy-start(bf16[2,2,6144]{2,1,0:T(2,128)(2,1)} %param.12) | copy-start | bytes 147460
  7.9 1.5 %copy-start.1 = (f32[6144]{0:T(1024)S(1)}, f32[6144]{0:T(1024)}, u32[]{:S(2)}) copy-start(f32[6144]{0:T(1024)} %param.14) | copy-start | bytes 73732
  7.9 1.5 %copy-start.2 = (f32[8,128]{1,0:T(8,128)S(1)}, f32[8,128]{1,0:T(8,128)}, u32[]{:S(2)}) copy-start(f32[8,128]{1,0:T(8,128)} %constant.80.clone.refs_9_.trig_ref) | copy-start | bytes 12292
  8.7 2.1 %copy-start.3 = (s32[2,48]{1,0:T(2,128)S(1)}, s32[2,48]{1,0:T(2,128)}, u32[]{:S(2)}) copy-start(s32[2,48]{1,0:T(2,128)} %param.15) | copy-start | bytes 1156
  8.7 2.1 %copy-start.4 = (s32[4]{0:T(128)S(1)}, s32[4]{0:T(128)}, u32[]{:S(2)}) copy-start(s32[4]{0:T(128)} %param.16) | copy-start | bytes 52
  10.7 1.2 %collective-permute-start.5 = (f32[8,128]{1,0:T(8,128)S(1)}, f32[8,128]{1,0:T(8,128)S(1)}, u32[]{:S(2)}, u32[]{:S(2)}) collective-permute-start(f32[8,128]{1,0:T(8,128)S(1)} %get-tuple-element.27.stat_ref), channel_id=1, source_target_pairs={{0,1},{1,0},{2,3},{3,2},{4,5},{5,4},{6,7},{7,6},{8,9},{9,8},{10,11... | collective-permute-start | bytes 12296 | tf_op jit(solution)/shard_map/ppermute | solution.py:383
  12.7 5.3 %collective-permute-start.6 = (bf16[4,6272]{1,0:T(4,128)(2,1)S(1)}, bf16[4,6272]{1,0:T(4,128)(2,1)S(1)}, u32[]{:S(2)}, u32[]{:S(2)}) collective-permute-start(bf16[4,6272]{1,0:T(4,128)(2,1)S(1)} %get-tuple-element.29), channel_id=1, source_target_pairs={{0,6},{1,7},{2,4},{3,5},{4,2},{5,3},{6,0},{7,1},{8,14},{9,15},{10,... | collective-permute-start | bytes 150536 | tf_op jit(solution)/shard_map/ppermute | solution.py:392
  14.9 4.1 %collective-permute-start.7 = (bf16[4,6272]{1,0:T(4,128)(2,1)S(1)}, bf16[4,6272]{1,0:T(4,128)(2,1)S(1)}, u32[]{:S(2)}, u32[]{:S(2)}) collective-permute-start(bf16[4,6272]{1,0:T(4,128)(2,1)S(1)} %get-tuple-element.30), channel_id=1, source_target_pairs={{0,4},{1,3},{2,6},{3,7},{4,0},{5,1},{6,2},{7,5},{8,12},{9,11},{10,... | collective-permute-start | bytes 150536 | tf_op jit(solution)/shard_map/ppermute | solution.py:392
  15.7 4.1 %collective-permute-start.8 = (bf16[4,6272]{1,0:T(4,128)(2,1)S(1)}, bf16[4,6272]{1,0:T(4,128)(2,1)S(1)}, u32[]{:S(2)}, u32[]{:S(2)}) collective-permute-start(bf16[4,6272]{1,0:T(4,128)(2,1)S(1)} %get-tuple-element.31), channel_id=1, source_target_pairs={{0,2},{1,5},{2,0},{3,1},{4,6},{5,7},{6,4},{7,3},{8,10},{9,13},{10,... | collective-permute-start | bytes 150536 | tf_op jit(solution)/shard_map/ppermute | solution.py:392
  20.1 6.0 %collective-permute-start.10 = (bf16[104,128]{1,0:T(8,128)(2,1)S(1)}, bf16[104,128]{1,0:T(8,128)(2,1)S(1)}, u32[]{:S(2)}, u32[]{:S(2)}) collective-permute-start(bf16[104,128]{1,0:T(8,128)(2,1)S(1)} %get-tuple-element.34), channel_id=1, source_target_pairs={{0,16},{1,17},{2,18},{3,19},{4,20},{5,21},{6,22},{7,23},{8,24},{9,... | collective-permute-start | bytes 79880 | tf_op jit(solution)/shard_map/ppermute | solution.py:395
  22.7 4.7 %collective-permute-start.11 = (bf16[104,128]{1,0:T(8,128)(2,1)S(1)}, bf16[104,128]{1,0:T(8,128)(2,1)S(1)}, u32[]{:S(2)}, u32[]{:S(2)}) collective-permute-start(bf16[104,128]{1,0:T(8,128)(2,1)S(1)} %get-tuple-element.35), channel_id=1, source_target_pairs={{0,24},{1,25},{2,26},{3,27},{4,28},{5,29},{6,30},{7,31},{8,16},{9,... | collective-permute-start | bytes 79880 | tf_op jit(solution)/shard_map/ppermute | solution.py:395
  23.9 3.8 %collective-permute-start.9 = (bf16[104,128]{1,0:T(8,128)(2,1)S(1)}, bf16[104,128]{1,0:T(8,128)(2,1)S(1)}, u32[]{:S(2)}, u32[]{:S(2)}) collective-permute-start(bf16[104,128]{1,0:T(8,128)(2,1)S(1)} %get-tuple-element.33), channel_id=1, source_target_pairs={{0,8},{1,9},{2,10},{3,11},{4,12},{5,13},{6,14},{7,15},{8,0},{9,1},... | collective-permute-start | bytes 79880 | tf_op jit(solution)/shard_map/ppermute | solution.py:395

commit v5 on v4

--- a/solution.py
+++ b/solution.py
@@ -28,7 +28,7 @@
     return rows
 
 
-CHIP_ROUTES = [[[3, 2, 1, 0], [2, 3, 0, 1], [1, 0, 3, 2]], [[3, 2, 1, 0], [1, 3, 0, 2], [2, 0, 3, 1]]]
+CHIP_ROUTES = [[[3, 2, 1, 0], [2, 3, 0, 1], [1, 0, 3, 2]], [[3, 2, 1, 0], [2, 3, 0, 1], [1, 0, 3, 2]]]
 GROUP_ROUTES = [[[2, 3, 1, 0], [3, 2, 0, 1], [1, 0, 3, 2]], [[2, 3, 1, 0], [3, 2, 0, 1], [1, 0, 3, 2]]]
 
 
@@ -66,7 +66,7 @@
     return (row == lax.broadcasted_iota(jnp.int32, (bins, LINE_LEN), 0)).astype(f32)
 
 
-def prep_half(h, part, defocus, tab_ref, y_ref, scr_ref, ctf_ref):
+def prep_half(place, step, part, defocus, tab_ref, y_ref, scr_ref, ctf_ref):
     n = defocus.shape[1]
     bins, pixels = tab_ref.shape
     lines = pixels // LINE_LEN
@@ -80,35 +80,33 @@
         ctf = ctf_ref[:, cols]
         for part in range(2):
             x = scr_ref[pl.ds(2 * l + part, n, stride=2 * lines), :] * ctf
-            base = (2 * part + h) * n
+            base = part * step + place
             y_ref[base : base + n, cols] = x.astype(bf16)
-            base += 4 * n
+            base += 2 * step
             y_ref[base : base + n, cols] = (x * math.cos(l * STEP)).astype(bf16)
-            base += 4 * n
+            base += 2 * step
             y_ref[base : base + n, cols] = (x * math.sin(l * STEP)).astype(bf16)
 
 
-def load_kernel(p_hbm, t_hbm, c_hbm, d_hbm, raw_ref, tab_ref, ints_ref, c_ref, d_ref, sems):
-    copies = [
-        pltpu.make_async_copy(src, dst, sems.at[i])
-        for i, (src, dst) in enumerate(
-            ((p_hbm, raw_ref), (t_hbm, tab_ref), (c_hbm, c_ref), (d_hbm, d_ref))
-        )
-    ]
-    for copy in copies:
-        copy.start()
-    for copy in copies:
-        copy.wait()
+def mark_kernel(o_ref):
+    o_ref[...] = jnp.zeros(o_ref.shape, jnp.int32)
+
+
+def ints_kernel(c_ref, d_ref, mark_ref, ints_ref):
     ints_ref[0:8] = c_ref[...]
-    ints_ref[8:] = jnp.broadcast_to(d_ref[...], (8, d_ref.shape[1]))
+    ints_ref[8:] = jnp.broadcast_to(d_ref[...], (8, d_ref.shape[1])) + mark_ref[...]
 
 
 def own_kernel(p_ref, tab_ref, d_ref, y_ref, scr_ref, ctf_ref):
-    prep_half(0, p_ref[...], d_ref[8:9], tab_ref, y_ref, scr_ref, ctf_ref)
-
-
-def partner_kernel(p_ref, tab_ref, d_ref, half_ref, y_ref, scr_ref, ctf_ref):
-    prep_half(1, p_ref[...], d_ref[8:9], tab_ref, y_ref, scr_ref, ctf_ref)
+    n = d_ref.shape[1]
+    prep_half(0, n, p_ref[...], d_ref[8:9], tab_ref, y_ref, scr_ref, ctf_ref)
+
+
+def partner_kernel(p_ref, tab_ref, d_ref, own_ref, y_ref, scr_ref, ctf_ref):
+    n = d_ref.shape[1]
+    prep_half(n, 2 * n, p_ref[...], d_ref[8:9], tab_ref, y_ref, scr_ref, ctf_ref)
+    for k in range(6):
+        y_ref[2 * k * n : (2 * k + 1) * n, :] = own_ref[k * n : (k + 1) * n, :]
 
 
 def score_kernel(chunks, *refs):
@@ -336,7 +334,7 @@
 
 
 def final_kernel(cap, bins, scale, own_ref, *refs):
-    *recv_refs, sel_ref, data_hbm, weight_hbm, data_ref, weight_ref, sems = refs
+    *recv_refs, sel_ref, data_ref, weight_ref = refs
     x = own_ref[...]
     for ref in recv_refs:
         x = x + ref[...].astype(f32)
@@ -344,8 +342,6 @@
         for j in range(2):
             row = (2 * part + j) * cap
             data_ref[0, j, part] = x[row : row + cap]
-    data_copy = pltpu.make_async_copy(data_ref, data_hbm, sems.at[0])
-    data_copy.start()
     tail = x[4 * cap :] * scale
     for j in range(2):
         total = None
@@ -353,10 +349,6 @@
             term = sel_ref[j, b * cap : (b + 1) * cap] * tail[j : j + 1, b : b + 1]
             total = term if b == 0 else total + term
         weight_ref[0, j] = total
-    weight_copy = pltpu.make_async_copy(weight_ref, weight_hbm, sems.at[1])
-    weight_copy.start()
-    data_copy.wait()
-    weight_copy.wait()
 
 
 def body(
@@ -414,44 +406,32 @@
     proj = {t: from_place(projections, t) for t in range(1, chunks)}
     proj = [as_lines(p) for p in [projections] + [proj[t] for t in range(1, chunks)]]
 
-    def in_hbm(x):
-        return pltpu.with_memory_space_constraint(x, pltpu.HBM)
-
     vmem = pl.BlockSpec(memory_space=pltpu.VMEM)
-    hbm = pl.BlockSpec(memory_space=pl.ANY)
     scratch = [pltpu.VMEM((2 * n * lines, LINE_LEN), f32), pltpu.VMEM((n, pixels), f32)]
-    raw, table, ints0 = call(
-        load_kernel,
-        (
-            jax.ShapeDtypeStruct(part0.shape, bf16),
-            jax.ShapeDtypeStruct((bins, pixels), bf16),
-            jax.ShapeDtypeStruct((16, n), jnp.int32),
-        ),
-        in_specs=[hbm] * 4,
-        scratch_shapes=[
-            pltpu.VMEM((8, n), jnp.int32),
-            pltpu.VMEM((1, n), jnp.int32),
-            pltpu.SemaphoreType.DMA((4,)),
-        ],
+    mark = call(
+        mark_kernel, jax.ShapeDtypeStruct((8, n), jnp.int32), flops=20000000000, moved=1000
+    )()
+    ints0 = call(
+        ints_kernel,
+        jax.ShapeDtypeStruct((16, n), jnp.int32),
+        in_specs=[vmem] * 3,
+        moved=1000,
+    )(candidates.T, defocus_bin[None, :], mark)
+    ints1 = swap(ints0)
+    own_rows = call(
+        own_kernel,
+        jax.ShapeDtypeStruct((6 * n, pixels), bf16),
+        scratch_shapes=scratch,
+        flops=20 * n * pixels,
         moved=32 * n * pixels,
-    )(in_hbm(part0), in_hbm(ctf_table), in_hbm(candidates.T), in_hbm(defocus_bin[None, :]))
-    ints1 = swap(ints0)
+    )(part0, ctf_table, ints0)
     y = call(
-        own_kernel,
+        partner_kernel,
         jax.ShapeDtypeStruct((12 * n, pixels), bf16),
         scratch_shapes=scratch,
         flops=20 * n * pixels,
         moved=32 * n * pixels,
-    )(raw, table, ints0)
-    y = call(
-        partner_kernel,
-        jax.ShapeDtypeStruct((12 * n, pixels), bf16),
-        in_specs=[vmem, vmem, vmem, hbm],
-        scratch_shapes=scratch,
-        input_output_aliases={3: 0},
-        flops=20 * n * pixels,
-        moved=32 * n * pixels,
-    )(part1, table, ints1, y)
+    )(part1, ctf_table, ints1, own_rows)
 
     row = lax.broadcasted_iota(jnp.int32, (2 * chunks, LINE_LEN), 0)
     chip = jnp.full(row.shape, dev // 2, jnp.int32)
@@ -471,7 +451,7 @@
         ],
         flops=2 * 192 * 3 * wide * pixels,
         moved=30 * n * pixels,
-    )(*proj, y, table, ints0, ints1, noise, trig, pid)
+    )(*proj, y, ctf_table, ints0, ints1, noise, trig, pid)
     line_slab, stat = lax.optimization_barrier((line_slab, stat))
     other = swap(stat)
     m, share = call(
@@ -511,7 +491,7 @@
         in_specs=[pl.BlockSpec(memory_space=pltpu.SMEM), vmem],
         flops=bins * pixels,
         moved=4 * bins * pixels,
-    )(slot, table)
+    )(slot, ctf_table)
     size = 4 * cap + 8
     keep, *send = call(
         functools.partial(pack_kernel, lines, cap, chunks),
@@ -528,12 +508,6 @@
         functools.partial(final_kernel, cap, bins, weight_scale),
         (jax.ShapeDtypeStruct(data, f32), jax.ShapeDtypeStruct(weight, f32)),
         in_specs=[vmem] * (groups + 1),
-        out_specs=(hbm, hbm),
-        scratch_shapes=[
-            pltpu.VMEM(data, f32),
-            pltpu.VMEM(weight, f32),
-            pltpu.SemaphoreType.DMA((2,)),
-        ],
         flops=1000,
         moved=8 * 4 * cap * LINE_LEN,
     )(keep, *recv, sel)

time: 28.7 us -> 28.7 us (level)
  Pallas kernels: 7.04 us -> 6.01 us
  waiting for transfers between devices: 7.24 us -> 8.21 us
    pallas_call x3 -> x4, Pallas kernels: 2.57 us -> 1.56 us  [the longest x1 0.81 us: body(): call(partner_kernel, jax.ShapeDtypeStruct((12 * n, pixels), bf16), scratc...]
    ppermute x3, waiting for transfers between devices: 0.69 us -> 1.45 us  [from_place(): return lax.ppermute(x, 'dev', [(j, i) for i, j in chip_pairs(t)])]
  transfers between devices with their start and end apart: 12 -> 12, of which waited for: 10 -> 10; matrix products, arithmetic and copies ran while one was open for 2% -> 2% of each run, Pallas kernels for 14% -> 10%
where the time goes in v5:
time: 28.7 us; the launch traced here: 28.6 us
  starting transfers between devices  13 us (45%)
  waiting for transfers between devices  8.21 us (29%)
  Pallas kernels  6.01 us (21%)
  between operations  0.92 us (3%)
  other arithmetic  0.44 us (2%)
    ppermute x3, starting transfers between devices, from_place(): return lax.ppermute(x, 'dev', [(j, i) for i, j in chip_pairs(t)])  4.55 us
    ppermute x3, starting transfers between devices, to_group(): lax.ppermute(x, ('grp', 'dev'), [(g * members + i, group_routes[i % 2][r...  4.22 us
    ppermute x3, starting transfers between devices, to_place(): return lax.ppermute(x, 'dev', chip_pairs(t))  3.55 us
    ppermute x3, waiting for transfers between devices, to_place(): return lax.ppermute(x, 'dev', chip_pairs(t))  3.49 us
    ppermute x3, waiting for transfers between devices, to_group(): lax.ppermute(x, ('grp', 'dev'), [(g * members + i, group_routes[i % 2][r...  2.15 us
    ppermute x3, waiting for transfers between devices, from_place(): return lax.ppermute(x, 'dev', [(j, i) for i, j in chip_pairs(t)])  1.45 us
    pallas_call x1, Pallas kernels, body(): call(functools.partial(table_kernel, lines, cap), jax.ShapeDtypeStruct((2...  1.34 us
    pallas_call x1, Pallas kernels, body(): call(functools.partial(score_kernel, chunks), (jax.ShapeDtypeStruct((18 *...  1.26 us
  transfers between devices with their start and end apart: 12, of which 10 were waited for; matrix products, arithmetic and copies ran while one was open for 2% of the time, Pallas kernels for 10%

profile of v5, /device:TPU:0, one launch (start us, length us, event | category | flops | bytes accessed | tf_op | source)
XLA Modules:
  0.0 28.6 jit_solution(2109437816863907543)
XLA Ops:
  0.6 0.0 copy-start.5
  0.6 0.0 copy-start.6
  0.7 0.0 copy-start.1
  0.7 0.0 copy-start
  0.7 3.0 %collective-permute-start.2 = (bf16[2,2,6144]{2,1,0:T(2,128)(2,1)}, bf16[2,2,6144]{2,1,0:T(2,128)(2,1)S(1)}, u32[]{:S(2)}, u32[]{:S(2)}) collective-permute-start(bf16[2,2,6144]{2,1,0:T(2,128)(2,1)} %param.12), channel_id=1, source_target_pairs={{2,0},{3,1},{0,2},{1,3},{6,4},{7,5},{4,6},{5,7},{10,8},{11,9},{8,1... | collective-permute-start | bytes 147464 | tf_op jit(solution)/shard_map/ppermute | solution.py:381
  3.7 1.5 %collective-permute-start = (bf16[2,2,6144]{2,1,0:T(2,128)(2,1)}, bf16[2,2,6144]{2,1,0:T(2,128)(2,1)S(1)}, u32[]{:S(2)}, u32[]{:S(2)}) collective-permute-start(bf16[2,2,6144]{2,1,0:T(2,128)(2,1)} %param.12), channel_id=1, source_target_pairs={{6,0},{7,1},{4,2},{5,3},{2,4},{3,5},{0,6},{1,7},{14,8},{15,9},{12,... | collective-permute-start | bytes 147464 | tf_op jit(solution)/shard_map/ppermute | solution.py:381
  5.2 0.1 collective-permute-start.1
  5.2 0.0 copy-done.5
  5.2 0.0 copy-done.6
  5.2 0.1 collective-permute-start.4
  5.3 0.0 copy-done.1
  5.3 0.5 %collective-permute-start.3 = (bf16[16,2,6144]{2,1,0:T(2,128)(2,1)S(1)}, bf16[16,2,6144]{2,1,0:T(2,128)(2,1)S(1)}, u32[]{:S(2)}, u32[]{:S(2)}) collective-permute-start(bf16[16,2,6144]{2,1,0:T(2,128)(2,1)S(1)} %copy-done.1), channel_id=1, source_target_pairs={{0,1},{1,0},{2,3},{3,2},{4,5},{5,4},{6,7},{7,6},{8,9},{9,8},{10,11... | collective-permute-start | bytes 1179656 | tf_op jit(solution)/shard_map/ppermute | solution.py:375
  5.9 0.1 select_add_fusion.refs_10_
  6.0 0.0 copy-done
  6.0 0.7 %shard_map.106.own_ref = bf16[96,6144]{1,0:T(8,128)(2,1)S(1)} custom-call(bf16[1536,128]{1,0:T(8,128)(2,1)S(1)} %bitcast.33, bf16[16,6144]{1,0:T(8,128)(2,1)S(1)} %copy-done, s32[16,16]{1,0:T(8,128)S(1)} %shard_map.105.d_ref.refs_6_.i0_ref), custom_call_target="tpu_custom_call" | custom-call | flops 1966080 | bytes 3145728 | tf_op jit(solution)/shard_map/pallas_call | solution.py:421
  6.8 0.0 copy-start.2
  6.8 0.0 copy-start.3
  6.8 0.0 copy-start.4
  6.8 0.0 collective-permute-done.4.d_ref.refs_7_.i1_ref
  6.8 0.3 %collective-permute-done.3 = bf16[16,2,6144]{2,1,0:T(2,128)(2,1)S(1)} collective-permute-done((bf16[16,2,6144]{2,1,0:T(2,128)(2,1)S(1)}, bf16[16,2,6144]{2,1,0:T(2,128)(2,1)S(1)}, u32[]{:S(2)}, u32[]{:S(2)}) %collective-permute-start.3) | collective-permute-done | bytes 393248 | tf_op jit(solution)/shard_map/ppermute | solution.py:375
  7.2 0.8 %shard_map.107.refs_4_.y_ref = bf16[192,6144]{1,0:T(8,128)(2,1)S(1)} custom-call(bf16[1536,128]{1,0:T(8,128)(2,1)S(1)} %bitcast.34, bf16[16,6144]{1,0:T(8,128)(2,1)S(1)} %copy-done, s32[16,16]{1,0:T(8,128)S(1)} %collective-permute-done.4.d_ref.refs_7_.i1_ref, bf16[96,6144]{1,0:T(8,128)(2,1)S(1)} %shard_map.106.own_ref), custom_call_target="tpu_custom_call" | custom-call | flops 1966080 | bytes 3145728 | tf_op jit(solution)/shard_map/pallas_call | solution.py:428
  8.0 0.0 copy-start.7
  8.0 0.0 copy-start.8
  8.0 0.0 collective-permute-done.2
  8.0 0.9 %collective-permute-done = bf16[2,2,6144]{2,1,0:T(2,128)(2,1)S(1)} collective-permute-done((bf16[2,2,6144]{2,1,0:T(2,128)(2,1)}, bf16[2,2,6144]{2,1,0:T(2,128)(2,1)S(1)}, u32[]{:S(2)}, u32[]{:S(2)}) %collective-permute-start) | collective-permute-done | bytes 49184 | tf_op jit(solution)/shard_map/ppermute | solution.py:381
  8.9 0.6 %collective-permute-done.1 = bf16[2,2,6144]{2,1,0:T(2,128)(2,1)S(1)} collective-permute-done((bf16[2,2,6144]{2,1,0:T(2,128)(2,1)}, bf16[2,2,6144]{2,1,0:T(2,128)(2,1)S(1)}, u32[]{:S(2)}, u32[]{:S(2)}) %collective-permute-start.1) | collective-permute-done | bytes 49184 | tf_op jit(solution)/shard_map/ppermute | solution.py:381
  9.5 0.0 copy-done.2
  9.5 0.0 copy-done.3
  9.5 0.0 copy-done.4
  9.5 1.3 %shard_map.108 = (f32[72,128]{1,0:T(8,128)S(1)}, f32[8,128]{1,0:T(8,128)S(1)}) custom-call(bf16[192,128]{1,0:T(8,128)(2,1)S(1)} %bitcast.35, bf16[192,128]{1,0:T(8,128)(2,1)S(1)} %bitcast.37, bf16[192,128]{1,0:T(8,128)(2,1)S(1)} %bitcast.38, bf16[192,128]{1,0:T(8,128)(2,1)S(1)} %bitcast.36, bf16[192,6144]{1,0:T(8,128)(2,1)S(1)} %shard_map.107.refs_4_.y_ref, ...), custom_call_target="tpu_custom_call" | custom-call | flops 113246208 | bytes 2949120 | tf_op jit(solution)/shard_map/pallas_call | solution.py:441
  10.7 0.1 collective-permute-start.5
  10.8 0.0 copy-done.7
  10.8 0.0 copy-done.8
  10.8 0.1 select_reduce_fusion
  10.9 0.2 convert_reduce_fusion
  11.1 0.1 shard_map.109
  11.2 0.8 %collective-permute-done.5.other_ref = f32[8,128]{1,0:T(8,128)S(1)} collective-permute-done((f32[8,128]{1,0:T(8,128)S(1)}, f32[8,128]{1,0:T(8,128)S(1)}, u32[]{:S(2)}, u32[]{:S(2)}) %collective-permute-start.5) | collective-permute-done | bytes 4128 | tf_op jit(solution)/shard_map/ppermute | solution.py:375
  12.0 0.8 %shard_map.110 = (f32[4,6272]{1,0:T(4,128)S(1)}, bf16[4,6272]{1,0:T(4,128)(2,1)S(1)}, bf16[4,6272]{1,0:T(4,128)(2,1)S(1)}, bf16[4,6272]{1,0:T(4,128)(2,1)S(1)}) custom-call(bf16[192,6144]{1,0:T(8,128)(2,1)S(1)} %shard_map.107.refs_4_.y_ref, f32[48,256]{1,0:T(8,128)S(1)} %get-tuple-element.19.m_ref, f32[8,128]{1,0:T(8,128)S(1)} %get-tuple-element.20.s_ref, ...), custom_call_target="tpu_custom_call" | custom-call | flops 113246208 | bytes 2949120 | tf_op jit(solution)/shard_map/pallas_call | solution.py:466
  12.7 1.6 %collective-permute-start.6 = (bf16[4,6272]{1,0:T(4,128)(2,1)S(1)}, bf16[4,6272]{1,0:T(4,128)(2,1)S(1)}, u32[]{:S(2)}, u32[]{:S(2)}) collective-permute-start(bf16[4,6272]{1,0:T(4,128)(2,1)S(1)} %get-tuple-element.23), channel_id=1, source_target_pairs={{0,6},{1,7},{2,4},{3,5},{4,2},{5,3},{6,0},{7,1},{8,14},{9,15},{10,... | collective-permute-start | bytes 150536 | tf_op jit(solution)/shard_map/ppermute | solution.py:384
  14.3 1.4 %collective-permute-start.7 = (bf16[4,6272]{1,0:T(4,128)(2,1)S(1)}, bf16[4,6272]{1,0:T(4,128)(2,1)S(1)}, u32[]{:S(2)}, u32[]{:S(2)}) collective-permute-start(bf16[4,6272]{1,0:T(4,128)(2,1)S(1)} %get-tuple-element.24), channel_id=1, source_target_pairs={{0,4},{1,5},{2,6},{3,7},{4,0},{5,1},{6,2},{7,3},{8,12},{9,13},{10,... | collective-permute-start | bytes 150536 | tf_op jit(solution)/shard_map/ppermute | solution.py:384
  15.7 0.5 %collective-permute-start.8 = (bf16[4,6272]{1,0:T(4,128)(2,1)S(1)}, bf16[4,6272]{1,0:T(4,128)(2,1)S(1)}, u32[]{:S(2)}, u32[]{:S(2)}) collective-permute-start(bf16[4,6272]{1,0:T(4,128)(2,1)S(1)} %get-tuple-element.25), channel_id=1, source_target_pairs={{0,2},{1,3},{2,0},{3,1},{4,6},{5,7},{6,4},{7,5},{8,10},{9,11},{10,... | collective-permute-start | bytes 150536 | tf_op jit(solution)/shard_map/ppermute | solution.py:384
  16.3 0.1 fusion.2.slot_ref
  16.4 1.5 %collective-permute-done.6.refs_0_ = bf16[4,6272]{1,0:T(4,128)(2,1)S(1)} collective-permute-done((bf16[4,6272]{1,0:T(4,128)(2,1)S(1)}, bf16[4,6272]{1,0:T(4,128)(2,1)S(1)}, u32[]{:S(2)}, u32[]{:S(2)}) %collective-permute-start.6) | collective-permute-done | bytes 50208 | tf_op jit(solution)/shard_map/ppermute | solution.py:384
  17.9 0.8 %collective-permute-done.7.refs_1_ = bf16[4,6272]{1,0:T(4,128)(2,1)S(1)} collective-permute-done((bf16[4,6272]{1,0:T(4,128)(2,1)S(1)}, bf16[4,6272]{1,0:T(4,128)(2,1)S(1)}, u32[]{:S(2)}, u32[]{:S(2)}) %collective-permute-start.7) | collective-permute-done | bytes 50208 | tf_op jit(solution)/shard_map/ppermute | solution.py:384
  18.6 1.2 %collective-permute-done.8.refs_2_ = bf16[4,6272]{1,0:T(4,128)(2,1)S(1)} collective-permute-done((bf16[4,6272]{1,0:T(4,128)(2,1)S(1)}, bf16[4,6272]{1,0:T(4,128)(2,1)S(1)}, u32[]{:S(2)}, u32[]{:S(2)}) %collective-permute-start.8) | collective-permute-done | bytes 50208 | tf_op jit(solution)/shard_map/ppermute | solution.py:384
  19.8 0.3 shard_map.111
  20.1 2.6 %collective-permute-start.10 = (bf16[104,128]{1,0:T(8,128)(2,1)S(1)}, bf16[104,128]{1,0:T(8,128)(2,1)S(1)}, u32[]{:S(2)}, u32[]{:S(2)}) collective-permute-start(bf16[104,128]{1,0:T(8,128)(2,1)S(1)} %get-tuple-element.28), channel_id=1, source_target_pairs={{0,16},{1,17},{2,18},{3,19},{4,20},{5,21},{6,22},{7,23},{8,24},{9,... | collective-permute-start | bytes 79880 | tf_op jit(solution)/shard_map/ppermute | solution.py:387
  22.7 1.2 %collective-permute-start.11 = (bf16[104,128]{1,0:T(8,128)(2,1)S(1)}, bf16[104,128]{1,0:T(8,128)(2,1)S(1)}, u32[]{:S(2)}, u32[]{:S(2)}) collective-permute-start(bf16[104,128]{1,0:T(8,128)(2,1)S(1)} %get-tuple-element.29), channel_id=1, source_target_pairs={{0,24},{1,25},{2,26},{3,27},{4,28},{5,29},{6,30},{7,31},{8,16},{9,... | collective-permute-start | bytes 79880 | tf_op jit(solution)/shard_map/ppermute | solution.py:387
  24.0 0.3 %collective-permute-start.9 = (bf16[104,128]{1,0:T(8,128)(2,1)S(1)}, bf16[104,128]{1,0:T(8,128)(2,1)S(1)}, u32[]{:S(2)}, u32[]{:S(2)}) collective-permute-start(bf16[104,128]{1,0:T(8,128)(2,1)S(1)} %get-tuple-element.27), channel_id=1, source_target_pairs={{0,8},{1,9},{2,10},{3,11},{4,12},{5,13},{6,14},{7,15},{8,0},{9,1},... | collective-permute-start | bytes 79880 | tf_op jit(solution)/shard_map/ppermute | solution.py:387
  24.3 1.3 %shard_map.112.refs_3_ = f32[2,384,128]{2,1,0:T(8,128)S(1)} custom-call(s32[2,48]{1,0:T(2,128)S(1)} %fusion.2.slot_ref, bf16[16,6144]{1,0:T(8,128)(2,1)S(1)} %copy-done), custom_call_target="tpu_custom_call" | custom-call | flops 98304 | bytes 393216 | tf_op jit(solution)/shard_map/pallas_call | solution.py:488
  25.7 0.2 collective-permute-done.10.refs_1_
  25.9 1.6 %collective-permute-done.11.refs_2_ = bf16[104,128]{1,0:T(8,128)(2,1)S(1)} collective-permute-done((bf16[104,128]{1,0:T(8,128)(2,1)S(1)}, bf16[104,128]{1,0:T(8,128)(2,1)S(1)}, u32[]{:S(2)}, u32[]{:S(2)}) %collective-permute-start.11) | collective-permute-done | bytes 26656 | tf_op jit(solution)/shard_map/ppermute | solution.py:387
  27.5 0.3 %collective-permute-done.9.refs_0_ = bf16[104,128]{1,0:T(8,128)(2,1)S(1)} collective-permute-done((bf16[104,128]{1,0:T(8,128)(2,1)S(1)}, bf16[104,128]{1,0:T(8,128)(2,1)S(1)}, u32[]{:S(2)}, u32[]{:S(2)}) %collective-permute-start.9) | collective-permute-done | bytes 26656 | tf_op jit(solution)/shard_map/ppermute | solution.py:387
  27.8 0.8 %shard_map.113 = (f32[1,2,2,24,128]{4,3,2,1,0:T(8,128)}, f32[1,2,24,128]{3,2,1,0:T(8,128)}) custom-call(f32[104,128]{1,0:T(8,128)S(1)} %get-tuple-element.26.own_ref, bf16[104,128]{1,0:T(8,128)(2,1)S(1)} %collective-permute-done.9.refs_0_, bf16[104,128]{1,0:T(8,128)(2,1)S(1)} %collective-permute-done.10.refs_1_, ...), custom_call_target="tpu_custom_call" | custom-call | flops 1000 | bytes 98304 | tf_op jit(solution)/shard_map/pallas_call | solution.py:507
  (7 shorter events, 0.0 us)
Async XLA Ops:
  0.6 4.6 %copy-start.5 = (s32[16,8]{0,1:T(8,128)S(1)}, s32[16,8]{0,1:T(8,128)}, u32[]{:S(2)}) copy-start(s32[16,8]{0,1:T(8,128)} %param.11) | copy-start | bytes 1540
  0.6 4.6 %copy-start.6 = (s32[16]{0:T(128)S(1)}, s32[16]{0:T(128)}, u32[]{:S(2)}) copy-start(s32[16]{0:T(128)} %param.10) | copy-start | bytes 196
  0.7 4.7 %copy-start.1 = (bf16[16,2,6144]{2,1,0:T(2,128)(2,1)S(1)}, bf16[16,2,6144]{2,1,0:T(2,128)(2,1)}, u32[]{:S(2)}) copy-start(bf16[16,2,6144]{2,1,0:T(2,128)(2,1)} %param.9) | copy-start | bytes 1179652
  0.7 5.4 %copy-start = (bf16[16,6144]{1,0:T(8,128)(2,1)S(1)}, bf16[16,6144]{1,0:T(8,128)(2,1)}, u32[]{:S(2)}) copy-start(bf16[16,6144]{1,0:T(8,128)(2,1)} %table_ref.1) | copy-start | bytes 589828
  0.7 7.3 %collective-permute-start.2 = (bf16[2,2,6144]{2,1,0:T(2,128)(2,1)}, bf16[2,2,6144]{2,1,0:T(2,128)(2,1)S(1)}, u32[]{:S(2)}, u32[]{:S(2)}) collective-permute-start(bf16[2,2,6144]{2,1,0:T(2,128)(2,1)} %param.12), channel_id=1, source_target_pairs={{2,0},{3,1},{0,2},{1,3},{6,4},{7,5},{4,6},{5,7},{10,8},{11,9},{8,1... | collective-permute-start | bytes 147464 | tf_op jit(solution)/shard_map/ppermute | solution.py:381
  3.7 5.2 %collective-permute-start = (bf16[2,2,6144]{2,1,0:T(2,128)(2,1)}, bf16[2,2,6144]{2,1,0:T(2,128)(2,1)S(1)}, u32[]{:S(2)}, u32[]{:S(2)}) collective-permute-start(bf16[2,2,6144]{2,1,0:T(2,128)(2,1)} %param.12), channel_id=1, source_target_pairs={{6,0},{7,1},{4,2},{5,3},{2,4},{3,5},{0,6},{1,7},{14,8},{15,9},{12,... | collective-permute-start | bytes 147464 | tf_op jit(solution)/shard_map/ppermute | solution.py:381
  5.2 4.3 %collective-permute-start.1 = (bf16[2,2,6144]{2,1,0:T(2,128)(2,1)}, bf16[2,2,6144]{2,1,0:T(2,128)(2,1)S(1)}, u32[]{:S(2)}, u32[]{:S(2)}) collective-permute-start(bf16[2,2,6144]{2,1,0:T(2,128)(2,1)} %param.12), channel_id=1, source_target_pairs={{4,0},{5,1},{6,2},{7,3},{0,4},{1,5},{2,6},{3,7},{12,8},{13,9},{14,... | collective-permute-start | bytes 147464 | tf_op jit(solution)/shard_map/ppermute | solution.py:381
  5.2 1.6 %collective-permute-start.4 = (s32[16,16]{1,0:T(8,128)S(1)}, s32[16,16]{1,0:T(8,128)S(1)}, u32[]{:S(2)}, u32[]{:S(2)}) collective-permute-start(s32[16,16]{1,0:T(8,128)S(1)} %shard_map.105.d_ref.refs_6_.i0_ref), channel_id=1, source_target_pairs={{0,1},{1,0},{2,3},{3,2},{4,5},{5,4},{6,7},{7,6},{8,9},{9,8},{10,11... | collective-permute-start | bytes 3080 | tf_op jit(solution)/shard_map/ppermute | solution.py:375
  5.3 1.8 %collective-permute-start.3 = (bf16[16,2,6144]{2,1,0:T(2,128)(2,1)S(1)}, bf16[16,2,6144]{2,1,0:T(2,128)(2,1)S(1)}, u32[]{:S(2)}, u32[]{:S(2)}) collective-permute-start(bf16[16,2,6144]{2,1,0:T(2,128)(2,1)S(1)} %copy-done.1), channel_id=1, source_target_pairs={{0,1},{1,0},{2,3},{3,2},{4,5},{5,4},{6,7},{7,6},{8,9},{9,8},{10,11... | collective-permute-start | bytes 1179656 | tf_op jit(solution)/shard_map/ppermute | solution.py:375
  6.8 2.7 %copy-start.2 = (bf16[2,2,6144]{2,1,0:T(2,128)(2,1)S(1)}, bf16[2,2,6144]{2,1,0:T(2,128)(2,1)}, u32[]{:S(2)}) copy-start(bf16[2,2,6144]{2,1,0:T(2,128)(2,1)} %param.12) | copy-start | bytes 147460
  6.8 2.7 %copy-start.3 = (f32[6144]{0:T(1024)S(1)}, f32[6144]{0:T(1024)}, u32[]{:S(2)}) copy-start(f32[6144]{0:T(1024)} %param.14) | copy-start | bytes 73732
  6.8 2.7 %copy-start.4 = (f32[8,128]{1,0:T(8,128)S(1)}, f32[8,128]{1,0:T(8,128)}, u32[]{:S(2)}) copy-start(f32[8,128]{1,0:T(8,128)} %constant.80.clone.refs_9_.trig_ref) | copy-start | bytes 12292
  8.0 2.8 %copy-start.7 = (s32[2,48]{1,0:T(2,128)S(1)}, s32[2,48]{1,0:T(2,128)}, u32[]{:S(2)}) copy-start(s32[2,48]{1,0:T(2,128)} %param.15) | copy-start | bytes 1156
  8.0 2.8 %copy-start.8 = (s32[4]{0:T(128)S(1)}, s32[4]{0:T(128)}, u32[]{:S(2)}) copy-start(s32[4]{0:T(128)} %param.16) | copy-start | bytes 52
  10.7 1.2 %collective-permute-start.5 = (f32[8,128]{1,0:T(8,128)S(1)}, f32[8,128]{1,0:T(8,128)S(1)}, u32[]{:S(2)}, u32[]{:S(2)}) collective-permute-start(f32[8,128]{1,0:T(8,128)S(1)} %get-tuple-element.21.stat_ref), channel_id=1, source_target_pairs={{0,1},{1,0},{2,3},{3,2},{4,5},{5,4},{6,7},{7,6},{8,9},{9,8},{10,11... | collective-permute-start | bytes 12296 | tf_op jit(solution)/shard_map/ppermute | solution.py:375
  12.7 5.1 %collective-permute-start.6 = (bf16[4,6272]{1,0:T(4,128)(2,1)S(1)}, bf16[4,6272]{1,0:T(4,128)(2,1)S(1)}, u32[]{:S(2)}, u32[]{:S(2)}) collective-permute-start(bf16[4,6272]{1,0:T(4,128)(2,1)S(1)} %get-tuple-element.23), channel_id=1, source_target_pairs={{0,6},{1,7},{2,4},{3,5},{4,2},{5,3},{6,0},{7,1},{8,14},{9,15},{10,... | collective-permute-start | bytes 150536 | tf_op jit(solution)/shard_map/ppermute | solution.py:384
  14.3 4.3 %collective-permute-start.7 = (bf16[4,6272]{1,0:T(4,128)(2,1)S(1)}, bf16[4,6272]{1,0:T(4,128)(2,1)S(1)}, u32[]{:S(2)}, u32[]{:S(2)}) collective-permute-start(bf16[4,6272]{1,0:T(4,128)(2,1)S(1)} %get-tuple-element.24), channel_id=1, source_target_pairs={{0,4},{1,5},{2,6},{3,7},{4,0},{5,1},{6,2},{7,3},{8,12},{9,13},{10,... | collective-permute-start | bytes 150536 | tf_op jit(solution)/shard_map/ppermute | solution.py:384
  15.7 4.1 %collective-permute-start.8 = (bf16[4,6272]{1,0:T(4,128)(2,1)S(1)}, bf16[4,6272]{1,0:T(4,128)(2,1)S(1)}, u32[]{:S(2)}, u32[]{:S(2)}) collective-permute-start(bf16[4,6272]{1,0:T(4,128)(2,1)S(1)} %get-tuple-element.25), channel_id=1, source_target_pairs={{0,2},{1,3},{2,0},{3,1},{4,6},{5,7},{6,4},{7,5},{8,10},{9,11},{10,... | collective-permute-start | bytes 150536 | tf_op jit(solution)/shard_map/ppermute | solution.py:384
  20.1 5.8 %collective-permute-start.10 = (bf16[104,128]{1,0:T(8,128)(2,1)S(1)}, bf16[104,128]{1,0:T(8,128)(2,1)S(1)}, u32[]{:S(2)}, u32[]{:S(2)}) collective-permute-start(bf16[104,128]{1,0:T(8,128)(2,1)S(1)} %get-tuple-element.28), channel_id=1, source_target_pairs={{0,16},{1,17},{2,18},{3,19},{4,20},{5,21},{6,22},{7,23},{8,24},{9,... | collective-permute-start | bytes 79880 | tf_op jit(solution)/shard_map/ppermute | solution.py:387
  22.7 4.7 %collective-permute-start.11 = (bf16[104,128]{1,0:T(8,128)(2,1)S(1)}, bf16[104,128]{1,0:T(8,128)(2,1)S(1)}, u32[]{:S(2)}, u32[]{:S(2)}) collective-permute-start(bf16[104,128]{1,0:T(8,128)(2,1)S(1)} %get-tuple-element.29), channel_id=1, source_target_pairs={{0,24},{1,25},{2,26},{3,27},{4,28},{5,29},{6,30},{7,31},{8,16},{9,... | collective-permute-start | bytes 79880 | tf_op jit(solution)/shard_map/ppermute | solution.py:387
  24.0 3.8 %collective-permute-start.9 = (bf16[104,128]{1,0:T(8,128)(2,1)S(1)}, bf16[104,128]{1,0:T(8,128)(2,1)S(1)}, u32[]{:S(2)}, u32[]{:S(2)}) collective-permute-start(bf16[104,128]{1,0:T(8,128)(2,1)S(1)} %get-tuple-element.27), channel_id=1, source_target_pairs={{0,8},{1,9},{2,10},{3,11},{4,12},{5,13},{6,14},{7,15},{8,0},{9,1},... | collective-permute-start | bytes 79880 | tf_op jit(solution)/shard_map/ppermute | solution.py:387

commit v6 on v5

--- a/solution.py
+++ b/solution.py
@@ -28,7 +28,7 @@
     return rows
 
 
-CHIP_ROUTES = [[[3, 2, 1, 0], [2, 3, 0, 1], [1, 0, 3, 2]], [[3, 2, 1, 0], [2, 3, 0, 1], [1, 0, 3, 2]]]
+CHIP_ROUTES = [[[2, 3, 0, 1], [1, 0, 3, 2], [3, 2, 1, 0]], [[2, 3, 0, 1], [1, 0, 3, 2], [3, 2, 1, 0]]]
 GROUP_ROUTES = [[[2, 3, 1, 0], [3, 2, 0, 1], [1, 0, 3, 2]], [[2, 3, 1, 0], [3, 2, 0, 1], [1, 0, 3, 2]]]
 
 
@@ -247,7 +247,7 @@
 
 
 def slice_kernel(
-    y_ref, m_ref, s_ref, stat_ref, other_ref, i0_ref, i1_ref, trig_ref, keep_ref, *send_refs
+    y_ref, m_ref, s_ref, stat_ref, other_ref, i0_ref, i1_ref, trig_ref, *send_refs
 ):
     n = i0_ref.shape[1]
     pixels = y_ref.shape[1]
@@ -282,21 +282,19 @@
         cols = slice(c * width, (c + 1) * width)
         x = jnp.dot(m, y_ref[:, cols], preferred_element_type=f32)
         x = x[:wide] + x[wide : 2 * wide] * cos_row + x[2 * wide :] * sin_row
-        keep_ref[:, cols] = x[:4]
-        for s, ref in enumerate(send_refs, 1):
+        for s, ref in enumerate(send_refs):
             ref[:, cols] = x[4 * s : 4 * s + 4].astype(bf16)
-    keep_ref[:, pixels:] = share[:4]
-    for s, ref in enumerate(send_refs, 1):
+    for s, ref in enumerate(send_refs):
         ref[:, pixels:] = share[4 * s : 4 * s + 4].astype(bf16)
 
 
 def pack_kernel(lines, cap, chunks, slot_ref, own_ref, *refs):
     recv_refs = refs[: chunks - 1]
-    keep_ref, *send_refs, scr_ref = refs[chunks - 1 :]
+    *send_refs, scr_ref = refs[chunks - 1 :]
     size = 2 * cap
     for l in range(lines + 1):
         cols = slice(l * LINE_LEN, (l + 1) * LINE_LEN)
-        x = own_ref[:, cols]
+        x = own_ref[:, cols].astype(f32)
         for ref in recv_refs:
             x = x + ref[:, cols].astype(f32)
         if l < lines:
@@ -307,12 +305,12 @@
         else:
             tail = jnp.concatenate([x, jnp.zeros((4, LINE_LEN), f32)], axis=0)
     slots = jnp.concatenate([slot_ref[0:1], slot_ref[1:2]], axis=1)
-    rows = size * (len(send_refs) + 1)
+    rows = size * len(send_refs)
     pick = slots == lax.broadcasted_iota(jnp.int32, (rows, 2 * lines), 0)
     packed = jnp.dot(
         pick.astype(f32).astype(bf16), scr_ref[...].astype(bf16), preferred_element_type=f32
     )
-    for r, ref in enumerate([keep_ref] + send_refs):
+    for r, ref in enumerate(send_refs):
         for part in range(2):
             piece = packed[r * size : (r + 1) * size, part * LINE_LEN : (part + 1) * LINE_LEN]
             ref[part * size : (part + 1) * size] = piece.astype(ref.dtype)
@@ -335,7 +333,7 @@
 
 def final_kernel(cap, bins, scale, own_ref, *refs):
     *recv_refs, sel_ref, data_ref, weight_ref = refs
-    x = own_ref[...]
+    x = own_ref[...].astype(f32)
     for ref in recv_refs:
         x = x + ref[...].astype(f32)
     for part in range(2):
@@ -381,14 +379,14 @@
         return lax.ppermute(x, "dev", [(j, i) for i, j in chip_pairs(t)])
 
     def to_place(x, t):
-        return lax.ppermute(x, "dev", chip_pairs(t))
+        return lax.ppermute(x, "dev", [(i, j ^ 1) for i, j in chip_pairs(t)])
 
     def to_group(x, r):
         return lax.ppermute(
             x,
             ("grp", "dev"),
             [
-                (g * members + i, group_routes[i % 2][r - 1][g] * members + i)
+                (g * members + i, group_routes[i % 2][r - 1][g] * members + (i ^ 1))
                 for g in range(groups)
                 for i in range(members)
             ],
@@ -463,14 +461,14 @@
         flops=100000,
         moved=100000,
     )(terms)
-    own, *send = call(
+    send = call(
         slice_kernel,
-        (jax.ShapeDtypeStruct((4, pixels + LINE_LEN), f32),)
-        + (jax.ShapeDtypeStruct((4, pixels + LINE_LEN), bf16),) * (chunks - 1),
+        (jax.ShapeDtypeStruct((4, pixels + LINE_LEN), bf16),) * chunks,
         flops=2 * 192 * 3 * wide * pixels,
         moved=30 * n * pixels,
     )(y, m, share, stat, other, ints0, ints1, trig)
-    got = [to_place(send[t - 1], t) for t in range(1, chunks)]
+    got = [to_place(send[t], t) for t in range(1, chunks)]
+    own = swap(send[0])
 
     group_ids = jnp.arange(groups, dtype=jnp.int32)
     slab_hit = line_slab[:, :, None] == group_ids[None, None, :]
@@ -493,15 +491,15 @@
         moved=4 * bins * pixels,
     )(slot, ctf_table)
     size = 4 * cap + 8
-    keep, *send = call(
+    send = call(
         functools.partial(pack_kernel, lines, cap, chunks),
-        (jax.ShapeDtypeStruct((size, LINE_LEN), f32),)
-        + (jax.ShapeDtypeStruct((size, LINE_LEN), bf16),) * (groups - 1),
+        (jax.ShapeDtypeStruct((size, LINE_LEN), bf16),) * groups,
         scratch_shapes=[pltpu.VMEM((2 * lines, 2 * LINE_LEN), f32)],
         flops=16 * pixels,
         moved=64 * pixels,
-    )(slot, own, *got)
-    recv = [to_group(send[r - 1], r) for r in [groups - 1, *range(1, groups - 1)]]
+    )(swap(slot), own, *got)
+    recv = [to_group(send[r], r) for r in range(1, groups)]
+    keep = swap(send[0])
     weight_scale = 2 * members / (n * groups * members)
     data, weight = (1, 2, 2, cap, LINE_LEN), (1, 2, cap, LINE_LEN)
     return call(

time: 28.7 us -> 27.6 us (0.962)
  waiting for transfers between devices: 8.21 us -> 7.13 us
    ppermute x3, waiting for transfers between devices: 3.49 us -> 1.38 us  [to_place(): return lax.ppermute(x, 'dev', [(i, j ^ 1) for i, j in chip_pairs(t)])]
    ppermute x3 -> x6, waiting for transfers between devices: 1.12 us -> 2.1 us  [swap(): return lax.ppermute(x, 'dev', [(i, i ^ 1) for i in range(members)])]
    ppermute x3 -> x6, starting transfers between devices: 0.63 us -> 1.15 us  [swap(): return lax.ppermute(x, 'dev', [(i, i ^ 1) for i in range(members)])]
    ppermute x3, starting transfers between devices: 4.22 us -> 3.88 us  [to_group(): lax.ppermute(x, ('grp', 'dev'), [(g * members + i, group_routes[i % 2][r...]
    ppermute x3, starting transfers between devices: 3.55 us -> 3.22 us  [to_place(): return lax.ppermute(x, 'dev', [(i, j ^ 1) for i, j in chip_pairs(t)])]
  transfers between devices with their start and end apart: 12 -> 15, of which waited for: 10 -> 10; matrix products, arithmetic and copies ran while one was open for 2% -> 2% of each run, Pallas kernels for 10% -> 11%
where the time goes in v6:
time: 27.6 us; the launch traced here: 27.4 us
  starting transfers between devices  12.9 us (47%)
  waiting for transfers between devices  7.13 us (26%)
  Pallas kernels  6.01 us (22%)
  between operations  0.94 us (3%)
  other arithmetic  0.44 us (2%)
    ppermute x3, starting transfers between devices, from_place(): return lax.ppermute(x, 'dev', [(j, i) for i, j in chip_pairs(t)])  4.6 us
    ppermute x3, starting transfers between devices, to_group(): lax.ppermute(x, ('grp', 'dev'), [(g * members + i, group_routes[i % 2][r...  3.88 us
    ppermute x3, starting transfers between devices, to_place(): return lax.ppermute(x, 'dev', [(i, j ^ 1) for i, j in chip_pairs(t)])  3.22 us
    ppermute x3, waiting for transfers between devices, to_group(): lax.ppermute(x, ('grp', 'dev'), [(g * members + i, group_routes[i % 2][r...  2.28 us
    ppermute x6, waiting for transfers between devices, swap(): return lax.ppermute(x, 'dev', [(i, i ^ 1) for i in range(members)])  2.1 us
    ppermute x3, waiting for transfers between devices, to_place(): return lax.ppermute(x, 'dev', [(i, j ^ 1) for i, j in chip_pairs(t)])  1.38 us
    ppermute x3, waiting for transfers between devices, from_place(): return lax.ppermute(x, 'dev', [(j, i) for i, j in chip_pairs(t)])  1.37 us
    pallas_call x1, Pallas kernels, body(): call(functools.partial(table_kernel, lines, cap), jax.ShapeDtypeStruct((2...  1.35 us
  transfers between devices with their start and end apart: 15, of which 10 were waited for; matrix products, arithmetic and copies ran while one was open for 2% of the time, Pallas kernels for 11%

profile of v6, /device:TPU:0, one launch (start us, length us, event | category | flops | bytes accessed | tf_op | source)
XLA Modules:
  0.0 27.4 jit_solution(8878474869512459135)
XLA Ops:
  0.6 0.0 copy-start.5
  0.6 0.0 copy-start.6
  0.7 0.0 copy-start.1
  0.7 0.0 copy-start
  0.7 4.0 %collective-permute-start.2 = (bf16[2,2,6144]{2,1,0:T(2,128)(2,1)}, bf16[2,2,6144]{2,1,0:T(2,128)(2,1)S(1)}, u32[]{:S(2)}, u32[]{:S(2)}) collective-permute-start(bf16[2,2,6144]{2,1,0:T(2,128)(2,1)} %param.12), channel_id=1, source_target_pairs={{6,0},{7,1},{4,2},{5,3},{2,4},{3,5},{0,6},{1,7},{14,8},{15,9},{12,... | collective-permute-start | bytes 147464 | tf_op jit(solution)/shard_map/ppermute | solution.py:379
  4.6 0.5 %collective-permute-start = (bf16[2,2,6144]{2,1,0:T(2,128)(2,1)}, bf16[2,2,6144]{2,1,0:T(2,128)(2,1)S(1)}, u32[]{:S(2)}, u32[]{:S(2)}) collective-permute-start(bf16[2,2,6144]{2,1,0:T(2,128)(2,1)} %param.12), channel_id=1, source_target_pairs={{4,0},{5,1},{6,2},{7,3},{0,4},{1,5},{2,6},{3,7},{12,8},{13,9},{14,... | collective-permute-start | bytes 147464 | tf_op jit(solution)/shard_map/ppermute | solution.py:379
  5.1 0.1 collective-permute-start.1
  5.3 0.0 copy-done.5
  5.3 0.0 copy-done.6
  5.3 0.1 collective-permute-start.4
  5.4 0.0 copy-done.1
  5.4 0.5 %collective-permute-start.3 = (bf16[16,2,6144]{2,1,0:T(2,128)(2,1)S(1)}, bf16[16,2,6144]{2,1,0:T(2,128)(2,1)S(1)}, u32[]{:S(2)}, u32[]{:S(2)}) collective-permute-start(bf16[16,2,6144]{2,1,0:T(2,128)(2,1)S(1)} %copy-done.1), channel_id=1, source_target_pairs={{0,1},{1,0},{2,3},{3,2},{4,5},{5,4},{6,7},{7,6},{8,9},{9,8},{10,11... | collective-permute-start | bytes 1179656 | tf_op jit(solution)/shard_map/ppermute | solution.py:373
  6.0 0.1 select_add_fusion.refs_10_
  6.1 0.0 copy-done
  6.1 0.7 %shard_map.106.own_ref = bf16[96,6144]{1,0:T(8,128)(2,1)S(1)} custom-call(bf16[1536,128]{1,0:T(8,128)(2,1)S(1)} %bitcast.33, bf16[16,6144]{1,0:T(8,128)(2,1)S(1)} %copy-done, s32[16,16]{1,0:T(8,128)S(1)} %shard_map.105.d_ref.refs_6_.i0_ref), custom_call_target="tpu_custom_call" | custom-call | flops 1966080 | bytes 3145728 | tf_op jit(solution)/shard_map/pallas_call | solution.py:419
  6.8 0.0 copy-start.2
  6.8 0.0 copy-start.3
  6.8 0.0 copy-start.4
  6.9 0.0 collective-permute-done.4.d_ref.refs_7_.i1_ref
  6.9 0.3 %collective-permute-done.3 = bf16[16,2,6144]{2,1,0:T(2,128)(2,1)S(1)} collective-permute-done((bf16[16,2,6144]{2,1,0:T(2,128)(2,1)S(1)}, bf16[16,2,6144]{2,1,0:T(2,128)(2,1)S(1)}, u32[]{:S(2)}, u32[]{:S(2)}) %collective-permute-start.3) | collective-permute-done | bytes 393248 | tf_op jit(solution)/shard_map/ppermute | solution.py:373
  7.2 0.8 %shard_map.107.refs_4_.y_ref = bf16[192,6144]{1,0:T(8,128)(2,1)S(1)} custom-call(bf16[1536,128]{1,0:T(8,128)(2,1)S(1)} %bitcast.34, bf16[16,6144]{1,0:T(8,128)(2,1)S(1)} %copy-done, s32[16,16]{1,0:T(8,128)S(1)} %collective-permute-done.4.d_ref.refs_7_.i1_ref, bf16[96,6144]{1,0:T(8,128)(2,1)S(1)} %shard_map.106.own_ref), custom_call_target="tpu_custom_call" | custom-call | flops 1966080 | bytes 3145728 | tf_op jit(solution)/shard_map/pallas_call | solution.py:426
  8.0 0.0 copy-start.7
  8.0 0.0 copy-start.8
  8.1 0.0 collective-permute-done.2
  8.1 0.9 %collective-permute-done = bf16[2,2,6144]{2,1,0:T(2,128)(2,1)S(1)} collective-permute-done((bf16[2,2,6144]{2,1,0:T(2,128)(2,1)}, bf16[2,2,6144]{2,1,0:T(2,128)(2,1)S(1)}, u32[]{:S(2)}, u32[]{:S(2)}) %collective-permute-start) | collective-permute-done | bytes 49184 | tf_op jit(solution)/shard_map/ppermute | solution.py:379
  8.9 0.5 %collective-permute-done.1 = bf16[2,2,6144]{2,1,0:T(2,128)(2,1)S(1)} collective-permute-done((bf16[2,2,6144]{2,1,0:T(2,128)(2,1)}, bf16[2,2,6144]{2,1,0:T(2,128)(2,1)S(1)}, u32[]{:S(2)}, u32[]{:S(2)}) %collective-permute-start.1) | collective-permute-done | bytes 49184 | tf_op jit(solution)/shard_map/ppermute | solution.py:379
  9.4 0.0 copy-done.2
  9.4 0.0 copy-done.3
  9.4 0.0 copy-done.4
  9.4 1.3 %shard_map.108 = (f32[72,128]{1,0:T(8,128)S(1)}, f32[8,128]{1,0:T(8,128)S(1)}) custom-call(bf16[192,128]{1,0:T(8,128)(2,1)S(1)} %bitcast.35, bf16[192,128]{1,0:T(8,128)(2,1)S(1)} %bitcast.37, bf16[192,128]{1,0:T(8,128)(2,1)S(1)} %bitcast.38, bf16[192,128]{1,0:T(8,128)(2,1)S(1)} %bitcast.36, bf16[192,6144]{1,0:T(8,128)(2,1)S(1)} %shard_map.107.refs_4_.y_ref, ...), custom_call_target="tpu_custom_call" | custom-call | flops 113246208 | bytes 2949120 | tf_op jit(solution)/shard_map/pallas_call | solution.py:439
  10.7 0.1 collective-permute-start.6
  10.8 0.0 copy-done.7
  10.8 0.0 copy-done.8
  10.8 0.1 select_reduce_fusion
  10.9 0.2 convert_reduce_fusion
  11.1 0.1 shard_map.109
  11.2 0.8 %collective-permute-done.6.other_ref = f32[8,128]{1,0:T(8,128)S(1)} collective-permute-done((f32[8,128]{1,0:T(8,128)S(1)}, f32[8,128]{1,0:T(8,128)S(1)}, u32[]{:S(2)}, u32[]{:S(2)}) %collective-permute-start.6) | collective-permute-done | bytes 4128 | tf_op jit(solution)/shard_map/ppermute | solution.py:373
  11.9 0.8 %shard_map.110 = (bf16[4,6272]{1,0:T(4,128)(2,1)S(1)}, bf16[4,6272]{1,0:T(4,128)(2,1)S(1)}, bf16[4,6272]{1,0:T(4,128)(2,1)S(1)}, bf16[4,6272]{1,0:T(4,128)(2,1)S(1)}) custom-call(bf16[192,6144]{1,0:T(8,128)(2,1)S(1)} %shard_map.107.refs_4_.y_ref, f32[48,256]{1,0:T(8,128)S(1)} %get-tuple-element.19.m_ref, f32[8,128]{1,0:T(8,128)S(1)} %get-tuple-element.20.s_ref, ...), custom_call_target="tpu_custom_call" | custom-call | flops 113246208 | bytes 2949120 | tf_op jit(solution)/shard_map/pallas_call | solution.py:464
  12.7 1.6 %collective-permute-start.10 = (bf16[4,6272]{1,0:T(4,128)(2,1)S(1)}, bf16[4,6272]{1,0:T(4,128)(2,1)S(1)}, u32[]{:S(2)}, u32[]{:S(2)}) collective-permute-start(bf16[4,6272]{1,0:T(4,128)(2,1)S(1)} %get-tuple-element.25), channel_id=1, source_target_pairs={{0,7},{1,6},{2,5},{3,4},{4,3},{5,2},{6,1},{7,0},{8,15},{9,14},{10,... | collective-permute-start | bytes 150536 | tf_op jit(solution)/shard_map/ppermute | solution.py:382
  14.3 0.2 collective-permute-start.7
  14.4 0.5 %collective-permute-start.8 = (bf16[4,6272]{1,0:T(4,128)(2,1)S(1)}, bf16[4,6272]{1,0:T(4,128)(2,1)S(1)}, u32[]{:S(2)}, u32[]{:S(2)}) collective-permute-start(bf16[4,6272]{1,0:T(4,128)(2,1)S(1)} %get-tuple-element.23), channel_id=1, source_target_pairs={{0,5},{1,4},{2,7},{3,6},{4,1},{5,0},{6,3},{7,2},{8,13},{9,12},{10,... | collective-permute-start | bytes 150536 | tf_op jit(solution)/shard_map/ppermute | solution.py:382
  14.9 1.2 %collective-permute-start.9 = (bf16[4,6272]{1,0:T(4,128)(2,1)S(1)}, bf16[4,6272]{1,0:T(4,128)(2,1)S(1)}, u32[]{:S(2)}, u32[]{:S(2)}) collective-permute-start(bf16[4,6272]{1,0:T(4,128)(2,1)S(1)} %get-tuple-element.24), channel_id=1, source_target_pairs={{0,3},{1,2},{2,1},{3,0},{4,7},{5,6},{6,5},{7,4},{8,11},{9,10},{10,... | collective-permute-start | bytes 150536 | tf_op jit(solution)/shard_map/ppermute | solution.py:382
  16.1 0.1 fusion.2.slot_ref
  16.2 0.2 collective-permute-start.5
  16.3 1.0 %collective-permute-done.5.slot_ref = s32[2,48]{1,0:T(2,128)S(1)} collective-permute-done((s32[2,48]{1,0:T(2,128)S(1)}, s32[2,48]{1,0:T(2,128)S(1)}, u32[]{:S(2)}, u32[]{:S(2)}) %collective-permute-start.5) | collective-permute-done | bytes 416 | tf_op jit(solution)/shard_map/ppermute | solution.py:373
  17.3 0.2 collective-permute-done.10.refs_2_
  17.5 0.0 collective-permute-done.7.own_ref
  17.5 1.1 %collective-permute-done.8.refs_0_ = bf16[4,6272]{1,0:T(4,128)(2,1)S(1)} collective-permute-done((bf16[4,6272]{1,0:T(4,128)(2,1)S(1)}, bf16[4,6272]{1,0:T(4,128)(2,1)S(1)}, u32[]{:S(2)}, u32[]{:S(2)}) %collective-permute-start.8) | collective-permute-done | bytes 50208 | tf_op jit(solution)/shard_map/ppermute | solution.py:382
  18.6 0.1 collective-permute-done.9.refs_1_
  18.7 0.3 shard_map.111
  18.9 0.2 collective-permute-start.11
  19.1 2.6 %collective-permute-start.12 = (bf16[104,128]{1,0:T(8,128)(2,1)S(1)}, bf16[104,128]{1,0:T(8,128)(2,1)S(1)}, u32[]{:S(2)}, u32[]{:S(2)}) collective-permute-start(bf16[104,128]{1,0:T(8,128)(2,1)S(1)} %get-tuple-element.27), channel_id=1, source_target_pairs={{0,17},{1,16},{2,19},{3,18},{4,21},{5,20},{6,23},{7,22},{8,25},{9,... | collective-permute-start | bytes 79880 | tf_op jit(solution)/shard_map/ppermute | solution.py:385
  21.7 1.0 %collective-permute-start.13 = (bf16[104,128]{1,0:T(8,128)(2,1)S(1)}, bf16[104,128]{1,0:T(8,128)(2,1)S(1)}, u32[]{:S(2)}, u32[]{:S(2)}) collective-permute-start(bf16[104,128]{1,0:T(8,128)(2,1)S(1)} %get-tuple-element.28), channel_id=1, source_target_pairs={{0,25},{1,24},{2,27},{3,26},{4,29},{5,28},{6,31},{7,30},{8,17},{9,... | collective-permute-start | bytes 79880 | tf_op jit(solution)/shard_map/ppermute | solution.py:385
  22.7 0.3 %collective-permute-start.14 = (bf16[104,128]{1,0:T(8,128)(2,1)S(1)}, bf16[104,128]{1,0:T(8,128)(2,1)S(1)}, u32[]{:S(2)}, u32[]{:S(2)}) collective-permute-start(bf16[104,128]{1,0:T(8,128)(2,1)S(1)} %get-tuple-element.29), channel_id=1, source_target_pairs={{0,9},{1,8},{2,11},{3,10},{4,13},{5,12},{6,15},{7,14},{8,1},{9,0},... | collective-permute-start | bytes 79880 | tf_op jit(solution)/shard_map/ppermute | solution.py:385
  23.0 1.3 %shard_map.112.refs_3_ = f32[2,384,128]{2,1,0:T(8,128)S(1)} custom-call(s32[2,48]{1,0:T(2,128)S(1)} %fusion.2.slot_ref, bf16[16,6144]{1,0:T(8,128)(2,1)S(1)} %copy-done), custom_call_target="tpu_custom_call" | custom-call | flops 98304 | bytes 393216 | tf_op jit(solution)/shard_map/pallas_call | solution.py:486
  24.4 0.0 collective-permute-done.11.own_ref
  24.4 0.0 collective-permute-done.12.refs_0_
  24.4 1.5 %collective-permute-done.13.refs_1_ = bf16[104,128]{1,0:T(8,128)(2,1)S(1)} collective-permute-done((bf16[104,128]{1,0:T(8,128)(2,1)S(1)}, bf16[104,128]{1,0:T(8,128)(2,1)S(1)}, u32[]{:S(2)}, u32[]{:S(2)}) %collective-permute-start.13) | collective-permute-done | bytes 26656 | tf_op jit(solution)/shard_map/ppermute | solution.py:385
  25.9 0.8 %collective-permute-done.14.refs_2_ = bf16[104,128]{1,0:T(8,128)(2,1)S(1)} collective-permute-done((bf16[104,128]{1,0:T(8,128)(2,1)S(1)}, bf16[104,128]{1,0:T(8,128)(2,1)S(1)}, u32[]{:S(2)}, u32[]{:S(2)}) %collective-permute-start.14) | collective-permute-done | bytes 26656 | tf_op jit(solution)/shard_map/ppermute | solution.py:385
  26.7 0.8 %shard_map.113 = (f32[1,2,2,24,128]{4,3,2,1,0:T(8,128)}, f32[1,2,24,128]{3,2,1,0:T(8,128)}) custom-call(bf16[104,128]{1,0:T(8,128)(2,1)S(1)} %collective-permute-done.11.own_ref, bf16[104,128]{1,0:T(8,128)(2,1)S(1)} %collective-permute-done.12.refs_0_, bf16[104,128]{1,0:T(8,128)(2,1)S(1)} %collective-permute-done.13.refs_1_, ...), custom_call_target="tpu_custom_call" | custom-call | flops 1000 | bytes 98304 | tf_op jit(solution)/shard_map/pallas_call | solution.py:505
  (7 shorter events, 0.0 us)
Async XLA Ops:
  0.6 4.6 %copy-start.5 = (s32[16,8]{0,1:T(8,128)S(1)}, s32[16,8]{0,1:T(8,128)}, u32[]{:S(2)}) copy-start(s32[16,8]{0,1:T(8,128)} %param.11) | copy-start | bytes 1540
  0.6 4.6 %copy-start.6 = (s32[16]{0:T(128)S(1)}, s32[16]{0:T(128)}, u32[]{:S(2)}) copy-start(s32[16]{0:T(128)} %param.10) | copy-start | bytes 196
  0.7 4.7 %copy-start.1 = (bf16[16,2,6144]{2,1,0:T(2,128)(2,1)S(1)}, bf16[16,2,6144]{2,1,0:T(2,128)(2,1)}, u32[]{:S(2)}) copy-start(bf16[16,2,6144]{2,1,0:T(2,128)(2,1)} %param.9) | copy-start | bytes 1179652
  0.7 5.4 %copy-start = (bf16[16,6144]{1,0:T(8,128)(2,1)S(1)}, bf16[16,6144]{1,0:T(8,128)(2,1)}, u32[]{:S(2)}) copy-start(bf16[16,6144]{1,0:T(8,128)(2,1)} %table_ref.1) | copy-start | bytes 589828
  0.7 7.4 %collective-permute-start.2 = (bf16[2,2,6144]{2,1,0:T(2,128)(2,1)}, bf16[2,2,6144]{2,1,0:T(2,128)(2,1)S(1)}, u32[]{:S(2)}, u32[]{:S(2)}) collective-permute-start(bf16[2,2,6144]{2,1,0:T(2,128)(2,1)} %param.12), channel_id=1, source_target_pairs={{6,0},{7,1},{4,2},{5,3},{2,4},{3,5},{0,6},{1,7},{14,8},{15,9},{12,... | collective-permute-start | bytes 147464 | tf_op jit(solution)/shard_map/ppermute | solution.py:379
  4.6 4.3 %collective-permute-start = (bf16[2,2,6144]{2,1,0:T(2,128)(2,1)}, bf16[2,2,6144]{2,1,0:T(2,128)(2,1)S(1)}, u32[]{:S(2)}, u32[]{:S(2)}) collective-permute-start(bf16[2,2,6144]{2,1,0:T(2,128)(2,1)} %param.12), channel_id=1, source_target_pairs={{4,0},{5,1},{6,2},{7,3},{0,4},{1,5},{2,6},{3,7},{12,8},{13,9},{14,... | collective-permute-start | bytes 147464 | tf_op jit(solution)/shard_map/ppermute | solution.py:379
  5.1 4.3 %collective-permute-start.1 = (bf16[2,2,6144]{2,1,0:T(2,128)(2,1)}, bf16[2,2,6144]{2,1,0:T(2,128)(2,1)S(1)}, u32[]{:S(2)}, u32[]{:S(2)}) collective-permute-start(bf16[2,2,6144]{2,1,0:T(2,128)(2,1)} %param.12), channel_id=1, source_target_pairs={{2,0},{3,1},{0,2},{1,3},{6,4},{7,5},{4,6},{5,7},{10,8},{11,9},{8,1... | collective-permute-start | bytes 147464 | tf_op jit(solution)/shard_map/ppermute | solution.py:379
  5.3 1.6 %collective-permute-start.4 = (s32[16,16]{1,0:T(8,128)S(1)}, s32[16,16]{1,0:T(8,128)S(1)}, u32[]{:S(2)}, u32[]{:S(2)}) collective-permute-start(s32[16,16]{1,0:T(8,128)S(1)} %shard_map.105.d_ref.refs_6_.i0_ref), channel_id=1, source_target_pairs={{0,1},{1,0},{2,3},{3,2},{4,5},{5,4},{6,7},{7,6},{8,9},{9,8},{10,11... | collective-permute-start | bytes 3080 | tf_op jit(solution)/shard_map/ppermute | solution.py:373
  5.4 1.8 %collective-permute-start.3 = (bf16[16,2,6144]{2,1,0:T(2,128)(2,1)S(1)}, bf16[16,2,6144]{2,1,0:T(2,128)(2,1)S(1)}, u32[]{:S(2)}, u32[]{:S(2)}) collective-permute-start(bf16[16,2,6144]{2,1,0:T(2,128)(2,1)S(1)} %copy-done.1), channel_id=1, source_target_pairs={{0,1},{1,0},{2,3},{3,2},{4,5},{5,4},{6,7},{7,6},{8,9},{9,8},{10,11... | collective-permute-start | bytes 1179656 | tf_op jit(solution)/shard_map/ppermute | solution.py:373
  6.8 2.6 %copy-start.2 = (bf16[2,2,6144]{2,1,0:T(2,128)(2,1)S(1)}, bf16[2,2,6144]{2,1,0:T(2,128)(2,1)}, u32[]{:S(2)}) copy-start(bf16[2,2,6144]{2,1,0:T(2,128)(2,1)} %param.12) | copy-start | bytes 147460
  6.8 2.6 %copy-start.3 = (f32[6144]{0:T(1024)S(1)}, f32[6144]{0:T(1024)}, u32[]{:S(2)}) copy-start(f32[6144]{0:T(1024)} %param.14) | copy-start | bytes 73732
  6.8 2.6 %copy-start.4 = (f32[8,128]{1,0:T(8,128)S(1)}, f32[8,128]{1,0:T(8,128)}, u32[]{:S(2)}) copy-start(f32[8,128]{1,0:T(8,128)} %constant.80.clone.refs_9_.trig_ref) | copy-start | bytes 12292
  8.0 2.8 %copy-start.7 = (s32[2,48]{1,0:T(2,128)S(1)}, s32[2,48]{1,0:T(2,128)}, u32[]{:S(2)}) copy-start(s32[2,48]{1,0:T(2,128)} %param.15) | copy-start | bytes 1156
  8.0 2.8 %copy-start.8 = (s32[4]{0:T(128)S(1)}, s32[4]{0:T(128)}, u32[]{:S(2)}) copy-start(s32[4]{0:T(128)} %param.16) | copy-start | bytes 52
  10.7 1.2 %collective-permute-start.6 = (f32[8,128]{1,0:T(8,128)S(1)}, f32[8,128]{1,0:T(8,128)S(1)}, u32[]{:S(2)}, u32[]{:S(2)}) collective-permute-start(f32[8,128]{1,0:T(8,128)S(1)} %get-tuple-element.21.stat_ref), channel_id=1, source_target_pairs={{0,1},{1,0},{2,3},{3,2},{4,5},{5,4},{6,7},{7,6},{8,9},{9,8},{10,11... | collective-permute-start | bytes 12296 | tf_op jit(solution)/shard_map/ppermute | solution.py:373
  12.7 4.8 %collective-permute-start.10 = (bf16[4,6272]{1,0:T(4,128)(2,1)S(1)}, bf16[4,6272]{1,0:T(4,128)(2,1)S(1)}, u32[]{:S(2)}, u32[]{:S(2)}) collective-permute-start(bf16[4,6272]{1,0:T(4,128)(2,1)S(1)} %get-tuple-element.25), channel_id=1, source_target_pairs={{0,7},{1,6},{2,5},{3,4},{4,3},{5,2},{6,1},{7,0},{8,15},{9,14},{10,... | collective-permute-start | bytes 150536 | tf_op jit(solution)/shard_map/ppermute | solution.py:382
  14.3 3.2 %collective-permute-start.7 = (bf16[4,6272]{1,0:T(4,128)(2,1)S(1)}, bf16[4,6272]{1,0:T(4,128)(2,1)S(1)}, u32[]{:S(2)}, u32[]{:S(2)}) collective-permute-start(bf16[4,6272]{1,0:T(4,128)(2,1)S(1)} %get-tuple-element.22), channel_id=1, source_target_pairs={{0,1},{1,0},{2,3},{3,2},{4,5},{5,4},{6,7},{7,6},{8,9},{9,8},{10,11... | collective-permute-start | bytes 150536 | tf_op jit(solution)/shard_map/ppermute | solution.py:373
  14.4 4.2 %collective-permute-start.8 = (bf16[4,6272]{1,0:T(4,128)(2,1)S(1)}, bf16[4,6272]{1,0:T(4,128)(2,1)S(1)}, u32[]{:S(2)}, u32[]{:S(2)}) collective-permute-start(bf16[4,6272]{1,0:T(4,128)(2,1)S(1)} %get-tuple-element.23), channel_id=1, source_target_pairs={{0,5},{1,4},{2,7},{3,6},{4,1},{5,0},{6,3},{7,2},{8,13},{9,12},{10,... | collective-permute-start | bytes 150536 | tf_op jit(solution)/shard_map/ppermute | solution.py:382
  14.9 3.8 %collective-permute-start.9 = (bf16[4,6272]{1,0:T(4,128)(2,1)S(1)}, bf16[4,6272]{1,0:T(4,128)(2,1)S(1)}, u32[]{:S(2)}, u32[]{:S(2)}) collective-permute-start(bf16[4,6272]{1,0:T(4,128)(2,1)S(1)} %get-tuple-element.24), channel_id=1, source_target_pairs={{0,3},{1,2},{2,1},{3,0},{4,7},{5,6},{6,5},{7,4},{8,11},{9,10},{10,... | collective-permute-start | bytes 150536 | tf_op jit(solution)/shard_map/ppermute | solution.py:382
  16.2 1.1 %collective-permute-start.5 = (s32[2,48]{1,0:T(2,128)S(1)}, s32[2,48]{1,0:T(2,128)S(1)}, u32[]{:S(2)}, u32[]{:S(2)}) collective-permute-start(s32[2,48]{1,0:T(2,128)S(1)} %fusion.2.slot_ref), channel_id=1, source_target_pairs={{0,1},{1,0},{2,3},{3,2},{4,5},{5,4},{6,7},{7,6},{8,9},{9,8},{10,11... | collective-permute-start | bytes 1160 | tf_op jit(solution)/shard_map/ppermute | solution.py:373
  18.9 5.4 %collective-permute-start.11 = (bf16[104,128]{1,0:T(8,128)(2,1)S(1)}, bf16[104,128]{1,0:T(8,128)(2,1)S(1)}, u32[]{:S(2)}, u32[]{:S(2)}) collective-permute-start(bf16[104,128]{1,0:T(8,128)(2,1)S(1)} %get-tuple-element.26), channel_id=1, source_target_pairs={{0,1},{1,0},{2,3},{3,2},{4,5},{5,4},{6,7},{7,6},{8,9},{9,8},{10,11... | collective-permute-start | bytes 79880 | tf_op jit(solution)/shard_map/ppermute | solution.py:373
  19.1 5.3 %collective-permute-start.12 = (bf16[104,128]{1,0:T(8,128)(2,1)S(1)}, bf16[104,128]{1,0:T(8,128)(2,1)S(1)}, u32[]{:S(2)}, u32[]{:S(2)}) collective-permute-start(bf16[104,128]{1,0:T(8,128)(2,1)S(1)} %get-tuple-element.27), channel_id=1, source_target_pairs={{0,17},{1,16},{2,19},{3,18},{4,21},{5,20},{6,23},{7,22},{8,25},{9,... | collective-permute-start | bytes 79880 | tf_op jit(solution)/shard_map/ppermute | solution.py:385
  21.7 4.2 %collective-permute-start.13 = (bf16[104,128]{1,0:T(8,128)(2,1)S(1)}, bf16[104,128]{1,0:T(8,128)(2,1)S(1)}, u32[]{:S(2)}, u32[]{:S(2)}) collective-permute-start(bf16[104,128]{1,0:T(8,128)(2,1)S(1)} %get-tuple-element.28), channel_id=1, source_target_pairs={{0,25},{1,24},{2,27},{3,26},{4,29},{5,28},{6,31},{7,30},{8,17},{9,... | collective-permute-start | bytes 79880 | tf_op jit(solution)/shard_map/ppermute | solution.py:385
  22.7 3.9 %collective-permute-start.14 = (bf16[104,128]{1,0:T(8,128)(2,1)S(1)}, bf16[104,128]{1,0:T(8,128)(2,1)S(1)}, u32[]{:S(2)}, u32[]{:S(2)}) collective-permute-start(bf16[104,128]{1,0:T(8,128)(2,1)S(1)} %get-tuple-element.29), channel_id=1, source_target_pairs={{0,9},{1,8},{2,11},{3,10},{4,13},{5,12},{6,15},{7,14},{8,1},{9,0},... | collective-permute-start | bytes 79880 | tf_op jit(solution)/shard_map/ppermute | solution.py:385

commit v7 on v6

--- a/solution.py
+++ b/solution.py
@@ -29,7 +29,7 @@
 
 
 CHIP_ROUTES = [[[2, 3, 0, 1], [1, 0, 3, 2], [3, 2, 1, 0]], [[2, 3, 0, 1], [1, 0, 3, 2], [3, 2, 1, 0]]]
-GROUP_ROUTES = [[[2, 3, 1, 0], [3, 2, 0, 1], [1, 0, 3, 2]], [[2, 3, 1, 0], [3, 2, 0, 1], [1, 0, 3, 2]]]
+GROUP_ROUTES = [[[1, 2, 3, 0], [2, 3, 0, 1], [3, 0, 1, 2]], [[1, 2, 3, 0], [2, 3, 0, 1], [3, 0, 1, 2]]]
 
 
 def routes(count, chosen):

time: 27.6 us -> 27.2 us (0.986)
  waiting for transfers between devices: 7.13 us -> 5.45 us
  starting transfers between devices: 12.9 us -> 14.2 us
    ppermute x3, waiting for transfers between devices: 2.28 us -> 0.6 us  [to_group(): lax.ppermute(x, ('grp', 'dev'), [(g * members + i, group_routes[i % 2][r...]
    ppermute x3, starting transfers between devices: 3.88 us -> 5.23 us  [to_group(): lax.ppermute(x, ('grp', 'dev'), [(g * members + i, group_routes[i % 2][r...]
  transfers between devices with their start and end apart: 15 -> 15, of which waited for: 10 -> 9; matrix products, arithmetic and copies ran while one was open for 2% -> 2% of each run, Pallas kernels for 11% -> 11%
where the time goes in v7:
time: 27.2 us; the launch traced here: 27 us
  starting transfers between devices  14.2 us (52%)
  Pallas kernels  5.95 us (22%)
  waiting for transfers between devices  5.45 us (20%)
  between operations  0.95 us (3%)
  other arithmetic  0.44 us (2%)
    ppermute x3, starting transfers between devices, to_group(): lax.ppermute(x, ('grp', 'dev'), [(g * members + i, group_routes[i % 2][r...  5.23 us
    ppermute x3, starting transfers between devices, from_place(): return lax.ppermute(x, 'dev', [(j, i) for i, j in chip_pairs(t)])  4.6 us
    ppermute x3, starting transfers between devices, to_place(): return lax.ppermute(x, 'dev', [(i, j ^ 1) for i, j in chip_pairs(t)])  3.22 us
    ppermute x6, waiting for transfers between devices, swap(): return lax.ppermute(x, 'dev', [(i, i ^ 1) for i in range(members)])  2.1 us
    ppermute x3, waiting for transfers between devices, to_place(): return lax.ppermute(x, 'dev', [(i, j ^ 1) for i, j in chip_pairs(t)])  1.38 us
    ppermute x3, waiting for transfers between devices, from_place(): return lax.ppermute(x, 'dev', [(j, i) for i, j in chip_pairs(t)])  1.37 us
    pallas_call x1, Pallas kernels, body(): call(functools.partial(table_kernel, lines, cap), jax.ShapeDtypeStruct((2...  1.29 us
    pallas_call x1, Pallas kernels, body(): call(functools.partial(score_kernel, chunks), (jax.ShapeDtypeStruct((18 *...  1.26 us
  transfers between devices with their start and end apart: 15, of which 9 were waited for; matrix products, arithmetic and copies ran while one was open for 2% of the time, Pallas kernels for 11%

profile of v7, /device:TPU:0, one launch (start us, length us, event | category | flops | bytes accessed | tf_op | source)
XLA Modules:
  0.0 27.0 jit_solution(8630636930437472629)
XLA Ops:
  0.6 0.0 copy-start.5
  0.6 0.0 copy-start.6
  0.7 0.0 copy-start.1
  0.7 0.0 copy-start
  0.7 4.0 %collective-permute-start.2 = (bf16[2,2,6144]{2,1,0:T(2,128)(2,1)}, bf16[2,2,6144]{2,1,0:T(2,128)(2,1)S(1)}, u32[]{:S(2)}, u32[]{:S(2)}) collective-permute-start(bf16[2,2,6144]{2,1,0:T(2,128)(2,1)} %param.12), channel_id=1, source_target_pairs={{6,0},{7,1},{4,2},{5,3},{2,4},{3,5},{0,6},{1,7},{14,8},{15,9},{12,... | collective-permute-start | bytes 147464 | tf_op jit(solution)/shard_map/ppermute | solution.py:379
  4.6 0.5 %collective-permute-start = (bf16[2,2,6144]{2,1,0:T(2,128)(2,1)}, bf16[2,2,6144]{2,1,0:T(2,128)(2,1)S(1)}, u32[]{:S(2)}, u32[]{:S(2)}) collective-permute-start(bf16[2,2,6144]{2,1,0:T(2,128)(2,1)} %param.12), channel_id=1, source_target_pairs={{4,0},{5,1},{6,2},{7,3},{0,4},{1,5},{2,6},{3,7},{12,8},{13,9},{14,... | collective-permute-start | bytes 147464 | tf_op jit(solution)/shard_map/ppermute | solution.py:379
  5.1 0.1 collective-permute-start.1
  5.3 0.0 copy-done.5
  5.3 0.0 copy-done.6
  5.3 0.1 collective-permute-start.4
  5.4 0.0 copy-done.1
  5.4 0.5 %collective-permute-start.3 = (bf16[16,2,6144]{2,1,0:T(2,128)(2,1)S(1)}, bf16[16,2,6144]{2,1,0:T(2,128)(2,1)S(1)}, u32[]{:S(2)}, u32[]{:S(2)}) collective-permute-start(bf16[16,2,6144]{2,1,0:T(2,128)(2,1)S(1)} %copy-done.1), channel_id=1, source_target_pairs={{0,1},{1,0},{2,3},{3,2},{4,5},{5,4},{6,7},{7,6},{8,9},{9,8},{10,11... | collective-permute-start | bytes 1179656 | tf_op jit(solution)/shard_map/ppermute | solution.py:373
  6.0 0.1 select_add_fusion.refs_10_
  6.1 0.0 copy-done
  6.1 0.7 %shard_map.106.own_ref = bf16[96,6144]{1,0:T(8,128)(2,1)S(1)} custom-call(bf16[1536,128]{1,0:T(8,128)(2,1)S(1)} %bitcast.33, bf16[16,6144]{1,0:T(8,128)(2,1)S(1)} %copy-done, s32[16,16]{1,0:T(8,128)S(1)} %shard_map.105.d_ref.refs_6_.i0_ref), custom_call_target="tpu_custom_call" | custom-call | flops 1966080 | bytes 3145728 | tf_op jit(solution)/shard_map/pallas_call | solution.py:419
  6.8 0.0 copy-start.2
  6.8 0.0 copy-start.3
  6.8 0.0 copy-start.4
  6.9 0.0 collective-permute-done.4.d_ref.refs_7_.i1_ref
  6.9 0.3 %collective-permute-done.3 = bf16[16,2,6144]{2,1,0:T(2,128)(2,1)S(1)} collective-permute-done((bf16[16,2,6144]{2,1,0:T(2,128)(2,1)S(1)}, bf16[16,2,6144]{2,1,0:T(2,128)(2,1)S(1)}, u32[]{:S(2)}, u32[]{:S(2)}) %collective-permute-start.3) | collective-permute-done | bytes 393248 | tf_op jit(solution)/shard_map/ppermute | solution.py:373
  7.2 0.8 %shard_map.107.refs_4_.y_ref = bf16[192,6144]{1,0:T(8,128)(2,1)S(1)} custom-call(bf16[1536,128]{1,0:T(8,128)(2,1)S(1)} %bitcast.34, bf16[16,6144]{1,0:T(8,128)(2,1)S(1)} %copy-done, s32[16,16]{1,0:T(8,128)S(1)} %collective-permute-done.4.d_ref.refs_7_.i1_ref, bf16[96,6144]{1,0:T(8,128)(2,1)S(1)} %shard_map.106.own_ref), custom_call_target="tpu_custom_call" | custom-call | flops 1966080 | bytes 3145728 | tf_op jit(solution)/shard_map/pallas_call | solution.py:426
  8.0 0.0 copy-start.7
  8.0 0.0 copy-start.8
  8.1 0.0 collective-permute-done.2
  8.1 0.9 %collective-permute-done = bf16[2,2,6144]{2,1,0:T(2,128)(2,1)S(1)} collective-permute-done((bf16[2,2,6144]{2,1,0:T(2,128)(2,1)}, bf16[2,2,6144]{2,1,0:T(2,128)(2,1)S(1)}, u32[]{:S(2)}, u32[]{:S(2)}) %collective-permute-start) | collective-permute-done | bytes 49184 | tf_op jit(solution)/shard_map/ppermute | solution.py:379
  8.9 0.5 %collective-permute-done.1 = bf16[2,2,6144]{2,1,0:T(2,128)(2,1)S(1)} collective-permute-done((bf16[2,2,6144]{2,1,0:T(2,128)(2,1)}, bf16[2,2,6144]{2,1,0:T(2,128)(2,1)S(1)}, u32[]{:S(2)}, u32[]{:S(2)}) %collective-permute-start.1) | collective-permute-done | bytes 49184 | tf_op jit(solution)/shard_map/ppermute | solution.py:379
  9.4 0.0 copy-done.2
  9.4 0.0 copy-done.3
  9.4 0.0 copy-done.4
  9.4 1.3 %shard_map.108 = (f32[72,128]{1,0:T(8,128)S(1)}, f32[8,128]{1,0:T(8,128)S(1)}) custom-call(bf16[192,128]{1,0:T(8,128)(2,1)S(1)} %bitcast.35, bf16[192,128]{1,0:T(8,128)(2,1)S(1)} %bitcast.37, bf16[192,128]{1,0:T(8,128)(2,1)S(1)} %bitcast.38, bf16[192,128]{1,0:T(8,128)(2,1)S(1)} %bitcast.36, bf16[192,6144]{1,0:T(8,128)(2,1)S(1)} %shard_map.107.refs_4_.y_ref, ...), custom_call_target="tpu_custom_call" | custom-call | flops 113246208 | bytes 2949120 | tf_op jit(solution)/shard_map/pallas_call | solution.py:439
  10.7 0.1 collective-permute-start.6
  10.8 0.0 copy-done.7
  10.8 0.0 copy-done.8
  10.8 0.1 select_reduce_fusion
  10.9 0.2 convert_reduce_fusion
  11.1 0.1 shard_map.109
  11.2 0.8 %collective-permute-done.6.other_ref = f32[8,128]{1,0:T(8,128)S(1)} collective-permute-done((f32[8,128]{1,0:T(8,128)S(1)}, f32[8,128]{1,0:T(8,128)S(1)}, u32[]{:S(2)}, u32[]{:S(2)}) %collective-permute-start.6) | collective-permute-done | bytes 4128 | tf_op jit(solution)/shard_map/ppermute | solution.py:373
  11.9 0.8 %shard_map.110 = (bf16[4,6272]{1,0:T(4,128)(2,1)S(1)}, bf16[4,6272]{1,0:T(4,128)(2,1)S(1)}, bf16[4,6272]{1,0:T(4,128)(2,1)S(1)}, bf16[4,6272]{1,0:T(4,128)(2,1)S(1)}) custom-call(bf16[192,6144]{1,0:T(8,128)(2,1)S(1)} %shard_map.107.refs_4_.y_ref, f32[48,256]{1,0:T(8,128)S(1)} %get-tuple-element.19.m_ref, f32[8,128]{1,0:T(8,128)S(1)} %get-tuple-element.20.s_ref, ...), custom_call_target="tpu_custom_call" | custom-call | flops 113246208 | bytes 2949120 | tf_op jit(solution)/shard_map/pallas_call | solution.py:464
  12.7 1.6 %collective-permute-start.10 = (bf16[4,6272]{1,0:T(4,128)(2,1)S(1)}, bf16[4,6272]{1,0:T(4,128)(2,1)S(1)}, u32[]{:S(2)}, u32[]{:S(2)}) collective-permute-start(bf16[4,6272]{1,0:T(4,128)(2,1)S(1)} %get-tuple-element.25), channel_id=1, source_target_pairs={{0,7},{1,6},{2,5},{3,4},{4,3},{5,2},{6,1},{7,0},{8,15},{9,14},{10,... | collective-permute-start | bytes 150536 | tf_op jit(solution)/shard_map/ppermute | solution.py:382
  14.3 0.2 collective-permute-start.7
  14.4 0.5 %collective-permute-start.8 = (bf16[4,6272]{1,0:T(4,128)(2,1)S(1)}, bf16[4,6272]{1,0:T(4,128)(2,1)S(1)}, u32[]{:S(2)}, u32[]{:S(2)}) collective-permute-start(bf16[4,6272]{1,0:T(4,128)(2,1)S(1)} %get-tuple-element.23), channel_id=1, source_target_pairs={{0,5},{1,4},{2,7},{3,6},{4,1},{5,0},{6,3},{7,2},{8,13},{9,12},{10,... | collective-permute-start | bytes 150536 | tf_op jit(solution)/shard_map/ppermute | solution.py:382
  14.9 1.2 %collective-permute-start.9 = (bf16[4,6272]{1,0:T(4,128)(2,1)S(1)}, bf16[4,6272]{1,0:T(4,128)(2,1)S(1)}, u32[]{:S(2)}, u32[]{:S(2)}) collective-permute-start(bf16[4,6272]{1,0:T(4,128)(2,1)S(1)} %get-tuple-element.24), channel_id=1, source_target_pairs={{0,3},{1,2},{2,1},{3,0},{4,7},{5,6},{6,5},{7,4},{8,11},{9,10},{10,... | collective-permute-start | bytes 150536 | tf_op jit(solution)/shard_map/ppermute | solution.py:382
  16.1 0.1 fusion.2.slot_ref
  16.2 0.2 collective-permute-start.5
  16.3 1.0 %collective-permute-done.5.slot_ref = s32[2,48]{1,0:T(2,128)S(1)} collective-permute-done((s32[2,48]{1,0:T(2,128)S(1)}, s32[2,48]{1,0:T(2,128)S(1)}, u32[]{:S(2)}, u32[]{:S(2)}) %collective-permute-start.5) | collective-permute-done | bytes 416 | tf_op jit(solution)/shard_map/ppermute | solution.py:373
  17.3 0.2 collective-permute-done.10.refs_2_
  17.5 0.0 collective-permute-done.7.own_ref
  17.5 1.1 %collective-permute-done.8.refs_0_ = bf16[4,6272]{1,0:T(4,128)(2,1)S(1)} collective-permute-done((bf16[4,6272]{1,0:T(4,128)(2,1)S(1)}, bf16[4,6272]{1,0:T(4,128)(2,1)S(1)}, u32[]{:S(2)}, u32[]{:S(2)}) %collective-permute-start.8) | collective-permute-done | bytes 50208 | tf_op jit(solution)/shard_map/ppermute | solution.py:382
  18.6 0.1 collective-permute-done.9.refs_1_
  18.7 0.3 shard_map.111
  18.9 0.2 collective-permute-start.11
  19.1 1.6 %collective-permute-start.12 = (bf16[104,128]{1,0:T(8,128)(2,1)S(1)}, bf16[104,128]{1,0:T(8,128)(2,1)S(1)}, u32[]{:S(2)}, u32[]{:S(2)}) collective-permute-start(bf16[104,128]{1,0:T(8,128)(2,1)S(1)} %get-tuple-element.27), channel_id=1, source_target_pairs={{0,9},{1,8},{2,11},{3,10},{4,13},{5,12},{6,15},{7,14},{8,17},{9,16... | collective-permute-start | bytes 79880 | tf_op jit(solution)/shard_map/ppermute | solution.py:385
  20.7 2.3 %collective-permute-start.13 = (bf16[104,128]{1,0:T(8,128)(2,1)S(1)}, bf16[104,128]{1,0:T(8,128)(2,1)S(1)}, u32[]{:S(2)}, u32[]{:S(2)}) collective-permute-start(bf16[104,128]{1,0:T(8,128)(2,1)S(1)} %get-tuple-element.28), channel_id=1, source_target_pairs={{0,17},{1,16},{2,19},{3,18},{4,21},{5,20},{6,23},{7,22},{8,25},{9,... | collective-permute-start | bytes 79880 | tf_op jit(solution)/shard_map/ppermute | solution.py:385
  23.0 1.3 %collective-permute-start.14 = (bf16[104,128]{1,0:T(8,128)(2,1)S(1)}, bf16[104,128]{1,0:T(8,128)(2,1)S(1)}, u32[]{:S(2)}, u32[]{:S(2)}) collective-permute-start(bf16[104,128]{1,0:T(8,128)(2,1)S(1)} %get-tuple-element.29), channel_id=1, source_target_pairs={{0,25},{1,24},{2,27},{3,26},{4,29},{5,28},{6,31},{7,30},{8,1},{9,0... | collective-permute-start | bytes 79880 | tf_op jit(solution)/shard_map/ppermute | solution.py:385
  24.4 1.3 %shard_map.112.refs_3_ = f32[2,384,128]{2,1,0:T(8,128)S(1)} custom-call(s32[2,48]{1,0:T(2,128)S(1)} %fusion.2.slot_ref, bf16[16,6144]{1,0:T(8,128)(2,1)S(1)} %copy-done), custom_call_target="tpu_custom_call" | custom-call | flops 98304 | bytes 393216 | tf_op jit(solution)/shard_map/pallas_call | solution.py:486
  25.7 0.0 collective-permute-done.11.own_ref
  25.7 0.0 collective-permute-done.12.refs_0_
  25.7 0.0 collective-permute-done.13.refs_1_
  25.7 0.6 %collective-permute-done.14.refs_2_ = bf16[104,128]{1,0:T(8,128)(2,1)S(1)} collective-permute-done((bf16[104,128]{1,0:T(8,128)(2,1)S(1)}, bf16[104,128]{1,0:T(8,128)(2,1)S(1)}, u32[]{:S(2)}, u32[]{:S(2)}) %collective-permute-start.14) | collective-permute-done | bytes 26656 | tf_op jit(solution)/shard_map/ppermute | solution.py:385
  26.3 0.8 %shard_map.113 = (f32[1,2,2,24,128]{4,3,2,1,0:T(8,128)}, f32[1,2,24,128]{3,2,1,0:T(8,128)}) custom-call(bf16[104,128]{1,0:T(8,128)(2,1)S(1)} %collective-permute-done.11.own_ref, bf16[104,128]{1,0:T(8,128)(2,1)S(1)} %collective-permute-done.12.refs_0_, bf16[104,128]{1,0:T(8,128)(2,1)S(1)} %collective-permute-done.13.refs_1_, ...), custom_call_target="tpu_custom_call" | custom-call | flops 1000 | bytes 98304 | tf_op jit(solution)/shard_map/pallas_call | solution.py:505
  (7 shorter events, 0.0 us)
Async XLA Ops:
  0.6 4.6 %copy-start.5 = (s32[16,8]{0,1:T(8,128)S(1)}, s32[16,8]{0,1:T(8,128)}, u32[]{:S(2)}) copy-start(s32[16,8]{0,1:T(8,128)} %param.11) | copy-start | bytes 1540
  0.6 4.6 %copy-start.6 = (s32[16]{0:T(128)S(1)}, s32[16]{0:T(128)}, u32[]{:S(2)}) copy-start(s32[16]{0:T(128)} %param.10) | copy-start | bytes 196
  0.7 4.7 %copy-start.1 = (bf16[16,2,6144]{2,1,0:T(2,128)(2,1)S(1)}, bf16[16,2,6144]{2,1,0:T(2,128)(2,1)}, u32[]{:S(2)}) copy-start(bf16[16,2,6144]{2,1,0:T(2,128)(2,1)} %param.9) | copy-start | bytes 1179652
  0.7 5.4 %copy-start = (bf16[16,6144]{1,0:T(8,128)(2,1)S(1)}, bf16[16,6144]{1,0:T(8,128)(2,1)}, u32[]{:S(2)}) copy-start(bf16[16,6144]{1,0:T(8,128)(2,1)} %table_ref.1) | copy-start | bytes 589828
  0.7 7.4 %collective-permute-start.2 = (bf16[2,2,6144]{2,1,0:T(2,128)(2,1)}, bf16[2,2,6144]{2,1,0:T(2,128)(2,1)S(1)}, u32[]{:S(2)}, u32[]{:S(2)}) collective-permute-start(bf16[2,2,6144]{2,1,0:T(2,128)(2,1)} %param.12), channel_id=1, source_target_pairs={{6,0},{7,1},{4,2},{5,3},{2,4},{3,5},{0,6},{1,7},{14,8},{15,9},{12,... | collective-permute-start | bytes 147464 | tf_op jit(solution)/shard_map/ppermute | solution.py:379
  4.6 4.3 %collective-permute-start = (bf16[2,2,6144]{2,1,0:T(2,128)(2,1)}, bf16[2,2,6144]{2,1,0:T(2,128)(2,1)S(1)}, u32[]{:S(2)}, u32[]{:S(2)}) collective-permute-start(bf16[2,2,6144]{2,1,0:T(2,128)(2,1)} %param.12), channel_id=1, source_target_pairs={{4,0},{5,1},{6,2},{7,3},{0,4},{1,5},{2,6},{3,7},{12,8},{13,9},{14,... | collective-permute-start | bytes 147464 | tf_op jit(solution)/shard_map/ppermute | solution.py:379
  5.1 4.3 %collective-permute-start.1 = (bf16[2,2,6144]{2,1,0:T(2,128)(2,1)}, bf16[2,2,6144]{2,1,0:T(2,128)(2,1)S(1)}, u32[]{:S(2)}, u32[]{:S(2)}) collective-permute-start(bf16[2,2,6144]{2,1,0:T(2,128)(2,1)} %param.12), channel_id=1, source_target_pairs={{2,0},{3,1},{0,2},{1,3},{6,4},{7,5},{4,6},{5,7},{10,8},{11,9},{8,1... | collective-permute-start | bytes 147464 | tf_op jit(solution)/shard_map/ppermute | solution.py:379
  5.3 1.6 %collective-permute-start.4 = (s32[16,16]{1,0:T(8,128)S(1)}, s32[16,16]{1,0:T(8,128)S(1)}, u32[]{:S(2)}, u32[]{:S(2)}) collective-permute-start(s32[16,16]{1,0:T(8,128)S(1)} %shard_map.105.d_ref.refs_6_.i0_ref), channel_id=1, source_target_pairs={{0,1},{1,0},{2,3},{3,2},{4,5},{5,4},{6,7},{7,6},{8,9},{9,8},{10,11... | collective-permute-start | bytes 3080 | tf_op jit(solution)/shard_map/ppermute | solution.py:373
  5.4 1.8 %collective-permute-start.3 = (bf16[16,2,6144]{2,1,0:T(2,128)(2,1)S(1)}, bf16[16,2,6144]{2,1,0:T(2,128)(2,1)S(1)}, u32[]{:S(2)}, u32[]{:S(2)}) collective-permute-start(bf16[16,2,6144]{2,1,0:T(2,128)(2,1)S(1)} %copy-done.1), channel_id=1, source_target_pairs={{0,1},{1,0},{2,3},{3,2},{4,5},{5,4},{6,7},{7,6},{8,9},{9,8},{10,11... | collective-permute-start | bytes 1179656 | tf_op jit(solution)/shard_map/ppermute | solution.py:373
  6.8 2.6 %copy-start.2 = (bf16[2,2,6144]{2,1,0:T(2,128)(2,1)S(1)}, bf16[2,2,6144]{2,1,0:T(2,128)(2,1)}, u32[]{:S(2)}) copy-start(bf16[2,2,6144]{2,1,0:T(2,128)(2,1)} %param.12) | copy-start | bytes 147460
  6.8 2.6 %copy-start.3 = (f32[6144]{0:T(1024)S(1)}, f32[6144]{0:T(1024)}, u32[]{:S(2)}) copy-start(f32[6144]{0:T(1024)} %param.14) | copy-start | bytes 73732
  6.8 2.6 %copy-start.4 = (f32[8,128]{1,0:T(8,128)S(1)}, f32[8,128]{1,0:T(8,128)}, u32[]{:S(2)}) copy-start(f32[8,128]{1,0:T(8,128)} %constant.80.clone.refs_9_.trig_ref) | copy-start | bytes 12292
  8.0 2.8 %copy-start.7 = (s32[2,48]{1,0:T(2,128)S(1)}, s32[2,48]{1,0:T(2,128)}, u32[]{:S(2)}) copy-start(s32[2,48]{1,0:T(2,128)} %param.15) | copy-start | bytes 1156
  8.0 2.8 %copy-start.8 = (s32[4]{0:T(128)S(1)}, s32[4]{0:T(128)}, u32[]{:S(2)}) copy-start(s32[4]{0:T(128)} %param.16) | copy-start | bytes 52
  10.7 1.2 %collective-permute-start.6 = (f32[8,128]{1,0:T(8,128)S(1)}, f32[8,128]{1,0:T(8,128)S(1)}, u32[]{:S(2)}, u32[]{:S(2)}) collective-permute-start(f32[8,128]{1,0:T(8,128)S(1)} %get-tuple-element.21.stat_ref), channel_id=1, source_target_pairs={{0,1},{1,0},{2,3},{3,2},{4,5},{5,4},{6,7},{7,6},{8,9},{9,8},{10,11... | collective-permute-start | bytes 12296 | tf_op jit(solution)/shard_map/ppermute | solution.py:373
  12.7 4.8 %collective-permute-start.10 = (bf16[4,6272]{1,0:T(4,128)(2,1)S(1)}, bf16[4,6272]{1,0:T(4,128)(2,1)S(1)}, u32[]{:S(2)}, u32[]{:S(2)}) collective-permute-start(bf16[4,6272]{1,0:T(4,128)(2,1)S(1)} %get-tuple-element.25), channel_id=1, source_target_pairs={{0,7},{1,6},{2,5},{3,4},{4,3},{5,2},{6,1},{7,0},{8,15},{9,14},{10,... | collective-permute-start | bytes 150536 | tf_op jit(solution)/shard_map/ppermute | solution.py:382
  14.3 3.2 %collective-permute-start.7 = (bf16[4,6272]{1,0:T(4,128)(2,1)S(1)}, bf16[4,6272]{1,0:T(4,128)(2,1)S(1)}, u32[]{:S(2)}, u32[]{:S(2)}) collective-permute-start(bf16[4,6272]{1,0:T(4,128)(2,1)S(1)} %get-tuple-element.22), channel_id=1, source_target_pairs={{0,1},{1,0},{2,3},{3,2},{4,5},{5,4},{6,7},{7,6},{8,9},{9,8},{10,11... | collective-permute-start | bytes 150536 | tf_op jit(solution)/shard_map/ppermute | solution.py:373
  14.4 4.2 %collective-permute-start.8 = (bf16[4,6272]{1,0:T(4,128)(2,1)S(1)}, bf16[4,6272]{1,0:T(4,128)(2,1)S(1)}, u32[]{:S(2)}, u32[]{:S(2)}) collective-permute-start(bf16[4,6272]{1,0:T(4,128)(2,1)S(1)} %get-tuple-element.23), channel_id=1, source_target_pairs={{0,5},{1,4},{2,7},{3,6},{4,1},{5,0},{6,3},{7,2},{8,13},{9,12},{10,... | collective-permute-start | bytes 150536 | tf_op jit(solution)/shard_map/ppermute | solution.py:382
  14.9 3.8 %collective-permute-start.9 = (bf16[4,6272]{1,0:T(4,128)(2,1)S(1)}, bf16[4,6272]{1,0:T(4,128)(2,1)S(1)}, u32[]{:S(2)}, u32[]{:S(2)}) collective-permute-start(bf16[4,6272]{1,0:T(4,128)(2,1)S(1)} %get-tuple-element.24), channel_id=1, source_target_pairs={{0,3},{1,2},{2,1},{3,0},{4,7},{5,6},{6,5},{7,4},{8,11},{9,10},{10,... | collective-permute-start | bytes 150536 | tf_op jit(solution)/shard_map/ppermute | solution.py:382
  16.2 1.1 %collective-permute-start.5 = (s32[2,48]{1,0:T(2,128)S(1)}, s32[2,48]{1,0:T(2,128)S(1)}, u32[]{:S(2)}, u32[]{:S(2)}) collective-permute-start(s32[2,48]{1,0:T(2,128)S(1)} %fusion.2.slot_ref), channel_id=1, source_target_pairs={{0,1},{1,0},{2,3},{3,2},{4,5},{5,4},{6,7},{7,6},{8,9},{9,8},{10,11... | collective-permute-start | bytes 1160 | tf_op jit(solution)/shard_map/ppermute | solution.py:373
  18.9 6.7 %collective-permute-start.11 = (bf16[104,128]{1,0:T(8,128)(2,1)S(1)}, bf16[104,128]{1,0:T(8,128)(2,1)S(1)}, u32[]{:S(2)}, u32[]{:S(2)}) collective-permute-start(bf16[104,128]{1,0:T(8,128)(2,1)S(1)} %get-tuple-element.26), channel_id=1, source_target_pairs={{0,1},{1,0},{2,3},{3,2},{4,5},{5,4},{6,7},{7,6},{8,9},{9,8},{10,11... | collective-permute-start | bytes 79880 | tf_op jit(solution)/shard_map/ppermute | solution.py:373
  19.1 6.5 %collective-permute-start.12 = (bf16[104,128]{1,0:T(8,128)(2,1)S(1)}, bf16[104,128]{1,0:T(8,128)(2,1)S(1)}, u32[]{:S(2)}, u32[]{:S(2)}) collective-permute-start(bf16[104,128]{1,0:T(8,128)(2,1)S(1)} %get-tuple-element.27), channel_id=1, source_target_pairs={{0,9},{1,8},{2,11},{3,10},{4,13},{5,12},{6,15},{7,14},{8,17},{9,16... | collective-permute-start | bytes 79880 | tf_op jit(solution)/shard_map/ppermute | solution.py:385
  20.7 5.0 %collective-permute-start.13 = (bf16[104,128]{1,0:T(8,128)(2,1)S(1)}, bf16[104,128]{1,0:T(8,128)(2,1)S(1)}, u32[]{:S(2)}, u32[]{:S(2)}) collective-permute-start(bf16[104,128]{1,0:T(8,128)(2,1)S(1)} %get-tuple-element.28), channel_id=1, source_target_pairs={{0,17},{1,16},{2,19},{3,18},{4,21},{5,20},{6,23},{7,22},{8,25},{9,... | collective-permute-start | bytes 79880 | tf_op jit(solution)/shard_map/ppermute | solution.py:385
  23.0 3.3 %collective-permute-start.14 = (bf16[104,128]{1,0:T(8,128)(2,1)S(1)}, bf16[104,128]{1,0:T(8,128)(2,1)S(1)}, u32[]{:S(2)}, u32[]{:S(2)}) collective-permute-start(bf16[104,128]{1,0:T(8,128)(2,1)S(1)} %get-tuple-element.29), channel_id=1, source_target_pairs={{0,25},{1,24},{2,27},{3,26},{4,29},{5,28},{6,31},{7,30},{8,1},{9,0... | collective-permute-start | bytes 79880 | tf_op jit(solution)/shard_map/ppermute | solution.py:385

commit v8 on v7

--- a/solution.py
+++ b/solution.py
@@ -262,12 +262,9 @@
     grow = jnp.exp(peak0 - peak)
     scale = grow / (mass0 * grow + mass1 * jnp.exp(peak1 - peak))
     scale = jnp.where(lane < 2 * n, scale, 0.0)
+    onehot = onehot_of(i0_ref, i1_ref, LINE_LEN).astype(bf16)
     share = lax.dot_general(
-        s_ref[...] * scale,
-        onehot_of(i0_ref, i1_ref, LINE_LEN),
-        last_last,
-        precision=exact,
-        preferred_element_type=f32,
+        (s_ref[...] * scale).astype(bf16), onehot, last_last, preferred_element_type=f32
     )
     share = by_chunk(share, jnp.zeros_like(share))
     scales = scale

time: 27.2 us -> 27.2 us (level)
  transfers between devices with their start and end apart: 15 -> 15, of which waited for: 9 -> 8; matrix products, arithmetic and copies ran while one was open for 2% -> 2% of each run, Pallas kernels for 11% -> 11%
where the time goes in v8:
time: 27.2 us; the launch traced here: 27 us
  starting transfers between devices  14.3 us (53%)
  Pallas kernels  5.96 us (22%)
  waiting for transfers between devices  5.36 us (20%)
  between operations  0.94 us (3%)
  other arithmetic  0.44 us (2%)
    ppermute x3, starting transfers between devices, to_group(): lax.ppermute(x, ('grp', 'dev'), [(g * members + i, group_routes[i % 2][r...  5.26 us
    ppermute x3, starting transfers between devices, from_place(): return lax.ppermute(x, 'dev', [(j, i) for i, j in chip_pairs(t)])  4.6 us
    ppermute x3, starting transfers between devices, to_place(): return lax.ppermute(x, 'dev', [(i, j ^ 1) for i, j in chip_pairs(t)])  3.22 us
    ppermute x6, waiting for transfers between devices, swap(): return lax.ppermute(x, 'dev', [(i, i ^ 1) for i in range(members)])  2.1 us
    ppermute x3, waiting for transfers between devices, from_place(): return lax.ppermute(x, 'dev', [(j, i) for i, j in chip_pairs(t)])  1.37 us
    pallas_call x1, Pallas kernels, body(): call(functools.partial(table_kernel, lines, cap), jax.ShapeDtypeStruct((2...  1.34 us
    ppermute x3, waiting for transfers between devices, to_place(): return lax.ppermute(x, 'dev', [(i, j ^ 1) for i, j in chip_pairs(t)])  1.3 us
    pallas_call x1, Pallas kernels, body(): call(functools.partial(score_kernel, chunks), (jax.ShapeDtypeStruct((18 *...  1.26 us
  transfers between devices with their start and end apart: 15, of which 8 were waited for; matrix products, arithmetic and copies ran while one was open for 2% of the time, Pallas kernels for 11%

profile of v8, /device:TPU:0, one launch (start us, length us, event | category | flops | bytes accessed | tf_op | source)
XLA Modules:
  0.0 27.0 jit_solution(1971763929817037996)
XLA Ops:
  0.6 0.0 copy-start.5
  0.6 0.0 copy-start.6
  0.7 0.0 copy-start.1
  0.7 0.0 copy-start
  0.7 4.0 %collective-permute-start.2 = (bf16[2,2,6144]{2,1,0:T(2,128)(2,1)}, bf16[2,2,6144]{2,1,0:T(2,128)(2,1)S(1)}, u32[]{:S(2)}, u32[]{:S(2)}) collective-permute-start(bf16[2,2,6144]{2,1,0:T(2,128)(2,1)} %param.12), channel_id=1, source_target_pairs={{6,0},{7,1},{4,2},{5,3},{2,4},{3,5},{0,6},{1,7},{14,8},{15,9},{12,... | collective-permute-start | bytes 147464 | tf_op jit(solution)/shard_map/ppermute | solution.py:376
  4.6 0.5 %collective-permute-start = (bf16[2,2,6144]{2,1,0:T(2,128)(2,1)}, bf16[2,2,6144]{2,1,0:T(2,128)(2,1)S(1)}, u32[]{:S(2)}, u32[]{:S(2)}) collective-permute-start(bf16[2,2,6144]{2,1,0:T(2,128)(2,1)} %param.12), channel_id=1, source_target_pairs={{4,0},{5,1},{6,2},{7,3},{0,4},{1,5},{2,6},{3,7},{12,8},{13,9},{14,... | collective-permute-start | bytes 147464 | tf_op jit(solution)/shard_map/ppermute | solution.py:376
  5.1 0.1 collective-permute-start.1
  5.3 0.0 copy-done.5
  5.3 0.0 copy-done.6
  5.3 0.1 collective-permute-start.4
  5.4 0.0 copy-done.1
  5.4 0.5 %collective-permute-start.3 = (bf16[16,2,6144]{2,1,0:T(2,128)(2,1)S(1)}, bf16[16,2,6144]{2,1,0:T(2,128)(2,1)S(1)}, u32[]{:S(2)}, u32[]{:S(2)}) collective-permute-start(bf16[16,2,6144]{2,1,0:T(2,128)(2,1)S(1)} %copy-done.1), channel_id=1, source_target_pairs={{0,1},{1,0},{2,3},{3,2},{4,5},{5,4},{6,7},{7,6},{8,9},{9,8},{10,11... | collective-permute-start | bytes 1179656 | tf_op jit(solution)/shard_map/ppermute | solution.py:370
  6.0 0.1 select_add_fusion.refs_10_
  6.1 0.0 copy-done
  6.1 0.7 %shard_map.106.own_ref = bf16[96,6144]{1,0:T(8,128)(2,1)S(1)} custom-call(bf16[1536,128]{1,0:T(8,128)(2,1)S(1)} %bitcast.33, bf16[16,6144]{1,0:T(8,128)(2,1)S(1)} %copy-done, s32[16,16]{1,0:T(8,128)S(1)} %shard_map.105.d_ref.refs_6_.i0_ref), custom_call_target="tpu_custom_call" | custom-call | flops 1966080 | bytes 3145728 | tf_op jit(solution)/shard_map/pallas_call | solution.py:416
  6.8 0.0 copy-start.2
  6.8 0.0 copy-start.3
  6.8 0.0 copy-start.4
  6.9 0.0 collective-permute-done.4.d_ref.refs_7_.i1_ref
  6.9 0.3 %collective-permute-done.3 = bf16[16,2,6144]{2,1,0:T(2,128)(2,1)S(1)} collective-permute-done((bf16[16,2,6144]{2,1,0:T(2,128)(2,1)S(1)}, bf16[16,2,6144]{2,1,0:T(2,128)(2,1)S(1)}, u32[]{:S(2)}, u32[]{:S(2)}) %collective-permute-start.3) | collective-permute-done | bytes 393248 | tf_op jit(solution)/shard_map/ppermute | solution.py:370
  7.2 0.8 %shard_map.107.refs_4_.y_ref = bf16[192,6144]{1,0:T(8,128)(2,1)S(1)} custom-call(bf16[1536,128]{1,0:T(8,128)(2,1)S(1)} %bitcast.34, bf16[16,6144]{1,0:T(8,128)(2,1)S(1)} %copy-done, s32[16,16]{1,0:T(8,128)S(1)} %collective-permute-done.4.d_ref.refs_7_.i1_ref, bf16[96,6144]{1,0:T(8,128)(2,1)S(1)} %shard_map.106.own_ref), custom_call_target="tpu_custom_call" | custom-call | flops 1966080 | bytes 3145728 | tf_op jit(solution)/shard_map/pallas_call | solution.py:423
  8.0 0.0 copy-start.7
  8.0 0.0 copy-start.8
  8.1 0.0 collective-permute-done.2
  8.1 0.9 %collective-permute-done = bf16[2,2,6144]{2,1,0:T(2,128)(2,1)S(1)} collective-permute-done((bf16[2,2,6144]{2,1,0:T(2,128)(2,1)}, bf16[2,2,6144]{2,1,0:T(2,128)(2,1)S(1)}, u32[]{:S(2)}, u32[]{:S(2)}) %collective-permute-start) | collective-permute-done | bytes 49184 | tf_op jit(solution)/shard_map/ppermute | solution.py:376
  8.9 0.5 %collective-permute-done.1 = bf16[2,2,6144]{2,1,0:T(2,128)(2,1)S(1)} collective-permute-done((bf16[2,2,6144]{2,1,0:T(2,128)(2,1)}, bf16[2,2,6144]{2,1,0:T(2,128)(2,1)S(1)}, u32[]{:S(2)}, u32[]{:S(2)}) %collective-permute-start.1) | collective-permute-done | bytes 49184 | tf_op jit(solution)/shard_map/ppermute | solution.py:376
  9.4 0.0 copy-done.2
  9.4 0.0 copy-done.3
  9.4 0.0 copy-done.4
  9.4 1.3 %shard_map.108 = (f32[72,128]{1,0:T(8,128)S(1)}, f32[8,128]{1,0:T(8,128)S(1)}) custom-call(bf16[192,128]{1,0:T(8,128)(2,1)S(1)} %bitcast.35, bf16[192,128]{1,0:T(8,128)(2,1)S(1)} %bitcast.37, bf16[192,128]{1,0:T(8,128)(2,1)S(1)} %bitcast.38, bf16[192,128]{1,0:T(8,128)(2,1)S(1)} %bitcast.36, bf16[192,6144]{1,0:T(8,128)(2,1)S(1)} %shard_map.107.refs_4_.y_ref, ...), custom_call_target="tpu_custom_call" | custom-call | flops 113246208 | bytes 2949120 | tf_op jit(solution)/shard_map/pallas_call | solution.py:436
  10.7 0.1 collective-permute-start.6
  10.8 0.0 copy-done.7
  10.8 0.0 copy-done.8
  10.8 0.1 select_reduce_fusion
  10.9 0.2 convert_reduce_fusion
  11.1 0.1 shard_map.109
  11.2 0.8 %collective-permute-done.6.other_ref = f32[8,128]{1,0:T(8,128)S(1)} collective-permute-done((f32[8,128]{1,0:T(8,128)S(1)}, f32[8,128]{1,0:T(8,128)S(1)}, u32[]{:S(2)}, u32[]{:S(2)}) %collective-permute-start.6) | collective-permute-done | bytes 4128 | tf_op jit(solution)/shard_map/ppermute | solution.py:370
  11.9 0.7 %shard_map.110 = (bf16[4,6272]{1,0:T(4,128)(2,1)S(1)}, bf16[4,6272]{1,0:T(4,128)(2,1)S(1)}, bf16[4,6272]{1,0:T(4,128)(2,1)S(1)}, bf16[4,6272]{1,0:T(4,128)(2,1)S(1)}) custom-call(bf16[192,6144]{1,0:T(8,128)(2,1)S(1)} %shard_map.107.refs_4_.y_ref, f32[48,256]{1,0:T(8,128)S(1)} %get-tuple-element.19.m_ref, f32[8,128]{1,0:T(8,128)S(1)} %get-tuple-element.20.s_ref, ...), custom_call_target="tpu_custom_call" | custom-call | flops 113246208 | bytes 2949120 | tf_op jit(solution)/shard_map/pallas_call | solution.py:461
  12.7 1.6 %collective-permute-start.10 = (bf16[4,6272]{1,0:T(4,128)(2,1)S(1)}, bf16[4,6272]{1,0:T(4,128)(2,1)S(1)}, u32[]{:S(2)}, u32[]{:S(2)}) collective-permute-start(bf16[4,6272]{1,0:T(4,128)(2,1)S(1)} %get-tuple-element.25), channel_id=1, source_target_pairs={{0,7},{1,6},{2,5},{3,4},{4,3},{5,2},{6,1},{7,0},{8,15},{9,14},{10,... | collective-permute-start | bytes 150536 | tf_op jit(solution)/shard_map/ppermute | solution.py:379
  14.2 0.2 collective-permute-start.7
  14.4 0.5 %collective-permute-start.8 = (bf16[4,6272]{1,0:T(4,128)(2,1)S(1)}, bf16[4,6272]{1,0:T(4,128)(2,1)S(1)}, u32[]{:S(2)}, u32[]{:S(2)}) collective-permute-start(bf16[4,6272]{1,0:T(4,128)(2,1)S(1)} %get-tuple-element.23), channel_id=1, source_target_pairs={{0,5},{1,4},{2,7},{3,6},{4,1},{5,0},{6,3},{7,2},{8,13},{9,12},{10,... | collective-permute-start | bytes 150536 | tf_op jit(solution)/shard_map/ppermute | solution.py:379
  14.8 1.2 %collective-permute-start.9 = (bf16[4,6272]{1,0:T(4,128)(2,1)S(1)}, bf16[4,6272]{1,0:T(4,128)(2,1)S(1)}, u32[]{:S(2)}, u32[]{:S(2)}) collective-permute-start(bf16[4,6272]{1,0:T(4,128)(2,1)S(1)} %get-tuple-element.24), channel_id=1, source_target_pairs={{0,3},{1,2},{2,1},{3,0},{4,7},{5,6},{6,5},{7,4},{8,11},{9,10},{10,... | collective-permute-start | bytes 150536 | tf_op jit(solution)/shard_map/ppermute | solution.py:379
  16.0 0.1 fusion.2.slot_ref
  16.1 0.2 collective-permute-start.5
  16.3 1.0 %collective-permute-done.5.slot_ref = s32[2,48]{1,0:T(2,128)S(1)} collective-permute-done((s32[2,48]{1,0:T(2,128)S(1)}, s32[2,48]{1,0:T(2,128)S(1)}, u32[]{:S(2)}, u32[]{:S(2)}) %collective-permute-start.5) | collective-permute-done | bytes 416 | tf_op jit(solution)/shard_map/ppermute | solution.py:370
  17.3 0.2 collective-permute-done.10.refs_2_
  17.4 0.0 collective-permute-done.7.own_ref
  17.4 1.1 %collective-permute-done.8.refs_0_ = bf16[4,6272]{1,0:T(4,128)(2,1)S(1)} collective-permute-done((bf16[4,6272]{1,0:T(4,128)(2,1)S(1)}, bf16[4,6272]{1,0:T(4,128)(2,1)S(1)}, u32[]{:S(2)}, u32[]{:S(2)}) %collective-permute-start.8) | collective-permute-done | bytes 50208 | tf_op jit(solution)/shard_map/ppermute | solution.py:379
  18.5 0.0 collective-permute-done.9.refs_1_
  18.6 0.3 shard_map.111
  18.8 0.2 collective-permute-start.11
  19.0 1.5 %collective-permute-start.12 = (bf16[104,128]{1,0:T(8,128)(2,1)S(1)}, bf16[104,128]{1,0:T(8,128)(2,1)S(1)}, u32[]{:S(2)}, u32[]{:S(2)}) collective-permute-start(bf16[104,128]{1,0:T(8,128)(2,1)S(1)} %get-tuple-element.27), channel_id=1, source_target_pairs={{0,9},{1,8},{2,11},{3,10},{4,13},{5,12},{6,15},{7,14},{8,17},{9,16... | collective-permute-start | bytes 79880 | tf_op jit(solution)/shard_map/ppermute | solution.py:382
  20.6 2.4 %collective-permute-start.13 = (bf16[104,128]{1,0:T(8,128)(2,1)S(1)}, bf16[104,128]{1,0:T(8,128)(2,1)S(1)}, u32[]{:S(2)}, u32[]{:S(2)}) collective-permute-start(bf16[104,128]{1,0:T(8,128)(2,1)S(1)} %get-tuple-element.28), channel_id=1, source_target_pairs={{0,17},{1,16},{2,19},{3,18},{4,21},{5,20},{6,23},{7,22},{8,25},{9,... | collective-permute-start | bytes 79880 | tf_op jit(solution)/shard_map/ppermute | solution.py:382
  23.0 1.3 %collective-permute-start.14 = (bf16[104,128]{1,0:T(8,128)(2,1)S(1)}, bf16[104,128]{1,0:T(8,128)(2,1)S(1)}, u32[]{:S(2)}, u32[]{:S(2)}) collective-permute-start(bf16[104,128]{1,0:T(8,128)(2,1)S(1)} %get-tuple-element.29), channel_id=1, source_target_pairs={{0,25},{1,24},{2,27},{3,26},{4,29},{5,28},{6,31},{7,30},{8,1},{9,0... | collective-permute-start | bytes 79880 | tf_op jit(solution)/shard_map/ppermute | solution.py:382
  24.3 1.3 %shard_map.112.refs_3_ = f32[2,384,128]{2,1,0:T(8,128)S(1)} custom-call(s32[2,48]{1,0:T(2,128)S(1)} %fusion.2.slot_ref, bf16[16,6144]{1,0:T(8,128)(2,1)S(1)} %copy-done), custom_call_target="tpu_custom_call" | custom-call | flops 98304 | bytes 393216 | tf_op jit(solution)/shard_map/pallas_call | solution.py:483
  25.7 0.0 collective-permute-done.11.own_ref
  25.7 0.0 collective-permute-done.12.refs_0_
  25.7 0.0 collective-permute-done.13.refs_1_
  25.7 0.6 %collective-permute-done.14.refs_2_ = bf16[104,128]{1,0:T(8,128)(2,1)S(1)} collective-permute-done((bf16[104,128]{1,0:T(8,128)(2,1)S(1)}, bf16[104,128]{1,0:T(8,128)(2,1)S(1)}, u32[]{:S(2)}, u32[]{:S(2)}) %collective-permute-start.14) | collective-permute-done | bytes 26656 | tf_op jit(solution)/shard_map/ppermute | solution.py:382
  26.3 0.8 %shard_map.113 = (f32[1,2,2,24,128]{4,3,2,1,0:T(8,128)}, f32[1,2,24,128]{3,2,1,0:T(8,128)}) custom-call(bf16[104,128]{1,0:T(8,128)(2,1)S(1)} %collective-permute-done.11.own_ref, bf16[104,128]{1,0:T(8,128)(2,1)S(1)} %collective-permute-done.12.refs_0_, bf16[104,128]{1,0:T(8,128)(2,1)S(1)} %collective-permute-done.13.refs_1_, ...), custom_call_target="tpu_custom_call" | custom-call | flops 1000 | bytes 98304 | tf_op jit(solution)/shard_map/pallas_call | solution.py:502
  (7 shorter events, 0.0 us)
Async XLA Ops:
  0.6 4.6 %copy-start.5 = (s32[16,8]{0,1:T(8,128)S(1)}, s32[16,8]{0,1:T(8,128)}, u32[]{:S(2)}) copy-start(s32[16,8]{0,1:T(8,128)} %param.11) | copy-start | bytes 1540
  0.6 4.6 %copy-start.6 = (s32[16]{0:T(128)S(1)}, s32[16]{0:T(128)}, u32[]{:S(2)}) copy-start(s32[16]{0:T(128)} %param.10) | copy-start | bytes 196
  0.7 4.7 %copy-start.1 = (bf16[16,2,6144]{2,1,0:T(2,128)(2,1)S(1)}, bf16[16,2,6144]{2,1,0:T(2,128)(2,1)}, u32[]{:S(2)}) copy-start(bf16[16,2,6144]{2,1,0:T(2,128)(2,1)} %param.9) | copy-start | bytes 1179652
  0.7 5.4 %copy-start = (bf16[16,6144]{1,0:T(8,128)(2,1)S(1)}, bf16[16,6144]{1,0:T(8,128)(2,1)}, u32[]{:S(2)}) copy-start(bf16[16,6144]{1,0:T(8,128)(2,1)} %table_ref.1) | copy-start | bytes 589828
  0.7 7.4 %collective-permute-start.2 = (bf16[2,2,6144]{2,1,0:T(2,128)(2,1)}, bf16[2,2,6144]{2,1,0:T(2,128)(2,1)S(1)}, u32[]{:S(2)}, u32[]{:S(2)}) collective-permute-start(bf16[2,2,6144]{2,1,0:T(2,128)(2,1)} %param.12), channel_id=1, source_target_pairs={{6,0},{7,1},{4,2},{5,3},{2,4},{3,5},{0,6},{1,7},{14,8},{15,9},{12,... | collective-permute-start | bytes 147464 | tf_op jit(solution)/shard_map/ppermute | solution.py:376
  4.6 4.3 %collective-permute-start = (bf16[2,2,6144]{2,1,0:T(2,128)(2,1)}, bf16[2,2,6144]{2,1,0:T(2,128)(2,1)S(1)}, u32[]{:S(2)}, u32[]{:S(2)}) collective-permute-start(bf16[2,2,6144]{2,1,0:T(2,128)(2,1)} %param.12), channel_id=1, source_target_pairs={{4,0},{5,1},{6,2},{7,3},{0,4},{1,5},{2,6},{3,7},{12,8},{13,9},{14,... | collective-permute-start | bytes 147464 | tf_op jit(solution)/shard_map/ppermute | solution.py:376
  5.1 4.3 %collective-permute-start.1 = (bf16[2,2,6144]{2,1,0:T(2,128)(2,1)}, bf16[2,2,6144]{2,1,0:T(2,128)(2,1)S(1)}, u32[]{:S(2)}, u32[]{:S(2)}) collective-permute-start(bf16[2,2,6144]{2,1,0:T(2,128)(2,1)} %param.12), channel_id=1, source_target_pairs={{2,0},{3,1},{0,2},{1,3},{6,4},{7,5},{4,6},{5,7},{10,8},{11,9},{8,1... | collective-permute-start | bytes 147464 | tf_op jit(solution)/shard_map/ppermute | solution.py:376
  5.3 1.6 %collective-permute-start.4 = (s32[16,16]{1,0:T(8,128)S(1)}, s32[16,16]{1,0:T(8,128)S(1)}, u32[]{:S(2)}, u32[]{:S(2)}) collective-permute-start(s32[16,16]{1,0:T(8,128)S(1)} %shard_map.105.d_ref.refs_6_.i0_ref), channel_id=1, source_target_pairs={{0,1},{1,0},{2,3},{3,2},{4,5},{5,4},{6,7},{7,6},{8,9},{9,8},{10,11... | collective-permute-start | bytes 3080 | tf_op jit(solution)/shard_map/ppermute | solution.py:370
  5.4 1.8 %collective-permute-start.3 = (bf16[16,2,6144]{2,1,0:T(2,128)(2,1)S(1)}, bf16[16,2,6144]{2,1,0:T(2,128)(2,1)S(1)}, u32[]{:S(2)}, u32[]{:S(2)}) collective-permute-start(bf16[16,2,6144]{2,1,0:T(2,128)(2,1)S(1)} %copy-done.1), channel_id=1, source_target_pairs={{0,1},{1,0},{2,3},{3,2},{4,5},{5,4},{6,7},{7,6},{8,9},{9,8},{10,11... | collective-permute-start | bytes 1179656 | tf_op jit(solution)/shard_map/ppermute | solution.py:370
  6.8 2.6 %copy-start.2 = (bf16[2,2,6144]{2,1,0:T(2,128)(2,1)S(1)}, bf16[2,2,6144]{2,1,0:T(2,128)(2,1)}, u32[]{:S(2)}) copy-start(bf16[2,2,6144]{2,1,0:T(2,128)(2,1)} %param.12) | copy-start | bytes 147460
  6.8 2.6 %copy-start.3 = (f32[6144]{0:T(1024)S(1)}, f32[6144]{0:T(1024)}, u32[]{:S(2)}) copy-start(f32[6144]{0:T(1024)} %param.14) | copy-start | bytes 73732
  6.8 2.6 %copy-start.4 = (f32[8,128]{1,0:T(8,128)S(1)}, f32[8,128]{1,0:T(8,128)}, u32[]{:S(2)}) copy-start(f32[8,128]{1,0:T(8,128)} %constant.80.clone.refs_9_.trig_ref) | copy-start | bytes 12292
  8.0 2.8 %copy-start.7 = (s32[2,48]{1,0:T(2,128)S(1)}, s32[2,48]{1,0:T(2,128)}, u32[]{:S(2)}) copy-start(s32[2,48]{1,0:T(2,128)} %param.15) | copy-start | bytes 1156
  8.0 2.8 %copy-start.8 = (s32[4]{0:T(128)S(1)}, s32[4]{0:T(128)}, u32[]{:S(2)}) copy-start(s32[4]{0:T(128)} %param.16) | copy-start | bytes 52
  10.7 1.2 %collective-permute-start.6 = (f32[8,128]{1,0:T(8,128)S(1)}, f32[8,128]{1,0:T(8,128)S(1)}, u32[]{:S(2)}, u32[]{:S(2)}) collective-permute-start(f32[8,128]{1,0:T(8,128)S(1)} %get-tuple-element.21.stat_ref), channel_id=1, source_target_pairs={{0,1},{1,0},{2,3},{3,2},{4,5},{5,4},{6,7},{7,6},{8,9},{9,8},{10,11... | collective-permute-start | bytes 12296 | tf_op jit(solution)/shard_map/ppermute | solution.py:370
  12.7 4.8 %collective-permute-start.10 = (bf16[4,6272]{1,0:T(4,128)(2,1)S(1)}, bf16[4,6272]{1,0:T(4,128)(2,1)S(1)}, u32[]{:S(2)}, u32[]{:S(2)}) collective-permute-start(bf16[4,6272]{1,0:T(4,128)(2,1)S(1)} %get-tuple-element.25), channel_id=1, source_target_pairs={{0,7},{1,6},{2,5},{3,4},{4,3},{5,2},{6,1},{7,0},{8,15},{9,14},{10,... | collective-permute-start | bytes 150536 | tf_op jit(solution)/shard_map/ppermute | solution.py:379
  14.2 3.2 %collective-permute-start.7 = (bf16[4,6272]{1,0:T(4,128)(2,1)S(1)}, bf16[4,6272]{1,0:T(4,128)(2,1)S(1)}, u32[]{:S(2)}, u32[]{:S(2)}) collective-permute-start(bf16[4,6272]{1,0:T(4,128)(2,1)S(1)} %get-tuple-element.22), channel_id=1, source_target_pairs={{0,1},{1,0},{2,3},{3,2},{4,5},{5,4},{6,7},{7,6},{8,9},{9,8},{10,11... | collective-permute-start | bytes 150536 | tf_op jit(solution)/shard_map/ppermute | solution.py:370
  14.4 4.2 %collective-permute-start.8 = (bf16[4,6272]{1,0:T(4,128)(2,1)S(1)}, bf16[4,6272]{1,0:T(4,128)(2,1)S(1)}, u32[]{:S(2)}, u32[]{:S(2)}) collective-permute-start(bf16[4,6272]{1,0:T(4,128)(2,1)S(1)} %get-tuple-element.23), channel_id=1, source_target_pairs={{0,5},{1,4},{2,7},{3,6},{4,1},{5,0},{6,3},{7,2},{8,13},{9,12},{10,... | collective-permute-start | bytes 150536 | tf_op jit(solution)/shard_map/ppermute | solution.py:379
  14.8 3.7 %collective-permute-start.9 = (bf16[4,6272]{1,0:T(4,128)(2,1)S(1)}, bf16[4,6272]{1,0:T(4,128)(2,1)S(1)}, u32[]{:S(2)}, u32[]{:S(2)}) collective-permute-start(bf16[4,6272]{1,0:T(4,128)(2,1)S(1)} %get-tuple-element.24), channel_id=1, source_target_pairs={{0,3},{1,2},{2,1},{3,0},{4,7},{5,6},{6,5},{7,4},{8,11},{9,10},{10,... | collective-permute-start | bytes 150536 | tf_op jit(solution)/shard_map/ppermute | solution.py:379
  16.1 1.1 %collective-permute-start.5 = (s32[2,48]{1,0:T(2,128)S(1)}, s32[2,48]{1,0:T(2,128)S(1)}, u32[]{:S(2)}, u32[]{:S(2)}) collective-permute-start(s32[2,48]{1,0:T(2,128)S(1)} %fusion.2.slot_ref), channel_id=1, source_target_pairs={{0,1},{1,0},{2,3},{3,2},{4,5},{5,4},{6,7},{7,6},{8,9},{9,8},{10,11... | collective-permute-start | bytes 1160 | tf_op jit(solution)/shard_map/ppermute | solution.py:370
  18.8 6.9 %collective-permute-start.11 = (bf16[104,128]{1,0:T(8,128)(2,1)S(1)}, bf16[104,128]{1,0:T(8,128)(2,1)S(1)}, u32[]{:S(2)}, u32[]{:S(2)}) collective-permute-start(bf16[104,128]{1,0:T(8,128)(2,1)S(1)} %get-tuple-element.26), channel_id=1, source_target_pairs={{0,1},{1,0},{2,3},{3,2},{4,5},{5,4},{6,7},{7,6},{8,9},{9,8},{10,11... | collective-permute-start | bytes 79880 | tf_op jit(solution)/shard_map/ppermute | solution.py:370
  19.0 6.6 %collective-permute-start.12 = (bf16[104,128]{1,0:T(8,128)(2,1)S(1)}, bf16[104,128]{1,0:T(8,128)(2,1)S(1)}, u32[]{:S(2)}, u32[]{:S(2)}) collective-permute-start(bf16[104,128]{1,0:T(8,128)(2,1)S(1)} %get-tuple-element.27), channel_id=1, source_target_pairs={{0,9},{1,8},{2,11},{3,10},{4,13},{5,12},{6,15},{7,14},{8,17},{9,16... | collective-permute-start | bytes 79880 | tf_op jit(solution)/shard_map/ppermute | solution.py:382
  20.6 5.1 %collective-permute-start.13 = (bf16[104,128]{1,0:T(8,128)(2,1)S(1)}, bf16[104,128]{1,0:T(8,128)(2,1)S(1)}, u32[]{:S(2)}, u32[]{:S(2)}) collective-permute-start(bf16[104,128]{1,0:T(8,128)(2,1)S(1)} %get-tuple-element.28), channel_id=1, source_target_pairs={{0,17},{1,16},{2,19},{3,18},{4,21},{5,20},{6,23},{7,22},{8,25},{9,... | collective-permute-start | bytes 79880 | tf_op jit(solution)/shard_map/ppermute | solution.py:382
  23.0 3.3 %collective-permute-start.14 = (bf16[104,128]{1,0:T(8,128)(2,1)S(1)}, bf16[104,128]{1,0:T(8,128)(2,1)S(1)}, u32[]{:S(2)}, u32[]{:S(2)}) collective-permute-start(bf16[104,128]{1,0:T(8,128)(2,1)S(1)} %get-tuple-element.29), channel_id=1, source_target_pairs={{0,25},{1,24},{2,27},{3,26},{4,29},{5,28},{6,31},{7,30},{8,1},{9,0... | collective-permute-start | bytes 79880 | tf_op jit(solution)/shard_map/ppermute | solution.py:382
